TPU v7x, 128 devices: a whole 4x4x4 slice. The times are simulated.
128 devices in a mesh: lon: 32 (over z, x, y_lo), lat: 4 (over y_hi, core).
Axes of the slice: x: 4, y: 4 (y_hi: 2, y_lo: 2; y = y_hi * 2 + y_lo), z: 4, core: 2. Of those that a mesh axis runs over, the one named last changes fastest.
Arguments:
- control: float32 [100, 64, 4096], P(None, 'lat', 'lon'), may hold values from -6 to 6
- lon_coef: float32 [100, 64], P(None, 'lat'), may hold values from 0.02 to 0.2
- lat_coef: float32 [100, 64], P(None, 'lat'), may hold values from 0.02 to 0.2
- obs_base: int32 [128, 128, 128], P(('lon', 'lat')), may hold values from 0 to 1918, as said below
- obs_field: int32 [128, 128, 128], P(('lon', 'lat')), may hold values from 0 to 99
- obs_weight: float32 [4, 128, 128, 128], P(None, ('lon', 'lat')), may hold values from 0 to 1
- obs_count: int32 [128, 128], P(('lon', 'lat')), may hold values from 1 to 128, as said below
- obs_value: float32 [128, 128, 128], P(('lon', 'lat')), may hold values from -6 to 6
- obs_precision: float32 [128, 128, 128], P(('lon', 'lat')), may hold values from 0.5 to 2
Outputs:
- increment: float32 [100, 64, 4096], P(None, 'lat', 'lon')
- gradient: float32 [100, 64, 4096], P(None, 'lat', 'lon')
Inputs may be any that keep to these rules, and one draw needn't show every extreme that they name: `obs_base`: every corner lies in the holder's block: row below 15, column below 127. `obs_count`: each holder sends a full 128 slots to at least one owner.
All inputs are finite; a program needn't handle non-finite values.
Results may differ from a plain program's by a relative error of at most 0.00002.
Values sent between devices are 32-bit elements; how exact they have to be, the bound alone decides.
A program may use at most 64 MiB of HBM per device.

v0:
```python
import jax
import jax.numpy as jnp
from jax import lax
from jax.sharding import PartitionSpec as P

SWEEPS = 4


def passed_along(value, axis, steps):
    count = lax.axis_size(axis)
    leading, last = (max(0, -steps), min(count, count - steps))
    return lax.ppermute(value, axis, [(source, source + steps) for source in range(leading, last)])


def padded_2(block, sides, width, periodic):
    for axis, dim in sides:
        count = lax.axis_size(axis)
        forward = [(i, i + 1) for i in range(count - 1)]
        if periodic:
            forward.append((count - 1, 0))
        backward = [(target, source) for source, target in forward]
        low = lax.ppermute(
            lax.slice_in_dim(block, block.shape[dim] - width, None, axis=dim), axis, forward
        )
        high = lax.ppermute(lax.slice_in_dim(block, 0, width, axis=dim), axis, backward)
        block = jnp.concatenate([low, block, high], axis=dim)
    return block


def diffuse_step(padded, zonal_rate, merid_rate):
    centre = padded[:, 1:-1, 1:-1]
    zonal = padded[:, 1:-1, 2:] + padded[:, 1:-1, :-2] - 2.0 * centre
    north = merid_rate[:, 1:-1, None] * (padded[:, 2:, 1:-1] - centre)
    south = merid_rate[:, :-2, None] * (centre - padded[:, :-2, 1:-1])
    return centre + zonal_rate[:, 1:-1, None] * zonal + north - south


def rate_rims(rates):
    below = passed_along(rates[1][:, -1:], "lat", 1)
    blank = jnp.zeros_like(below)
    zonal_rim = jnp.pad(rates[0], ((0, 0), (1, 1)))
    merid_rim = jnp.concatenate([below, rates[1], blank], axis=1)
    return jnp.stack([zonal_rim, merid_rim])


def covariance_root(field, rate_rim):
    for step in range(SWEEPS):
        padded = padded_2(field, (("lat", 1),), 1, False)
        padded = padded_2(padded, (("lon", 2),), 1, True)
        field = diffuse_step(padded, rate_rim[0], rate_rim[1])
    return field


def per_device(
    control,
    lon_coef,
    lat_coef,
    obs_base,
    obs_field,
    obs_weight,
    obs_count,
    obs_value,
    obs_precision,
):
    fields, band_rows, block_cols = control.shape
    lat_devices = lax.axis_size("lat")
    slots = obs_base.shape[2]
    lat_rows = lax.axis_index("lat") * band_rows + jnp.arange(band_rows, dtype=jnp.int32)
    open_face = (lat_rows < band_rows * lat_devices - 1).astype(jnp.float32)
    rates = jnp.stack([lon_coef, lat_coef * open_face[None, :]])
    rate_rim = rate_rims(rates)
    increment = covariance_root(control, rate_rim)
    flat_field = increment.reshape(-1)
    corner_start = obs_field[0] * (band_rows * block_cols) + obs_base[0]
    offsets = (0, 1, block_cols, block_cols + 1)
    modelled = obs_weight[0, 0] * flat_field[corner_start + offsets[0]]
    for k in range(1, 4):
        modelled = modelled + obs_weight[k, 0] * flat_field[corner_start + offsets[k]]
    arrived = lax.all_to_all(modelled, ("lon", "lat"), split_axis=0, concat_axis=0, tiled=True)
    misfit = obs_precision[0] * (arrived - obs_value[0])
    returned = lax.all_to_all(misfit, ("lon", "lat"), split_axis=0, concat_axis=0, tiled=True)
    live_slot = jnp.arange(slots, dtype=jnp.int32)[None, :] < obs_count[0][:, None]
    returned = jnp.where(live_slot, returned, jnp.float32(0.0))
    places = jnp.concatenate([(corner_start + o).reshape(-1) for o in offsets])
    amounts = jnp.concatenate([(obs_weight[k, 0] * returned).reshape(-1) for k in range(4)])
    forcing = jnp.zeros((fields * band_rows * block_cols,), jnp.float32).at[places].add(amounts)
    adjoint = covariance_root(forcing.reshape(fields, band_rows, block_cols), rate_rim)
    return (increment, control + adjoint)


def solution(mesh):
    in_specs = (
        P(None, "lat", "lon"),
        P(None, "lat"),
        P(None, "lat"),
        P(("lon", "lat"), None, None),
        P(("lon", "lat"), None, None),
        P(None, ("lon", "lat"), None, None),
        P(("lon", "lat"), None),
        P(("lon", "lat"), None, None),
        P(("lon", "lat"), None, None),
    )
    out_specs = (P(None, "lat", "lon"), P(None, "lat", "lon"))
    return jax.shard_map(
        per_device, mesh=mesh, in_specs=in_specs, out_specs=out_specs, check_vma=False
    )
```

profile of v0, /device:TPU:1, one launch (start us, length us, event | category | flops | bytes accessed | tf_op | source)
XLA Modules:
  0.0 962.0 jit_solution(3522389019098375303)
XLA Ops:
  1.8 3.3 collective-permute-start.1
  5.2 4.8 collective-permute-start
  17.4 5.8 collective-permute-start.2
  29.1 3.3 collective-permute-start.6
  32.4 3.8 collective-permute-start.5
  40.7 6.0 collective-permute-start.7
  49.1 4.9 collective-permute-done.8
  55.5 3.2 fusion.63
  60.7 7.8 collective-permute-start.9
  75.2 5.7 collective-permute-start.11
  90.0 7.1 collective-permute-start.13
  102.7 5.7 collective-permute-start.15
  112.5 3.2 fusion.43
  115.8 90.5 %gather_fusion.3 = f32[16384]{0:T(1024)S(1)} fusion(f32[204800]{0:T(1024)S(1)} %bitcast.88, s32[16384]{0:T(1024)S(1)} %copy-done.5), kind=kCustom, calls=%fused_computation.3 | custom fusion | bytes 196608 | tf_op jit(solution)/shard_map/gather | solution.py:78
  206.3 90.5 %gather_fusion.2 = f32[16384]{0:T(1024)S(1)} fusion(f32[204800]{0:T(1024)S(1)} %bitcast.89, s32[16384]{0:T(1024)S(1)} %copy-done.4), kind=kCustom, calls=%fused_computation.2 | custom fusion | bytes 196608 | tf_op jit(solution)/shard_map/gather | solution.py:78
  296.9 90.5 %gather_fusion.1 = f32[16384]{0:T(1024)S(1)} fusion(f32[204800]{0:T(1024)S(1)} %bitcast.90, s32[16384]{0:T(1024)S(1)} %copy-done.3), kind=kCustom, calls=%fused_computation.1 | custom fusion | bytes 196608 | tf_op jit(solution)/shard_map/gather | solution.py:78
  387.5 90.5 %gather_fusion = f32[16384]{0:T(1024)S(1)} fusion(f32[204800]{0:T(1024)S(1)} %bitcast.91, s32[16384]{0:T(1024)S(1)} %get-tuple-element.4), kind=kCustom, calls=%fused_computation | custom fusion | bytes 196608 | tf_op jit(solution)/shard_map/gather | solution.py:76
  478.7 11.6 %all-to-all-start = ((f32[128,1,128]{2,1,0:T(1,128)}), f32[128,1,128]{2,1,0:T(1,128)S(1)}, u32[]{:S(2)}, u32[]{:S(2)}) async-start(f32[128,1,128]{2,1,0:T(1,128)} %bitcast.83), calls=%async_computation | async-start | bytes 131072 | tf_op jit(solution)/shard_map/all_to_all | solution.py:79
  490.3 9.7 %all-to-all-done = f32[128,1,128]{2,1,0:T(1,128)S(1)} async-done(((f32[128,1,128]{2,1,0:T(1,128)}), f32[128,1,128]{2,1,0:T(1,128)S(1)}, u32[]{:S(2)}, u32[]{:S(2)}) %all-to-all-start) | async-done | bytes 65568 | tf_op jit(solution)/shard_map/all_to_all | solution.py:79
  500.7 4.1 all-to-all-start.1
  505.0 9.5 all-to-all-done.1
  514.6 341.6 %scatter_custom_fusion = f32[204800]{0:T(1024)S(1)} fusion(s32[65536]{0:T(1024)S(1)} %bitcast.96, f32[65536]{0:T(1024)S(1)} %pad_maximum_fusion.72, f32[]{:T(128)} %constant.5.clone.1), kind=kCustom, calls=%fused_computation.159 | custom fusion | flops 65536 | bytes 819204 | tf_op jit(solution)/shard_map/scatter-add | solution.py:86
  858.8 4.5 collective-permute-start.17
  872.0 4.7 collective-permute-done.20
  878.3 3.2 fusion.33
  883.5 7.8 collective-permute-start.21
  900.9 3.8 collective-permute-done.24
  906.2 3.2 fusion.23
  911.4 7.8 collective-permute-start.25
  937.9 6.9 collective-permute-start.29
  952.7 4.0 collective-permute-done.32
  958.3 3.8 fusion.3
  (149 shorter events, 108.0 us)
Async XLA Ops:
  1.8 12.3 %collective-permute-start.1 = (f32[100,1,128]{2,1,0:T(1,128)S(1)}, f32[100,1,128]{2,1,0:T(1,128)S(1)}, u32[]{:S(2)}, u32[]{:S(2)}) collective-permute-start(f32[100,1,128]{2,1,0:T(1,128)S(1)} %get-tuple-element.36), channel_id=1, source_target_pairs={{1,0},{2,1},{3,2},{5,4},{6,5},{7,6},{9,8},{10,9},{11,10},{13,12},{... | collective-permute-start | bytes 153608 | tf_op jit(solution)/shard_map/ppermute | solution.py:25
  5.2 8.9 collective-permute-start
  10.8 12.3 %collective-permute-start.4 = (f32[100,1]{0,1:T(1,128)S(1)}, f32[100,1]{0,1:T(1,128)S(1)}, u32[]{:S(2)}, u32[]{:S(2)}) collective-permute-start(f32[100,1]{0,1:T(1,128)S(1)} %slice.342), channel_id=1, source_target_pairs={{0,1},{1,2},{2,3},{4,5},{5,6},{6,7},{8,9},{9,10},{10,11},{12,13},{... | collective-permute-start | bytes 1208 | tf_op jit(solution)/shard_map/ppermute | solution.py:12
  16.7 7.7 collective-permute-start.3
  17.4 6.6 collective-permute-start.2
  29.1 7.1 collective-permute-start.6
  32.4 5.0 collective-permute-start.5
  40.7 6.8 collective-permute-start.7
  47.2 6.8 collective-permute-start.8
  58.8 9.7 %collective-permute-start.10 = (f32[100,1,128]{2,1,0:T(1,128)S(1)}, f32[100,1,128]{2,1,0:T(1,128)S(1)}, u32[]{:S(2)}, u32[]{:S(2)}) collective-permute-start(f32[100,1,128]{2,1,0:T(1,128)S(1)} %get-tuple-element.32), channel_id=1, source_target_pairs={{1,0},{2,1},{3,2},{5,4},{6,5},{7,6},{9,8},{10,9},{11,10},{13,12},{... | collective-permute-start | bytes 153608 | tf_op jit(solution)/shard_map/ppermute | solution.py:25
  60.7 9.0 collective-permute-start.9
  75.1 8.1 collective-permute-start.12
  75.2 6.5 collective-permute-start.11
  88.0 9.7 %collective-permute-start.14 = (f32[100,1,128]{2,1,0:T(1,128)S(1)}, f32[100,1,128]{2,1,0:T(1,128)S(1)}, u32[]{:S(2)}, u32[]{:S(2)}) collective-permute-start(f32[100,1,128]{2,1,0:T(1,128)S(1)} %get-tuple-element.30), channel_id=1, source_target_pairs={{1,0},{2,1},{3,2},{5,4},{6,5},{7,6},{9,8},{10,9},{11,10},{13,12},{... | collective-permute-start | bytes 153608 | tf_op jit(solution)/shard_map/ppermute | solution.py:25
  90.0 8.2 collective-permute-start.13
  102.7 8.3 collective-permute-start.16
  102.7 6.7 collective-permute-start.15
  478.7 21.3 %all-to-all-start = ((f32[128,1,128]{2,1,0:T(1,128)}), f32[128,1,128]{2,1,0:T(1,128)S(1)}, u32[]{:S(2)}, u32[]{:S(2)}) async-start(f32[128,1,128]{2,1,0:T(1,128)} %bitcast.83), calls=%async_computation | async-start | bytes 131072 | tf_op jit(solution)/shard_map/all_to_all | solution.py:79
  500.7 13.8 %all-to-all-start.1 = ((f32[128,1,128]{2,1,0:T(1,128)}), f32[128,1,128]{2,1,0:T(1,128)S(1)}, u32[]{:S(2)}, u32[]{:S(2)}) async-start(f32[128,1,128]{2,1,0:T(1,128)} %bitcast.87), calls=%async_computation.1 | async-start | bytes 131072 | tf_op jit(solution)/shard_map/all_to_all | solution.py:81
  856.3 7.1 collective-permute-start.18
  858.8 5.7 collective-permute-start.17
  869.7 7.0 collective-permute-start.20
  881.5 9.7 %collective-permute-start.22 = (f32[100,1,128]{2,1,0:T(1,128)S(1)}, f32[100,1,128]{2,1,0:T(1,128)S(1)}, u32[]{:S(2)}, u32[]{:S(2)}) collective-permute-start(f32[100,1,128]{2,1,0:T(1,128)S(1)} %get-tuple-element.26), channel_id=1, source_target_pairs={{1,0},{2,1},{3,2},{5,4},{6,5},{7,6},{9,8},{10,9},{11,10},{13,12},{... | collective-permute-start | bytes 153608 | tf_op jit(solution)/shard_map/ppermute | solution.py:25
  883.5 9.0 collective-permute-start.21
  896.1 3.3 collective-permute-start.23
  897.9 6.8 collective-permute-start.24
  909.5 9.8 %collective-permute-start.26 = (f32[100,1,128]{2,1,0:T(1,128)S(1)}, f32[100,1,128]{2,1,0:T(1,128)S(1)}, u32[]{:S(2)}, u32[]{:S(2)}) collective-permute-start(f32[100,1,128]{2,1,0:T(1,128)S(1)} %get-tuple-element.24), channel_id=1, source_target_pairs={{1,0},{2,1},{3,2},{5,4},{6,5},{7,6},{9,8},{10,9},{11,10},{13,12},{... | collective-permute-start | bytes 153608 | tf_op jit(solution)/shard_map/ppermute | solution.py:25
  911.4 9.0 collective-permute-start.25
  924.3 6.8 collective-permute-start.28
  935.9 8.8 collective-permute-start.30
  937.9 8.1 collective-permute-start.29
  949.9 6.8 collective-permute-start.32
  (16 other events, 761.4 us)
where the time goes:
time: 965 us; the launch traced here: 962 us
  local copies, waits for them, and re-layouts  418 us (43%)
  other arithmetic  373 us (39%)
  starting transfers between devices  118 us (12%)
  waiting for transfers between devices  52 us (5%)
    scatter-add x1, other arithmetic, per_device(): jnp.zeros((fields * band_rows * block_cols,), jnp.float32).at[places]  342 us
    gather x3, local copies, waits for them, and re-layouts, per_device(): flat_field[corner_start + offsets[k]]  272 us
    gather x1, local copies, waits for them, and re-layouts, per_device(): modelled = obs_weight[0, 0] * flat_field[corner_start + offsets[0]]  90.5 us
    ppermute x16, starting transfers between devices, padded_2(): lax.ppermute(lax.slice_in_dim(block, block.shape[dim] - width, None, axis...  56 us
    ppermute x16, starting transfers between devices, padded_2(): lax.ppermute(lax.slice_in_dim(block, 0, width, axis=dim), axis, backward)  43.4 us
    ppermute x16, waiting for transfers between devices, padded_2(): lax.ppermute(lax.slice_in_dim(block, block.shape[dim] - width, None, axis...  27.8 us
    slice x24, local copies, waits for them, and re-layouts, padded_2(): lax.slice_in_dim(block, 0, width, axis=dim)  26 us
    sub x7, other arithmetic, diffuse_step(): return centre + zonal_rate[:, 1:-1, None] * zonal + north - south  22.2 us
  transfers between devices with their start and end apart: 35, of which 21 were waited for; matrix products, arithmetic and copies ran while one was open for 2% of the time, Pallas kernels for 0%

commit v1 on v0

--- a/solution.py
+++ b/solution.py
@@ -1,9 +1,13 @@
 import jax
 import jax.numpy as jnp
 from jax import lax
+from jax.experimental import pallas as pl
+from jax.experimental.pallas import tpu as pltpu
 from jax.sharding import PartitionSpec as P
 
 SWEEPS = 4
+PAD = 8
+NACC = 8
 
 
 def passed_along(value, axis, steps):
@@ -51,6 +55,159 @@
     return field
 
 
+def obs_kernel(cnt_ref, tab_ref, base_ref, field_ref, w_ref, val_ref, prec_ref, out_ref,
+               tab, stack, dense, cidx, ridx, ridx_s, sem, *accs):
+    rows = tab_ref.shape[0]
+    cells = 16 * 128
+    lane = lax.broadcasted_iota(jnp.int32, (8, 128), 1)
+    sub = lax.broadcasted_iota(jnp.int32, (8, 128), 0)
+    zero = jnp.zeros((8, 128), jnp.float32)
+
+    @pl.loop(0, rows // 80)
+    def _(i):
+        for k in range(10):
+            at = pl.multiple_of(i * 80 + 8 * k, 8)
+            tab[pl.ds(at + PAD, 8), :] = tab_ref[pl.ds(at, 8), :]
+
+    tab[pl.ds(0, 8), :] = zero
+    tab[pl.ds(rows + PAD, 8), :] = zero
+
+    @pl.loop(0, 16)
+    def _(b):
+        at = pl.multiple_of(b * 8, 8)
+        part = pl.ds(at, 8)
+        index = field_ref[part, :] * cells + base_ref[part, :]
+        arrays = [w_ref[k, part, :] for k in range(4)]
+        arrays += [val_ref[part, :], prec_ref[part, :], index.astype(jnp.float32)]
+        for k, array in enumerate(arrays):
+            stack[pl.ds(at * 8 + k, 8, stride=8), :] = array
+
+    def compact(o, start):
+        group = stack[pl.ds(pl.multiple_of(o * 8, 8), 8), :]
+        shift = lax.bitwise_and(start, 127)
+        row = pl.multiple_of(lax.shift_right_logical(start, 7) * 8, 8)
+        rolled = pltpu.roll(group, shift, 1)
+        dense[pl.ds(row, 8), :] = jnp.where(lane >= shift, rolled, dense[pl.ds(row, 8), :])
+        dense[pl.ds(row + 8, 8), :] = rolled
+        return start + cnt_ref[0, o]
+
+    total = lax.fori_loop(0, 128, compact, jnp.int32(0), unroll=8)
+    chunks = lax.shift_right_logical(total + 127, 7)
+
+    @pl.loop(0, 16)
+    def _(b):
+        at = pl.multiple_of(b * 8, 8)
+        index = dense[pl.ds(at * 8 + 6, 8, stride=8), :].astype(jnp.int32)
+        position = (at + sub) * 128 + lane
+        index = jnp.where(position < total, index, 0)
+        cidx[pl.ds(at, 8), :] = lax.bitwise_and(index, 127)
+        ridx[pl.ds(at, 8), :] = lax.shift_right_logical(index, 7) + PAD
+
+    copy = pltpu.make_async_copy(ridx, ridx_s, sem)
+    copy.start()
+
+    @pl.loop(0, (rows + 2 * PAD) // 8)
+    def _(i):
+        for acc in accs:
+            acc[pl.ds(pl.multiple_of(i * 8, 8), 8), :] = zero
+
+    copy.wait()
+
+    even = lax.bitwise_and(lane, 1) == 0
+    quad = lax.shift_right_logical(sub, 1)
+    first = lax.bitwise_and(sub, 1) == 0
+    keys = (
+        lax.shift_right_logical(lane, 1) - 16 * quad,
+        lax.shift_right_logical(lax.bitwise_and(lane - 1, 127), 1) - 16 * quad,
+    )
+
+    def spread(row):
+        return jnp.broadcast_to(row, (8, 128))
+
+    def gather(d):
+        group = dense[pl.ds(pl.multiple_of(d * 8, 8), 8), :]
+        cols = spread(cidx[pl.ds(d, 1), :])
+        after = pltpu.roll(cols, 1, 1) + 1
+        starts = (jnp.where(even, cols, after), jnp.where(even, after, cols))
+        w0 = jnp.where(first, spread(group[0:1]), spread(group[2:3]))
+        w1 = pltpu.roll(jnp.where(first, spread(group[1:2]), spread(group[3:4])), 1, 1)
+        weights = (jnp.where(even, w0, w1), jnp.where(even, w1, w0))
+        sums = []
+        for par in range(2):
+            found = zero
+            for g in range(16):
+                merged = None
+                for q in range(4):
+                    r = ridx_s[d, 2 * (g + 16 * q) + par]
+                    value = tab[pl.ds(r - 2 * q, 8), :]
+                    merged = value if q == 0 else jnp.where(sub >= 2 * q, value, merged)
+                picked = jnp.take_along_axis(merged, starts[par], axis=1, mode="promise_in_bounds")
+                found = jnp.where(keys[par] == g, picked, found)
+            sums.append(spread(jnp.sum(found * weights[par], axis=0, keepdims=True)))
+        here = jnp.where(even, sums[0], sums[1])
+        there = jnp.where(even, sums[1], sums[0])
+        modelled = here + pltpu.roll(there, 127, 1)
+        misfit = spread(group[5:6]) * (modelled - spread(group[4:5]))
+        misfit = jnp.where(d * 128 + lane < total, misfit, 0.0)
+        moved = pltpu.roll(misfit, 1, 1)
+        amounts = (
+            weights[0] * jnp.where(even, misfit, moved),
+            weights[1] * jnp.where(even, moved, misfit),
+        )
+        return amounts[0], amounts[1], lane - cols
+
+    def scatter(d, amounts, shift):
+        for par in range(2):
+            for g in range(16):
+                masked = jnp.where(keys[par] == g, amounts[par], 0.0)
+                turn = jnp.take_along_axis(shift, 2 * g + par + 32 * quad, axis=1, mode="promise_in_bounds")
+                source = lax.bitwise_and(lane + turn, 127)
+                placed = jnp.take_along_axis(masked, source, axis=1, mode="promise_in_bounds")
+                for q in range(4):
+                    r = ridx_s[d, 2 * (g + 16 * q) + par]
+                    acc = accs[(g % (len(accs) // 4)) * 4 + q]
+                    at = pl.ds(r - 2 * q, 8)
+                    acc[at, :] = acc[at, :] + jnp.where(quad == q, placed, 0.0)
+
+    def step(d, carry):
+        new = gather(jnp.minimum(d, chunks - 1))
+        scatter(jnp.maximum(d - 1, 0), carry[:2], carry[2])
+        return new
+
+    lax.fori_loop(0, chunks + 1, step, (zero, zero, lane))
+
+    @pl.loop(0, rows // 8)
+    def _(i):
+        at = pl.multiple_of(i * 8, 8)
+        parts = [acc[pl.ds(at + PAD, 8), :] for acc in accs]
+        while len(parts) > 1:
+            parts = [a + b for a, b in zip(parts[::2], parts[1::2])]
+        out_ref[pl.ds(at, 8), :] = parts[0]
+
+
+def observe(table, count, base, field, weight, value, precision):
+    rows, cols = table.shape
+    vmem = pl.BlockSpec(memory_space=pltpu.VMEM)
+    smem = pl.BlockSpec(memory_space=pltpu.SMEM)
+    return pl.pallas_call(
+        obs_kernel,
+        out_shape=jax.ShapeDtypeStruct((rows, cols), jnp.float32),
+        in_specs=[smem] + [vmem] * 6,
+        out_specs=vmem,
+        scratch_shapes=[
+            pltpu.VMEM((rows + 2 * PAD, cols), jnp.float32),
+            pltpu.VMEM((1024, 128), jnp.float32),
+            pltpu.VMEM((129 * 8, 128), jnp.float32),
+            pltpu.VMEM((128, 128), jnp.int32),
+            pltpu.VMEM((128, 128), jnp.int32),
+            pltpu.SMEM((128, 128), jnp.int32),
+            pltpu.SemaphoreType.DMA,
+        ] + [pltpu.VMEM((rows + 2 * PAD, cols), jnp.float32)] * NACC,
+        compiler_params=pltpu.CompilerParams(vmem_limit_bytes=40 * 2**20),
+        name="observe",
+    )(count, table, base, field, weight, value, precision)
+
+
 def per_device(
     control,
     lon_coef,
@@ -64,26 +221,22 @@
 ):
     fields, band_rows, block_cols = control.shape
     lat_devices = lax.axis_size("lat")
-    slots = obs_base.shape[2]
     lat_rows = lax.axis_index("lat") * band_rows + jnp.arange(band_rows, dtype=jnp.int32)
     open_face = (lat_rows < band_rows * lat_devices - 1).astype(jnp.float32)
     rates = jnp.stack([lon_coef, lat_coef * open_face[None, :]])
     rate_rim = rate_rims(rates)
     increment = covariance_root(control, rate_rim)
-    flat_field = increment.reshape(-1)
-    corner_start = obs_field[0] * (band_rows * block_cols) + obs_base[0]
-    offsets = (0, 1, block_cols, block_cols + 1)
-    modelled = obs_weight[0, 0] * flat_field[corner_start + offsets[0]]
-    for k in range(1, 4):
-        modelled = modelled + obs_weight[k, 0] * flat_field[corner_start + offsets[k]]
-    arrived = lax.all_to_all(modelled, ("lon", "lat"), split_axis=0, concat_axis=0, tiled=True)
-    misfit = obs_precision[0] * (arrived - obs_value[0])
-    returned = lax.all_to_all(misfit, ("lon", "lat"), split_axis=0, concat_axis=0, tiled=True)
-    live_slot = jnp.arange(slots, dtype=jnp.int32)[None, :] < obs_count[0][:, None]
-    returned = jnp.where(live_slot, returned, jnp.float32(0.0))
-    places = jnp.concatenate([(corner_start + o).reshape(-1) for o in offsets])
-    amounts = jnp.concatenate([(obs_weight[k, 0] * returned).reshape(-1) for k in range(4)])
-    forcing = jnp.zeros((fields * band_rows * block_cols,), jnp.float32).at[places].add(amounts)
+    sent = jnp.stack([obs_value[0], obs_precision[0]], axis=1)
+    held = lax.all_to_all(sent, ("lon", "lat"), split_axis=0, concat_axis=0, tiled=True)
+    forcing = observe(
+        increment.reshape(fields * band_rows, block_cols),
+        obs_count,
+        obs_base[0],
+        obs_field[0],
+        obs_weight[:, 0],
+        held[:, 0],
+        held[:, 1],
+    )
     adjoint = covariance_root(forcing.reshape(fields, band_rows, block_cols), rate_rim)
     return (increment, control + adjoint)
 

time: 965 us -> 205 us (0.21)
  local copies, waits for them, and re-layouts: 418 us -> 6.83 us
  other arithmetic: 373 us -> 8.23 us
  Pallas kernels: 0 us -> 31.3 us
  starting transfers between devices: 118 us -> 105 us
    gather x4 -> x0, local copies, waits for them, and re-layouts: 362 us -> none  [the longest x3 272 us: per_device(): flat_field[corner_start + offsets[k]]]
    scatter-add x1 -> x0, other arithmetic: 342 us -> none  [per_device(): jnp.zeros((fields * band_rows * block_cols,), jnp.float32).at[places]]
    pallas_call x0 -> x1, Pallas kernels: none -> 31.3 us  [observe(): pl.pallas_call(obs_kernel, out_shape=jax.ShapeDtypeStruct((rows, cols), j...]
    slice x24 -> x9, local copies, waits for them, and re-layouts: 26 us -> 0.75 us  [padded_2(): lax.slice_in_dim(block, 0, width, axis=dim)]
    all_to_all x2 -> x1, waiting for transfers between devices: 19.1 us -> 3.09 us  [per_device(): lax.all_to_all(sent, ('lon', 'lat'), split_axis=0, concat_axis=0, tiled=T...]
    sub x7, other arithmetic: 22.2 us -> 6.46 us  [diffuse_step(): return centre + zonal_rate[:, 1:-1, None] * zonal + north - south]
    ppermute x16, waiting for transfers between devices: 27.8 us -> 40.5 us  [padded_2(): lax.ppermute(lax.slice_in_dim(block, block.shape[dim] - width, None, axis...]
    ppermute x8 -> x1, local copies, waits for them, and re-layouts: 12.4 us -> 0.01 us  [padded_2(): lax.ppermute(lax.slice_in_dim(block, block.shape[dim] - width, None, axis...]
  transfers between devices with their start and end apart: 35 -> 34, of which waited for: 21 -> 21; matrix products, arithmetic and copies ran while one was open for 2% -> 0% of each run, Pallas kernels for 0% -> 0%
where the time goes in v1:
time: 205 us; the launch traced here: 203 us
  starting transfers between devices  105 us (51%)
  waiting for transfers between devices  50.3 us (25%)
  Pallas kernels  31.3 us (15%)
  other arithmetic  8.23 us (4%)
  local copies, waits for them, and re-layouts  6.83 us (3%)
    ppermute x16, starting transfers between devices, padded_2(): lax.ppermute(lax.slice_in_dim(block, block.shape[dim] - width, None, axis...  55.9 us
    ppermute x16, starting transfers between devices, padded_2(): lax.ppermute(lax.slice_in_dim(block, 0, width, axis=dim), axis, backward)  43.7 us
    ppermute x16, waiting for transfers between devices, padded_2(): lax.ppermute(lax.slice_in_dim(block, block.shape[dim] - width, None, axis...  40.5 us
    pallas_call x1, Pallas kernels, observe(): pl.pallas_call(obs_kernel, out_shape=jax.ShapeDtypeStruct((rows, cols), j...  31.3 us
    ppermute x16, waiting for transfers between devices, padded_2(): lax.ppermute(lax.slice_in_dim(block, 0, width, axis=dim), axis, backward)  6.68 us
    sub x7, other arithmetic, diffuse_step(): return centre + zonal_rate[:, 1:-1, None] * zonal + north - south  6.46 us
    unnamed x23, local copies, waits for them, and re-layouts  5.3 us
  transfers between devices with their start and end apart: 34, of which 21 were waited for; matrix products, arithmetic and copies ran while one was open for 0% of the time, Pallas kernels for 0%

profile of v1, /device:TPU:1, one launch (start us, length us, event | category | flops | bytes accessed | tf_op | source)
XLA Modules:
  0.0 203.4 jit_solution(3537144940787259857)
XLA Ops:
  2.5 3.3 %collective-permute-start.1 = (f32[100,1,128]{0,1,2:T(1,128)S(1)}, f32[100,1,128]{0,1,2:T(1,128)S(1)}, u32[]{:S(2)}, u32[]{:S(2)}) collective-permute-start(f32[100,1,128]{0,1,2:T(1,128)S(1)} %get-tuple-element.34), channel_id=1, source_target_pairs={{1,0},{2,1},{3,2},{5,4},{6,5},{7,6},{9,8},{10,9},{11,10},{13,12},{... | collective-permute-start | bytes 153608 | tf_op jit(solution)/shard_map/ppermute | solution.py:29
  5.8 4.8 %collective-permute-start = (f32[100,1,128]{0,1,2:T(1,128)S(1)}, f32[100,1,128]{0,1,2:T(1,128)S(1)}, u32[]{:S(2)}, u32[]{:S(2)}) collective-permute-start(f32[100,1,128]{0,1,2:T(1,128)S(1)} %get-tuple-element.35), channel_id=1, source_target_pairs={{0,1},{1,2},{2,3},{4,5},{5,6},{6,7},{8,9},{9,10},{10,11},{12,13},{... | collective-permute-start | bytes 153608 | tf_op jit(solution)/shard_map/ppermute | solution.py:26
  10.8 2.4 %collective-permute-start.4 = (f32[100,1]{0,1:T(1,128)S(1)}, f32[100,1]{0,1:T(1,128)S(1)}, u32[]{:S(2)}, u32[]{:S(2)}) collective-permute-start(f32[100,1]{0,1:T(1,128)S(1)} %slice.322), channel_id=1, source_target_pairs={{0,1},{1,2},{2,3},{4,5},{5,6},{6,7},{8,9},{9,10},{10,11},{12,13},{... | collective-permute-start | bytes 1208 | tf_op jit(solution)/shard_map/ppermute | solution.py:16
  13.2 6.3 %collective-permute-start.2 = (f32[100,18,1]{0,1,2:T(8,128)S(1)}, f32[100,18,1]{0,1,2:T(8,128)S(1)}, u32[]{:S(2)}, u32[]{:S(2)}) collective-permute-start(f32[100,18,1]{0,1,2:T(8,128)S(1)} %get-tuple-element.18), channel_id=1, source_target_pairs={{4,0},{8,4},{12,8},{16,12},{20,16},{24,20},{28,24},{32,28},{36,32}... | collective-permute-start | bytes 21608 | tf_op jit(solution)/shard_map/ppermute | solution.py:29
  20.3 5.9 %collective-permute-done.3 = f32[100,18,1]{0,1,2:T(8,128)S(1)} collective-permute-done((f32[100,18,1]{0,1,2:T(8,128)S(1)}, f32[100,18,1]{0,1,2:T(8,128)S(1)}, u32[]{:S(2)}, u32[]{:S(2)}) %collective-permute-start.3) | collective-permute-done | bytes 7232 | tf_op jit(solution)/shard_map/ppermute | solution.py:26
  27.2 3.8 %collective-permute-start.6 = (f32[100,1,128]{0,1,2:T(1,128)S(1)}, f32[100,1,128]{0,1,2:T(1,128)S(1)}, u32[]{:S(2)}, u32[]{:S(2)}) collective-permute-start(f32[100,1,128]{0,1,2:T(1,128)S(1)} %get-tuple-element.32), channel_id=1, source_target_pairs={{1,0},{2,1},{3,2},{5,4},{6,5},{7,6},{9,8},{10,9},{11,10},{13,12},{... | collective-permute-start | bytes 153608 | tf_op jit(solution)/shard_map/ppermute | solution.py:29
  31.0 5.2 %collective-permute-start.5 = (f32[100,1,128]{0,1,2:T(1,128)S(1)}, f32[100,1,128]{0,1,2:T(1,128)S(1)}, u32[]{:S(2)}, u32[]{:S(2)}) collective-permute-start(f32[100,1,128]{0,1,2:T(1,128)S(1)} %get-tuple-element.33), channel_id=1, source_target_pairs={{0,1},{1,2},{2,3},{4,5},{5,6},{6,7},{8,9},{9,10},{10,11},{12,13},{... | collective-permute-start | bytes 153608 | tf_op jit(solution)/shard_map/ppermute | solution.py:26
  40.4 4.0 %collective-permute-done.8 = f32[100,18,1]{0,1,2:T(8,128)S(1)} collective-permute-done((f32[100,18,1]{0,1,2:T(8,128)S(1)}, f32[100,18,1]{0,1,2:T(8,128)S(1)}, u32[]{:S(2)}, u32[]{:S(2)}) %collective-permute-start.8) | collective-permute-done | bytes 7232 | tf_op jit(solution)/shard_map/ppermute | solution.py:26
  45.3 1.9 collective-permute-start.10
  47.2 7.0 %collective-permute-start.9 = (f32[100,1,128]{0,1,2:T(1,128)S(1)}, f32[100,1,128]{0,1,2:T(1,128)S(1)}, u32[]{:S(2)}, u32[]{:S(2)}) collective-permute-start(f32[100,1,128]{0,1,2:T(1,128)S(1)} %get-tuple-element.31), channel_id=1, source_target_pairs={{0,1},{1,2},{2,3},{4,5},{5,6},{6,7},{8,9},{9,10},{10,11},{12,13},{... | collective-permute-start | bytes 153608 | tf_op jit(solution)/shard_map/ppermute | solution.py:26
  58.3 4.2 %collective-permute-done.12 = f32[100,18,1]{0,1,2:T(8,128)S(1)} collective-permute-done((f32[100,18,1]{0,1,2:T(8,128)S(1)}, f32[100,18,1]{0,1,2:T(8,128)S(1)}, u32[]{:S(2)}, u32[]{:S(2)}) %collective-permute-start.12) | collective-permute-done | bytes 7232 | tf_op jit(solution)/shard_map/ppermute | solution.py:26
  63.4 1.9 collective-permute-start.14
  65.3 7.0 %collective-permute-start.13 = (f32[100,1,128]{0,1,2:T(1,128)S(1)}, f32[100,1,128]{0,1,2:T(1,128)S(1)}, u32[]{:S(2)}, u32[]{:S(2)}) collective-permute-start(f32[100,1,128]{0,1,2:T(1,128)S(1)} %get-tuple-element.29), channel_id=1, source_target_pairs={{0,1},{1,2},{2,3},{4,5},{5,6},{6,7},{8,9},{9,10},{10,11},{12,13},{... | collective-permute-start | bytes 153608 | tf_op jit(solution)/shard_map/ppermute | solution.py:26
  73.1 3.5 %all-to-all-start = ((f32[128,2,128]{2,1,0:T(2,128)}), f32[128,2,128]{2,1,0:T(2,128)S(1)}, u32[]{:S(2)}, u32[]{:S(2)}) async-start(f32[128,2,128]{2,1,0:T(2,128)} %pad_maximum_fusion.64), calls=%async_computation | async-start | bytes 262144 | tf_op jit(solution)/shard_map/all_to_all | solution.py:230
  77.3 4.6 %collective-permute-start.15 = (f32[100,18,1]{0,1,2:T(8,128)S(1)}, f32[100,18,1]{0,1,2:T(8,128)S(1)}, u32[]{:S(2)}, u32[]{:S(2)}) collective-permute-start(f32[100,18,1]{0,1,2:T(8,128)S(1)} %get-tuple-element.12), channel_id=1, source_target_pairs={{4,0},{8,4},{12,8},{16,12},{20,16},{24,20},{28,24},{32,28},{36,32}... | collective-permute-start | bytes 21608 | tf_op jit(solution)/shard_map/ppermute | solution.py:29
  81.9 3.1 %all-to-all-done = f32[128,2,128]{2,1,0:T(2,128)S(1)} async-done(((f32[128,2,128]{2,1,0:T(2,128)}), f32[128,2,128]{2,1,0:T(2,128)S(1)}, u32[]{:S(2)}, u32[]{:S(2)}) %all-to-all-start) | async-done | bytes 131104 | tf_op jit(solution)/shard_map/all_to_all | solution.py:230
  85.1 3.6 %collective-permute-done.16 = f32[100,18,1]{0,1,2:T(8,128)S(1)} collective-permute-done((f32[100,18,1]{0,1,2:T(8,128)S(1)}, f32[100,18,1]{0,1,2:T(8,128)S(1)}, u32[]{:S(2)}, u32[]{:S(2)}) %collective-permute-start.16) | collective-permute-done | bytes 7232 | tf_op jit(solution)/shard_map/ppermute | solution.py:26
  88.7 1.8 fusion.43
  92.0 31.3 %observe.1 = f32[1600,128]{1,0:T(8,128)S(1)} custom-call(s32[1,128]{1,0:T(1,128)S(1)} %copy-done.4, f32[1600,128]{1,0:T(8,128)S(1)} %bitcast.13, s32[128,128]{1,0:T(8,128)S(1)} %bitcast.18, s32[128,128]{1,0:T(8,128)S(1)} %bitcast.19, f32[4,128,128]{2,1,0:T(8,128)S(1)} %bitcast.15, f32[128,128]{1,0:T(8,128)S(1)} %bitcast.17, f32[128,128]{1,0:T(8,128)S(1)} %bitcast.16), custom_call_target="tpu_custom_call" | custom-call | tf_op jit(solution)/shard_map/observe/pallas_call | solution.py:192
  124.1 4.1 %collective-permute-start.18 = (f32[100,1,128]{0,1,2:T(1,128)S(1)}, f32[100,1,128]{0,1,2:T(1,128)S(1)}, u32[]{:S(2)}, u32[]{:S(2)}) collective-permute-start(f32[100,1,128]{0,1,2:T(1,128)S(1)} %get-tuple-element.26), channel_id=1, source_target_pairs={{1,0},{2,1},{3,2},{5,4},{6,5},{7,6},{9,8},{10,9},{11,10},{13,12},{... | collective-permute-start | bytes 153608 | tf_op jit(solution)/shard_map/ppermute | solution.py:29
  128.2 4.3 %collective-permute-start.17 = (f32[100,1,128]{0,1,2:T(1,128)S(1)}, f32[100,1,128]{0,1,2:T(1,128)S(1)}, u32[]{:S(2)}, u32[]{:S(2)}) collective-permute-start(f32[100,1,128]{0,1,2:T(1,128)S(1)} %get-tuple-element.27), channel_id=1, source_target_pairs={{0,1},{1,2},{2,3},{4,5},{5,6},{6,7},{8,9},{9,10},{10,11},{12,13},{... | collective-permute-start | bytes 153608 | tf_op jit(solution)/shard_map/ppermute | solution.py:26
  134.0 5.9 %collective-permute-start.19 = (f32[100,18,1]{0,2,1:T(1,128)S(1)}, f32[100,18,1]{0,2,1:T(1,128)S(1)}, u32[]{:S(2)}, u32[]{:S(2)}) collective-permute-start(f32[100,18,1]{0,2,1:T(1,128)S(1)} %copy.29), channel_id=1, source_target_pairs={{4,0},{8,4},{12,8},{16,12},{20,16},{24,20},{28,24},{32,28},{36,32}... | collective-permute-start | bytes 21608 | tf_op jit(solution)/shard_map/ppermute | solution.py:29
  141.6 1.9 collective-permute-start.22
  143.5 6.9 %collective-permute-start.21 = (f32[100,1,128]{0,1,2:T(1,128)S(1)}, f32[100,1,128]{0,1,2:T(1,128)S(1)}, u32[]{:S(2)}, u32[]{:S(2)}) collective-permute-start(f32[100,1,128]{0,1,2:T(1,128)S(1)} %get-tuple-element.25), channel_id=1, source_target_pairs={{0,1},{1,2},{2,3},{4,5},{5,6},{6,7},{8,9},{9,10},{10,11},{12,13},{... | collective-permute-start | bytes 153608 | tf_op jit(solution)/shard_map/ppermute | solution.py:26
  151.7 5.7 %collective-permute-start.23 = (f32[100,18,1]{0,1,2:T(8,128)S(1)}, f32[100,18,1]{0,1,2:T(8,128)S(1)}, u32[]{:S(2)}, u32[]{:S(2)}) collective-permute-start(f32[100,18,1]{0,1,2:T(8,128)S(1)} %get-tuple-element.8), channel_id=1, source_target_pairs={{4,0},{8,4},{12,8},{16,12},{20,16},{24,20},{28,24},{32,28},{36,32}... | collective-permute-start | bytes 21608 | tf_op jit(solution)/shard_map/ppermute | solution.py:29
  158.3 5.9 %collective-permute-done.24 = f32[100,18,1]{0,1,2:T(8,128)S(1)} collective-permute-done((f32[100,18,1]{0,1,2:T(8,128)S(1)}, f32[100,18,1]{0,1,2:T(8,128)S(1)}, u32[]{:S(2)}, u32[]{:S(2)}) %collective-permute-start.24) | collective-permute-done | bytes 7232 | tf_op jit(solution)/shard_map/ppermute | solution.py:26
  165.0 1.9 collective-permute-start.26
  167.0 7.8 %collective-permute-start.25 = (f32[100,1,128]{0,1,2:T(1,128)S(1)}, f32[100,1,128]{0,1,2:T(1,128)S(1)}, u32[]{:S(2)}, u32[]{:S(2)}) collective-permute-start(f32[100,1,128]{0,1,2:T(1,128)S(1)} %get-tuple-element.23), channel_id=1, source_target_pairs={{0,1},{1,2},{2,3},{4,5},{5,6},{6,7},{8,9},{9,10},{10,11},{12,13},{... | collective-permute-start | bytes 153608 | tf_op jit(solution)/shard_map/ppermute | solution.py:26
  178.7 4.3 %collective-permute-done.28 = f32[100,18,1]{0,1,2:T(8,128)S(1)} collective-permute-done((f32[100,18,1]{0,1,2:T(8,128)S(1)}, f32[100,18,1]{0,1,2:T(8,128)S(1)}, u32[]{:S(2)}, u32[]{:S(2)}) %collective-permute-start.28) | collective-permute-done | bytes 7232 | tf_op jit(solution)/shard_map/ppermute | solution.py:26
  183.9 1.9 collective-permute-start.30
  185.8 6.9 %collective-permute-start.29 = (f32[100,1,128]{0,1,2:T(1,128)S(1)}, f32[100,1,128]{0,1,2:T(1,128)S(1)}, u32[]{:S(2)}, u32[]{:S(2)}) collective-permute-start(f32[100,1,128]{0,1,2:T(1,128)S(1)} %get-tuple-element.21), channel_id=1, source_target_pairs={{0,1},{1,2},{2,3},{4,5},{5,6},{6,7},{8,9},{9,10},{10,11},{12,13},{... | collective-permute-start | bytes 153608 | tf_op jit(solution)/shard_map/ppermute | solution.py:26
  197.0 4.1 %collective-permute-done.32 = f32[100,18,1]{0,1,2:T(8,128)S(1)} collective-permute-done((f32[100,18,1]{0,1,2:T(8,128)S(1)}, f32[100,18,1]{0,1,2:T(8,128)S(1)}, u32[]{:S(2)}, u32[]{:S(2)}) %collective-permute-start.32) | collective-permute-done | bytes 7232 | tf_op jit(solution)/shard_map/ppermute | solution.py:26
  (95 shorter events, 34.7 us)
Async XLA Ops:
  2.5 10.7 %collective-permute-start.1 = (f32[100,1,128]{0,1,2:T(1,128)S(1)}, f32[100,1,128]{0,1,2:T(1,128)S(1)}, u32[]{:S(2)}, u32[]{:S(2)}) collective-permute-start(f32[100,1,128]{0,1,2:T(1,128)S(1)} %get-tuple-element.34), channel_id=1, source_target_pairs={{1,0},{2,1},{3,2},{5,4},{6,5},{7,6},{9,8},{10,9},{11,10},{13,12},{... | collective-permute-start | bytes 153608 | tf_op jit(solution)/shard_map/ppermute | solution.py:29
  5.8 7.3 %collective-permute-start = (f32[100,1,128]{0,1,2:T(1,128)S(1)}, f32[100,1,128]{0,1,2:T(1,128)S(1)}, u32[]{:S(2)}, u32[]{:S(2)}) collective-permute-start(f32[100,1,128]{0,1,2:T(1,128)S(1)} %get-tuple-element.35), channel_id=1, source_target_pairs={{0,1},{1,2},{2,3},{4,5},{5,6},{6,7},{8,9},{9,10},{10,11},{12,13},{... | collective-permute-start | bytes 153608 | tf_op jit(solution)/shard_map/ppermute | solution.py:26
  10.8 8.8 %collective-permute-start.4 = (f32[100,1]{0,1:T(1,128)S(1)}, f32[100,1]{0,1:T(1,128)S(1)}, u32[]{:S(2)}, u32[]{:S(2)}) collective-permute-start(f32[100,1]{0,1:T(1,128)S(1)} %slice.322), channel_id=1, source_target_pairs={{0,1},{1,2},{2,3},{4,5},{5,6},{6,7},{8,9},{9,10},{10,11},{12,13},{... | collective-permute-start | bytes 1208 | tf_op jit(solution)/shard_map/ppermute | solution.py:16
  13.2 7.1 %collective-permute-start.2 = (f32[100,18,1]{0,1,2:T(8,128)S(1)}, f32[100,18,1]{0,1,2:T(8,128)S(1)}, u32[]{:S(2)}, u32[]{:S(2)}) collective-permute-start(f32[100,18,1]{0,1,2:T(8,128)S(1)} %get-tuple-element.18), channel_id=1, source_target_pairs={{4,0},{8,4},{12,8},{16,12},{20,16},{24,20},{28,24},{32,28},{36,32}... | collective-permute-start | bytes 21608 | tf_op jit(solution)/shard_map/ppermute | solution.py:29
  19.5 6.8 %collective-permute-start.3 = (f32[100,18,1]{0,1,2:T(8,128)S(1)}, f32[100,18,1]{0,1,2:T(8,128)S(1)}, u32[]{:S(2)}, u32[]{:S(2)}) collective-permute-start(f32[100,18,1]{0,1,2:T(8,128)S(1)} %get-tuple-element.19), channel_id=1, source_target_pairs={{0,4},{4,8},{8,12},{12,16},{16,20},{20,24},{24,28},{28,32},{32,36}... | collective-permute-start | bytes 21608 | tf_op jit(solution)/shard_map/ppermute | solution.py:26
  27.2 9.0 %collective-permute-start.6 = (f32[100,1,128]{0,1,2:T(1,128)S(1)}, f32[100,1,128]{0,1,2:T(1,128)S(1)}, u32[]{:S(2)}, u32[]{:S(2)}) collective-permute-start(f32[100,1,128]{0,1,2:T(1,128)S(1)} %get-tuple-element.32), channel_id=1, source_target_pairs={{1,0},{2,1},{3,2},{5,4},{6,5},{7,6},{9,8},{10,9},{11,10},{13,12},{... | collective-permute-start | bytes 153608 | tf_op jit(solution)/shard_map/ppermute | solution.py:29
  31.0 6.5 %collective-permute-start.5 = (f32[100,1,128]{0,1,2:T(1,128)S(1)}, f32[100,1,128]{0,1,2:T(1,128)S(1)}, u32[]{:S(2)}, u32[]{:S(2)}) collective-permute-start(f32[100,1,128]{0,1,2:T(1,128)S(1)} %get-tuple-element.33), channel_id=1, source_target_pairs={{0,1},{1,2},{2,3},{4,5},{5,6},{6,7},{8,9},{9,10},{10,11},{12,13},{... | collective-permute-start | bytes 153608 | tf_op jit(solution)/shard_map/ppermute | solution.py:26
  37.5 2.9 %collective-permute-start.7 = (f32[100,18,1]{0,1,2:T(8,128)S(1)}, f32[100,18,1]{0,1,2:T(8,128)S(1)}, u32[]{:S(2)}, u32[]{:S(2)}) collective-permute-start(f32[100,18,1]{0,1,2:T(8,128)S(1)} %get-tuple-element.16), channel_id=1, source_target_pairs={{4,0},{8,4},{12,8},{16,12},{20,16},{24,20},{28,24},{32,28},{36,32}... | collective-permute-start | bytes 21608 | tf_op jit(solution)/shard_map/ppermute | solution.py:29
  37.6 6.8 %collective-permute-start.8 = (f32[100,18,1]{0,1,2:T(8,128)S(1)}, f32[100,18,1]{0,1,2:T(8,128)S(1)}, u32[]{:S(2)}, u32[]{:S(2)}) collective-permute-start(f32[100,18,1]{0,1,2:T(8,128)S(1)} %get-tuple-element.17), channel_id=1, source_target_pairs={{0,4},{4,8},{8,12},{12,16},{16,20},{20,24},{24,28},{28,32},{32,36}... | collective-permute-start | bytes 21608 | tf_op jit(solution)/shard_map/ppermute | solution.py:26
  45.3 9.0 %collective-permute-start.10 = (f32[100,1,128]{0,1,2:T(1,128)S(1)}, f32[100,1,128]{0,1,2:T(1,128)S(1)}, u32[]{:S(2)}, u32[]{:S(2)}) collective-permute-start(f32[100,1,128]{0,1,2:T(1,128)S(1)} %get-tuple-element.30), channel_id=1, source_target_pairs={{1,0},{2,1},{3,2},{5,4},{6,5},{7,6},{9,8},{10,9},{11,10},{13,12},{... | collective-permute-start | bytes 153608 | tf_op jit(solution)/shard_map/ppermute | solution.py:29
  47.2 8.4 %collective-permute-start.9 = (f32[100,1,128]{0,1,2:T(1,128)S(1)}, f32[100,1,128]{0,1,2:T(1,128)S(1)}, u32[]{:S(2)}, u32[]{:S(2)}) collective-permute-start(f32[100,1,128]{0,1,2:T(1,128)S(1)} %get-tuple-element.31), channel_id=1, source_target_pairs={{0,1},{1,2},{2,3},{4,5},{5,6},{6,7},{8,9},{9,10},{10,11},{12,13},{... | collective-permute-start | bytes 153608 | tf_op jit(solution)/shard_map/ppermute | solution.py:26
  55.6 6.8 %collective-permute-start.12 = (f32[100,18,1]{0,1,2:T(8,128)S(1)}, f32[100,18,1]{0,1,2:T(8,128)S(1)}, u32[]{:S(2)}, u32[]{:S(2)}) collective-permute-start(f32[100,18,1]{0,1,2:T(8,128)S(1)} %get-tuple-element.15), channel_id=1, source_target_pairs={{0,4},{4,8},{8,12},{12,16},{16,20},{20,24},{24,28},{28,32},{32,36}... | collective-permute-start | bytes 21608 | tf_op jit(solution)/shard_map/ppermute | solution.py:26
  63.4 13.3 %collective-permute-start.14 = (f32[100,1,128]{0,1,2:T(1,128)S(1)}, f32[100,1,128]{0,1,2:T(1,128)S(1)}, u32[]{:S(2)}, u32[]{:S(2)}) collective-permute-start(f32[100,1,128]{0,1,2:T(1,128)S(1)} %get-tuple-element.28), channel_id=1, source_target_pairs={{1,0},{2,1},{3,2},{5,4},{6,5},{7,6},{9,8},{10,9},{11,10},{13,12},{... | collective-permute-start | bytes 153608 | tf_op jit(solution)/shard_map/ppermute | solution.py:29
  65.3 11.4 %collective-permute-start.13 = (f32[100,1,128]{0,1,2:T(1,128)S(1)}, f32[100,1,128]{0,1,2:T(1,128)S(1)}, u32[]{:S(2)}, u32[]{:S(2)}) collective-permute-start(f32[100,1,128]{0,1,2:T(1,128)S(1)} %get-tuple-element.29), channel_id=1, source_target_pairs={{0,1},{1,2},{2,3},{4,5},{5,6},{6,7},{8,9},{9,10},{10,11},{12,13},{... | collective-permute-start | bytes 153608 | tf_op jit(solution)/shard_map/ppermute | solution.py:26
  73.1 11.9 %all-to-all-start = ((f32[128,2,128]{2,1,0:T(2,128)}), f32[128,2,128]{2,1,0:T(2,128)S(1)}, u32[]{:S(2)}, u32[]{:S(2)}) async-start(f32[128,2,128]{2,1,0:T(2,128)} %pad_maximum_fusion.64), calls=%async_computation | async-start | bytes 262144 | tf_op jit(solution)/shard_map/all_to_all | solution.py:230
  77.3 7.8 %collective-permute-start.15 = (f32[100,18,1]{0,1,2:T(8,128)S(1)}, f32[100,18,1]{0,1,2:T(8,128)S(1)}, u32[]{:S(2)}, u32[]{:S(2)}) collective-permute-start(f32[100,18,1]{0,1,2:T(8,128)S(1)} %get-tuple-element.12), channel_id=1, source_target_pairs={{4,0},{8,4},{12,8},{16,12},{20,16},{24,20},{28,24},{32,28},{36,32}... | collective-permute-start | bytes 21608 | tf_op jit(solution)/shard_map/ppermute | solution.py:29
  81.9 6.8 %collective-permute-start.16 = (f32[100,18,1]{0,1,2:T(8,128)S(1)}, f32[100,18,1]{0,1,2:T(8,128)S(1)}, u32[]{:S(2)}, u32[]{:S(2)}) collective-permute-start(f32[100,18,1]{0,1,2:T(8,128)S(1)} %get-tuple-element.13), channel_id=1, source_target_pairs={{0,4},{4,8},{8,12},{12,16},{16,20},{20,24},{24,28},{28,32},{32,36}... | collective-permute-start | bytes 21608 | tf_op jit(solution)/shard_map/ppermute | solution.py:26
  124.1 8.5 %collective-permute-start.18 = (f32[100,1,128]{0,1,2:T(1,128)S(1)}, f32[100,1,128]{0,1,2:T(1,128)S(1)}, u32[]{:S(2)}, u32[]{:S(2)}) collective-permute-start(f32[100,1,128]{0,1,2:T(1,128)S(1)} %get-tuple-element.26), channel_id=1, source_target_pairs={{1,0},{2,1},{3,2},{5,4},{6,5},{7,6},{9,8},{10,9},{11,10},{13,12},{... | collective-permute-start | bytes 153608 | tf_op jit(solution)/shard_map/ppermute | solution.py:29
  128.2 5.7 %collective-permute-start.17 = (f32[100,1,128]{0,1,2:T(1,128)S(1)}, f32[100,1,128]{0,1,2:T(1,128)S(1)}, u32[]{:S(2)}, u32[]{:S(2)}) collective-permute-start(f32[100,1,128]{0,1,2:T(1,128)S(1)} %get-tuple-element.27), channel_id=1, source_target_pairs={{0,1},{1,2},{2,3},{4,5},{5,6},{6,7},{8,9},{9,10},{10,11},{12,13},{... | collective-permute-start | bytes 153608 | tf_op jit(solution)/shard_map/ppermute | solution.py:26
  133.9 6.8 %collective-permute-start.20 = (f32[100,18,1]{0,2,1:T(1,128)S(1)}, f32[100,18,1]{0,2,1:T(1,128)S(1)}, u32[]{:S(2)}, u32[]{:S(2)}) collective-permute-start(f32[100,18,1]{0,2,1:T(1,128)S(1)} %copy.31), channel_id=1, source_target_pairs={{0,4},{4,8},{8,12},{12,16},{16,20},{20,24},{24,28},{28,32},{32,36}... | collective-permute-start | bytes 21608 | tf_op jit(solution)/shard_map/ppermute | solution.py:26
  134.0 6.7 %collective-permute-start.19 = (f32[100,18,1]{0,2,1:T(1,128)S(1)}, f32[100,18,1]{0,2,1:T(1,128)S(1)}, u32[]{:S(2)}, u32[]{:S(2)}) collective-permute-start(f32[100,18,1]{0,2,1:T(1,128)S(1)} %copy.29), channel_id=1, source_target_pairs={{4,0},{8,4},{12,8},{16,12},{20,16},{24,20},{28,24},{32,28},{36,32}... | collective-permute-start | bytes 21608 | tf_op jit(solution)/shard_map/ppermute | solution.py:29
  141.6 8.9 %collective-permute-start.22 = (f32[100,1,128]{0,1,2:T(1,128)S(1)}, f32[100,1,128]{0,1,2:T(1,128)S(1)}, u32[]{:S(2)}, u32[]{:S(2)}) collective-permute-start(f32[100,1,128]{0,1,2:T(1,128)S(1)} %get-tuple-element.24), channel_id=1, source_target_pairs={{1,0},{2,1},{3,2},{5,4},{6,5},{7,6},{9,8},{10,9},{11,10},{13,12},{... | collective-permute-start | bytes 153608 | tf_op jit(solution)/shard_map/ppermute | solution.py:29
  143.5 8.2 %collective-permute-start.21 = (f32[100,1,128]{0,1,2:T(1,128)S(1)}, f32[100,1,128]{0,1,2:T(1,128)S(1)}, u32[]{:S(2)}, u32[]{:S(2)}) collective-permute-start(f32[100,1,128]{0,1,2:T(1,128)S(1)} %get-tuple-element.25), channel_id=1, source_target_pairs={{0,1},{1,2},{2,3},{4,5},{5,6},{6,7},{8,9},{9,10},{10,11},{12,13},{... | collective-permute-start | bytes 153608 | tf_op jit(solution)/shard_map/ppermute | solution.py:26
  151.7 6.5 %collective-permute-start.23 = (f32[100,18,1]{0,1,2:T(8,128)S(1)}, f32[100,18,1]{0,1,2:T(8,128)S(1)}, u32[]{:S(2)}, u32[]{:S(2)}) collective-permute-start(f32[100,18,1]{0,1,2:T(8,128)S(1)} %get-tuple-element.8), channel_id=1, source_target_pairs={{4,0},{8,4},{12,8},{16,12},{20,16},{24,20},{28,24},{32,28},{36,32}... | collective-permute-start | bytes 21608 | tf_op jit(solution)/shard_map/ppermute | solution.py:29
  157.4 6.8 %collective-permute-start.24 = (f32[100,18,1]{0,1,2:T(8,128)S(1)}, f32[100,18,1]{0,1,2:T(8,128)S(1)}, u32[]{:S(2)}, u32[]{:S(2)}) collective-permute-start(f32[100,18,1]{0,1,2:T(8,128)S(1)} %get-tuple-element.9), channel_id=1, source_target_pairs={{0,4},{4,8},{8,12},{12,16},{16,20},{20,24},{24,28},{28,32},{32,36}... | collective-permute-start | bytes 21608 | tf_op jit(solution)/shard_map/ppermute | solution.py:26
  165.0 9.7 %collective-permute-start.26 = (f32[100,1,128]{0,1,2:T(1,128)S(1)}, f32[100,1,128]{0,1,2:T(1,128)S(1)}, u32[]{:S(2)}, u32[]{:S(2)}) collective-permute-start(f32[100,1,128]{0,1,2:T(1,128)S(1)} %get-tuple-element.22), channel_id=1, source_target_pairs={{1,0},{2,1},{3,2},{5,4},{6,5},{7,6},{9,8},{10,9},{11,10},{13,12},{... | collective-permute-start | bytes 153608 | tf_op jit(solution)/shard_map/ppermute | solution.py:29
  167.0 9.1 %collective-permute-start.25 = (f32[100,1,128]{0,1,2:T(1,128)S(1)}, f32[100,1,128]{0,1,2:T(1,128)S(1)}, u32[]{:S(2)}, u32[]{:S(2)}) collective-permute-start(f32[100,1,128]{0,1,2:T(1,128)S(1)} %get-tuple-element.23), channel_id=1, source_target_pairs={{0,1},{1,2},{2,3},{4,5},{5,6},{6,7},{8,9},{9,10},{10,11},{12,13},{... | collective-permute-start | bytes 153608 | tf_op jit(solution)/shard_map/ppermute | solution.py:26
  176.2 6.8 %collective-permute-start.28 = (f32[100,18,1]{0,1,2:T(8,128)S(1)}, f32[100,18,1]{0,1,2:T(8,128)S(1)}, u32[]{:S(2)}, u32[]{:S(2)}) collective-permute-start(f32[100,18,1]{0,1,2:T(8,128)S(1)} %get-tuple-element.7), channel_id=1, source_target_pairs={{0,4},{4,8},{8,12},{12,16},{16,20},{20,24},{24,28},{28,32},{32,36}... | collective-permute-start | bytes 21608 | tf_op jit(solution)/shard_map/ppermute | solution.py:26
  183.9 8.9 %collective-permute-start.30 = (f32[100,1,128]{0,1,2:T(1,128)S(1)}, f32[100,1,128]{0,1,2:T(1,128)S(1)}, u32[]{:S(2)}, u32[]{:S(2)}) collective-permute-start(f32[100,1,128]{0,1,2:T(1,128)S(1)} %get-tuple-element.20), channel_id=1, source_target_pairs={{1,0},{2,1},{3,2},{5,4},{6,5},{7,6},{9,8},{10,9},{11,10},{13,12},{... | collective-permute-start | bytes 153608 | tf_op jit(solution)/shard_map/ppermute | solution.py:29
  185.8 8.2 %collective-permute-start.29 = (f32[100,1,128]{0,1,2:T(1,128)S(1)}, f32[100,1,128]{0,1,2:T(1,128)S(1)}, u32[]{:S(2)}, u32[]{:S(2)}) collective-permute-start(f32[100,1,128]{0,1,2:T(1,128)S(1)} %get-tuple-element.21), channel_id=1, source_target_pairs={{0,1},{1,2},{2,3},{4,5},{5,6},{6,7},{8,9},{9,10},{10,11},{12,13},{... | collective-permute-start | bytes 153608 | tf_op jit(solution)/shard_map/ppermute | solution.py:26
  194.1 2.9 %collective-permute-start.31 = (f32[100,18,1]{0,1,2:T(8,128)S(1)}, f32[100,18,1]{0,1,2:T(8,128)S(1)}, u32[]{:S(2)}, u32[]{:S(2)}) collective-permute-start(f32[100,18,1]{0,1,2:T(8,128)S(1)} %get-tuple-element.4), channel_id=1, source_target_pairs={{4,0},{8,4},{12,8},{16,12},{20,16},{24,20},{28,24},{32,28},{36,32}... | collective-permute-start | bytes 21608 | tf_op jit(solution)/shard_map/ppermute | solution.py:29
  194.2 6.8 %collective-permute-start.32 = (f32[100,18,1]{0,1,2:T(8,128)S(1)}, f32[100,18,1]{0,1,2:T(8,128)S(1)}, u32[]{:S(2)}, u32[]{:S(2)}) collective-permute-start(f32[100,18,1]{0,1,2:T(8,128)S(1)} %get-tuple-element.5), channel_id=1, source_target_pairs={{0,4},{4,8},{8,12},{12,16},{16,20},{20,24},{24,28},{28,32},{32,36}... | collective-permute-start | bytes 21608 | tf_op jit(solution)/shard_map/ppermute | solution.py:26
  (12 other events, 74.7 us)

commit v2 on v1

--- a/solution.py
+++ b/solution.py
@@ -1,3 +1,5 @@
+import functools
+
 import jax
 import jax.numpy as jnp
 from jax import lax
@@ -5,57 +7,228 @@
 from jax.experimental.pallas import tpu as pltpu
 from jax.sharding import PartitionSpec as P
 
-SWEEPS = 4
+MESH = pl.DeviceIdType.MESH
+DEEP = 4
+STRIP = 10
+
+def root_kernel(first, unroll, *refs):
+    if first:
+        (x_ref, lon_ref, lat_ref, out_ref, coef_out, *scratch) = refs
+    else:
+        (x_ref, coef_ref, out_ref, *scratch) = refs
+    (main, main2, side, side2, zonal, merid, centre, packed, left, right, *scratch) = scratch
+    if first:
+        (coef, square, *scratch) = scratch
+    send_sems, recv_sems = scratch
+    fields, rows, cols = x_ref.shape
+    ext = rows + 2 * DEEP
+    n_lon, n_lat = lax.axis_size("lon"), lax.axis_size("lat")
+    lon, lat = lax.axis_index("lon"), lax.axis_index("lat")
+    west, east = lax.rem(lon + n_lon - 1, n_lon), lax.rem(lon + 1, n_lon)
+    has_up, has_down = lat > 0, lat < n_lat - 1
+    lane = lax.broadcasted_iota(jnp.int32, (8, cols), 1)
+
+    barrier = pltpu.get_barrier_semaphore()
+
+    def greet(there_lon, there_lat):
+        pl.semaphore_signal(barrier, inc=1, device_id={"lon": there_lon, "lat": there_lat}, device_id_type=MESH)
+
+    greet(west, lat)
+    greet(east, lat)
+    for present, there_lat in ((has_up, lat - 1), (has_down, lat + 1)):
+        @pl.when(present)
+        def _():
+            for there_lon in (lon, west, east):
+                greet(there_lon, there_lat)
+
+    kinds = iter(range(16))
+
+    def sending(source, target, there_lon, there_lat):
+        kind = next(kinds)
+        return pltpu.make_async_remote_copy(
+            src_ref=source, dst_ref=target, send_sem=send_sems.at[kind], recv_sem=recv_sems.at[kind],
+            device_id={"lon": there_lon, "lat": there_lat}, device_id_type=MESH,
+        )
+
+    low, high, own = pl.ds(0, DEEP), pl.ds(rows + DEEP, DEEP), pl.ds(DEEP, rows)
+    top, bottom = pl.ds(0, DEEP), pl.ds(rows - DEEP, DEEP)
+    up_main = sending(x_ref.at[:, top], main.at[:, high], lon, lat - 1)
+    down_main = sending(x_ref.at[:, bottom], main.at[:, low], lon, lat + 1)
+    to_west = sending(packed, right.at[:, own], west, lat)
+    to_east = sending(packed, left.at[:, own], east, lat)
+    up_west = sending(packed.at[:, top], right.at[:, high], west, lat - 1)
+    up_east = sending(packed.at[:, top], left.at[:, high], east, lat - 1)
+    down_west = sending(packed.at[:, bottom], right.at[:, low], west, lat + 1)
+    down_east = sending(packed.at[:, bottom], left.at[:, low], east, lat + 1)
+    ups, downs, flats = [up_main, up_west, up_east], [down_main, down_west, down_east], [to_west, to_east]
+    if first:
+        pair = pl.ds(0, 2)
+        up_coef = sending(coef.at[pair, pl.ds(DEEP, DEEP)], coef.at[pair, high], lon, lat - 1)
+        down_coef = sending(coef.at[pair, pl.ds(rows, DEEP)], coef.at[pair, low], lon, lat + 1)
+        ups.append(up_coef)
+        downs.append(down_coef)
+        square[...] = jnp.zeros_like(square)
+        square[pl.ds(0, fields), pl.ds(0, rows)] = lon_ref[...]
+        square[pl.ds(0, fields), pl.ds(64, rows)] = lat_ref[...]
+        turned = square[...].T
+        coef[0, own] = turned[0:rows]
+        row = lax.broadcasted_iota(jnp.int32, (rows, cols), 0)
+        closed = jnp.logical_and(row == rows - 1, lat == n_lat - 1)
+        coef[1, own] = jnp.where(closed, 0.0, turned[64:64 + rows])
+
+    @pl.loop(0, fields // STRIP)
+    def _(g):
+        for part in range(rows // 8):
+            strips = None
+            for k in range(STRIP):
+                value = x_ref[g * STRIP + k, pl.ds(8 * part, 8), :]
+                if k == 0:
+                    strips = value
+                else:
+                    key = lax.shift_right_logical(lax.bitwise_and(lane + 4, 127), 3)
+                    strips = jnp.where(key == k, pltpu.roll(value, 8 * k, 1), strips)
+            packed[g, pl.ds(8 * part, 8), :] = strips
+
+    pl.semaphore_wait(barrier, 2 + 3 * has_up.astype(jnp.int32) + 3 * has_down.astype(jnp.int32))
+
+    for present, group, at in ((has_up, ups, low), (has_down, downs, high)):
+        @pl.when(present)
+        def _():
+            for copy in (group if not first else group[-1:] + group[:-1]):
+                copy.start()
+
+        @pl.when(jnp.logical_not(present))
+        def _():
+            main[:, at] = jnp.zeros((fields, DEEP, cols), jnp.float32)
+            for halo in (left, right):
+                halo[:, at] = jnp.zeros((fields // STRIP, DEEP, cols), jnp.float32)
+            if first:
+                coef[pl.ds(0, 2), at] = jnp.zeros((2, DEEP, cols), jnp.float32)
+
+    for copy in flats:
+        copy.start()
+
+    @pl.loop(0, fields // 10)
+    def _(g):
+        for k in range(10):
+            for part in range(rows // 8):
+                main[g * 10 + k, pl.ds(DEEP + 8 * part, 8), :] = x_ref[g * 10 + k, pl.ds(8 * part, 8), :]
+
+    if first:
+        @pl.when(has_up)
+        def _():
+            down_coef.wait_recv()
+
+        @pl.when(has_down)
+        def _():
+            up_coef.wait_recv()
+
+        coef[2] = jnp.zeros((ext, cols), jnp.float32)
+        for start in (1, 9, ext - 9):
+            at = pl.ds(start, 8)
+            coef[2, at] = 1.0 - 2.0 * coef[0, at] - coef[1, at] - coef[1, pl.ds(start - 1, 8)]
+        coef_ref = coef
+        coef_out[...] = coef[...]
+
+    @pl.loop(0, fields // 5)
+    def _(g):
+        tables = [[coef_ref[k, pl.ds(8 * part, 8), :] for part in range(ext // 8)] for k in range(3)]
+        for k in range(5):
+            f = g * 5 + k
+            which = jnp.full((8, cols), f, jnp.int32)
+            for table, target in zip(tables, (zonal, merid, centre)):
+                for part in range(ext // 8):
+                    target[f, pl.ds(8 * part, 8), :] = jnp.take_along_axis(
+                        table[part], which, axis=1, mode="promise_in_bounds")
+
+    for copy in flats:
+        copy.wait_recv()
+
+    @pl.when(has_up)
+    def _():
+        for copy in downs[:3]:
+            copy.wait_recv()
+
+    @pl.when(has_down)
+    def _():
+        for copy in ups[:3]:
+            copy.wait_recv()
+
+    @pl.loop(0, fields // STRIP)
+    def _(g):
+        for part in range(ext // 8):
+            at = pl.ds(8 * part, 8)
+            both = jnp.where(lax.bitwise_and(lane, 7) >= 4, left[g, at, :], right[g, at, :])
+            for k in range(STRIP):
+                side[g * STRIP + k, at, :] = pltpu.roll(both, (-8 * k) % 128, 1) if k else both
+
+    def sweep(source, source_side, target, target_side, starts, shift):
+        @pl.loop(0, fields // unroll)
+        def _(g):
+            for k in range(unroll):
+                f = g * unroll + k
+                for start in starts:
+                    at, before, after = pl.ds(start, 8), pl.ds(start - 1, 8), pl.ds(start + 1, 8)
+                    m, e = source[f, at, :], source_side[f, at, :]
+                    m_w, e_w, m_e, e_e = (pltpu.roll(m, 1, 1), pltpu.roll(e, 1, 1), pltpu.roll(m, 127, 1), pltpu.roll(e, 127, 1))
+                    c, z, n, s = centre[f, at, :], zonal[f, at, :], merid[f, at, :], merid[f, before, :]
+                    out = c * m + z * (jnp.where(lane == 0, e_w, m_w) + jnp.where(lane == 127, e_e, m_e))
+                    out = out + n * source[f, after, :] + s * source[f, before, :]
+                    target[f, pl.ds(start - shift, 8), :] = out
+                    if target_side is not None:
+                        out = c * e + z * (jnp.where(lane == 0, m_w, e_w) + jnp.where(lane == 127, m_e, e_e))
+                        out = out + n * source_side[f, after, :] + s * source_side[f, before, :]
+                        target_side[f, at, :] = out
+
+    sweep(main, side, main2, side2, (1, 9, 15), 0)
+    sweep(main2, side2, main, side, (2, 10, 14), 0)
+    sweep(main, side, main2, side2, (3, 11, 13), 0)
+    sweep(main2, side2, out_ref, None, (4, 12), 4)
+
+    for copy in flats:
+        copy.wait_send()
+
+    @pl.when(has_up)
+    def _():
+        for copy in ups:
+            copy.wait_send()
+
+    @pl.when(has_down)
+    def _():
+        for copy in downs:
+            copy.wait_send()
+
+
+def root(field, coefs, first, unroll=5):
+    fields, rows, cols = field.shape
+    ext = rows + 2 * DEEP
+    vmem = pl.BlockSpec(memory_space=pltpu.VMEM)
+    f32 = lambda *shape: jax.ShapeDtypeStruct(shape, jnp.float32)
+    big = pltpu.VMEM((fields, ext, cols), jnp.float32)
+    strips = fields // STRIP
+    scratch = [big] * 7 + [pltpu.VMEM((strips, rows, cols), jnp.float32)] + [pltpu.VMEM((strips, ext, cols), jnp.float32)] * 2
+    outs = [f32(fields, rows, cols)]
+    if first:
+        scratch += [pltpu.VMEM((3, ext, cols), jnp.float32), pltpu.VMEM((128, 128), jnp.float32)]
+        outs.append(f32(3, ext, cols))
+    count = 10 if first else 8
+    scratch += [pltpu.SemaphoreType.DMA((count,))] * 2
+    return pl.pallas_call(
+        functools.partial(root_kernel, first, unroll),
+        out_shape=outs,
+        in_specs=[vmem] * (1 + len(coefs)),
+        out_specs=[vmem] * len(outs),
+        scratch_shapes=scratch,
+        compiler_params=pltpu.CompilerParams(
+            collective_id=0 if first else 1, has_side_effects=True, vmem_limit_bytes=48 * 2**20),
+        name="root_first" if first else "root_second",
+    )(field, *coefs)
+
+
 PAD = 8
 NACC = 8
 
-
-def passed_along(value, axis, steps):
-    count = lax.axis_size(axis)
-    leading, last = (max(0, -steps), min(count, count - steps))
-    return lax.ppermute(value, axis, [(source, source + steps) for source in range(leading, last)])
-
-
-def padded_2(block, sides, width, periodic):
-    for axis, dim in sides:
-        count = lax.axis_size(axis)
-        forward = [(i, i + 1) for i in range(count - 1)]
-        if periodic:
-            forward.append((count - 1, 0))
-        backward = [(target, source) for source, target in forward]
-        low = lax.ppermute(
-            lax.slice_in_dim(block, block.shape[dim] - width, None, axis=dim), axis, forward
-        )
-        high = lax.ppermute(lax.slice_in_dim(block, 0, width, axis=dim), axis, backward)
-        block = jnp.concatenate([low, block, high], axis=dim)
-    return block
-
-
-def diffuse_step(padded, zonal_rate, merid_rate):
-    centre = padded[:, 1:-1, 1:-1]
-    zonal = padded[:, 1:-1, 2:] + padded[:, 1:-1, :-2] - 2.0 * centre
-    north = merid_rate[:, 1:-1, None] * (padded[:, 2:, 1:-1] - centre)
-    south = merid_rate[:, :-2, None] * (centre - padded[:, :-2, 1:-1])
-    return centre + zonal_rate[:, 1:-1, None] * zonal + north - south
-
-
-def rate_rims(rates):
-    below = passed_along(rates[1][:, -1:], "lat", 1)
-    blank = jnp.zeros_like(below)
-    zonal_rim = jnp.pad(rates[0], ((0, 0), (1, 1)))
-    merid_rim = jnp.concatenate([below, rates[1], blank], axis=1)
-    return jnp.stack([zonal_rim, merid_rim])
-
-
-def covariance_root(field, rate_rim):
-    for step in range(SWEEPS):
-        padded = padded_2(field, (("lat", 1),), 1, False)
-        padded = padded_2(padded, (("lon", 2),), 1, True)
-        field = diffuse_step(padded, rate_rim[0], rate_rim[1])
-    return field
-
-
-def obs_kernel(cnt_ref, tab_ref, base_ref, field_ref, w_ref, val_ref, prec_ref, out_ref,
+def obs_kernel(cnt_ref, tab_ref, base_ref, field_ref, w_ref, val_ref, prec_ref, inc_ref, out_ref,
                tab, stack, dense, cidx, ridx, ridx_s, sem, *accs):
     rows = tab_ref.shape[0]
     cells = 16 * 128
@@ -67,7 +240,9 @@
     def _(i):
         for k in range(10):
             at = pl.multiple_of(i * 80 + 8 * k, 8)
-            tab[pl.ds(at + PAD, 8), :] = tab_ref[pl.ds(at, 8), :]
+            value = tab_ref[pl.ds(at, 8), :]
+            tab[pl.ds(at + PAD, 8), :] = value
+            inc_ref[pl.ds(at, 8), :] = value
 
     tab[pl.ds(0, 8), :] = zero
     tab[pl.ds(rows + PAD, 8), :] = zero
@@ -191,9 +366,9 @@
     smem = pl.BlockSpec(memory_space=pltpu.SMEM)
     return pl.pallas_call(
         obs_kernel,
-        out_shape=jax.ShapeDtypeStruct((rows, cols), jnp.float32),
+        out_shape=[jax.ShapeDtypeStruct((rows, cols), jnp.float32)] * 2,
         in_specs=[smem] + [vmem] * 6,
-        out_specs=vmem,
+        out_specs=[vmem] * 2,
         scratch_shapes=[
             pltpu.VMEM((rows + 2 * PAD, cols), jnp.float32),
             pltpu.VMEM((1024, 128), jnp.float32),
@@ -220,15 +395,10 @@
     obs_precision,
 ):
     fields, band_rows, block_cols = control.shape
-    lat_devices = lax.axis_size("lat")
-    lat_rows = lax.axis_index("lat") * band_rows + jnp.arange(band_rows, dtype=jnp.int32)
-    open_face = (lat_rows < band_rows * lat_devices - 1).astype(jnp.float32)
-    rates = jnp.stack([lon_coef, lat_coef * open_face[None, :]])
-    rate_rim = rate_rims(rates)
-    increment = covariance_root(control, rate_rim)
     sent = jnp.stack([obs_value[0], obs_precision[0]], axis=1)
     held = lax.all_to_all(sent, ("lon", "lat"), split_axis=0, concat_axis=0, tiled=True)
-    forcing = observe(
+    increment, coefs = root(control, (lon_coef, lat_coef), True)
+    increment, forcing = observe(
         increment.reshape(fields * band_rows, block_cols),
         obs_count,
         obs_base[0],
@@ -237,8 +407,8 @@
         held[:, 0],
         held[:, 1],
     )
-    adjoint = covariance_root(forcing.reshape(fields, band_rows, block_cols), rate_rim)
-    return (increment, control + adjoint)
+    (adjoint,) = root(forcing.reshape(control.shape), (coefs,), False)
+    return (increment.reshape(control.shape), control + adjoint)
 
 
 def solution(mesh):

time: 205 us -> 100 us (0.49)
  starting transfers between devices: 105 us -> 11.5 us
  Pallas kernels: 31.3 us -> 82 us
  waiting for transfers between devices: 50.3 us -> 0.01 us
  other arithmetic: 8.23 us -> 2.64 us
  local copies, waits for them, and re-layouts: 6.83 us -> 2.86 us
    ppermute x33 -> x0, starting transfers between devices: 102 us -> none  [the longest x16 55.9 us: padded_2(): lax.ppermute(lax.slice_in_dim(block, block.shape[dim] - width, None, axis...]
    pallas_call x1 -> x3, Pallas kernels: 31.3 us -> 82 us  [the longest x2 47.3 us: root(): pl.pallas_call(functools.partial(root_kernel, first, unroll), out_shape=o...]
    ppermute x33 -> x0, waiting for transfers between devices: 47.2 us -> none  [the longest x16 40.5 us: padded_2(): lax.ppermute(lax.slice_in_dim(block, block.shape[dim] - width, None, axis...]
    all_to_all x1, starting transfers between devices: 3.54 us -> 11.5 us  [per_device(): lax.all_to_all(sent, ('lon', 'lat'), split_axis=0, concat_axis=0, tiled=T...]
    sub x7 -> x0, other arithmetic: 6.46 us -> none  [diffuse_step(): return centre + zonal_rate[:, 1:-1, None] * zonal + north - south]
    all_to_all x1, waiting for transfers between devices: 3.09 us -> 0.01 us  [per_device(): lax.all_to_all(sent, ('lon', 'lat'), split_axis=0, concat_axis=0, tiled=T...]
    unnamed x23 -> x18, local copies, waits for them, and re-layouts: 5.3 us -> 2.76 us
  transfers between devices with their start and end apart: 34 -> 1, of which waited for: 21 -> 0; matrix products, arithmetic and copies ran while one was open for 0% -> 0% of each run, Pallas kernels for 0% -> 25%
where the time goes in v2:
time: 100 us; the launch traced here: 99.7 us
  Pallas kernels  82 us (82%)
  starting transfers between devices  11.5 us (12%)
  local copies, waits for them, and re-layouts  2.86 us (3%)
  other arithmetic  2.64 us (3%)
    pallas_call x2, Pallas kernels, root(): pl.pallas_call(functools.partial(root_kernel, first, unroll), out_shape=o...  47.3 us
    pallas_call x1, Pallas kernels, observe(): pl.pallas_call(obs_kernel, out_shape=[jax.ShapeDtypeStruct((rows, cols),...  34.7 us
    all_to_all x1, starting transfers between devices, per_device(): lax.all_to_all(sent, ('lon', 'lat'), split_axis=0, concat_axis=0, tiled=T...  11.5 us
    unnamed x18, local copies, waits for them, and re-layouts  2.76 us
  transfers between devices with their start and end apart: 1, of which 0 were waited for; matrix products, arithmetic and copies ran while one was open for 0% of the time, Pallas kernels for 25%

profile of v2, /device:TPU:1, one launch (start us, length us, event | category | flops | bytes accessed | tf_op | source)
XLA Modules:
  0.0 99.7 jit_solution(7720747522598337622)
XLA Ops:
  0.6 1.6 %pad_maximum_fusion = f32[128,2,128]{2,1,0:T(2,128)} fusion(f32[128,1,128]{2,1,0:T(1,128)} %bitcast.21, f32[128,1,128]{2,1,0:T(1,128)} %bitcast.22), kind=kLoop, calls=%fused_computation | loop fusion | flops 32768 | bytes 262144 | tf_op jit(solution)/shard_map/stack | solution.py:398
  2.3 0.0 copy-start.6
  2.3 11.5 %all-to-all-start = ((f32[128,2,128]{2,1,0:T(2,128)}), f32[128,2,128]{2,1,0:T(2,128)S(1)}, u32[]{:S(2)}, u32[]{:S(2)}) async-start(f32[128,2,128]{2,1,0:T(2,128)} %pad_maximum_fusion), calls=%async_computation | async-start | bytes 262144 | tf_op jit(solution)/shard_map/all_to_all | solution.py:399
  13.8 0.0 copy-done.6
  13.8 0.0 copy-start.7
  13.8 0.1 copy.13.refs_1_
  13.9 0.6 copy-done.7
  14.5 0.1 copy.14.refs_2_
  14.6 0.0 copy-start
  14.6 1.1 %copy-done = f32[100,16,128]{2,1,0:T(8,128)S(1)} copy-done((f32[100,16,128]{2,1,0:T(8,128)S(1)}, f32[100,16,128]{2,1,0:T(8,128)}, u32[]{:S(2)}) %copy-start) | copy-done | bytes 819224
  15.7 0.0 copy-start.3
  15.7 0.0 copy-start.4
  15.8 25.3 %root_first.1 = (f32[100,16,128]{2,1,0:T(8,128)S(1)}, f32[3,24,128]{2,1,0:T(8,128)S(1)}) custom-call(f32[100,16,128]{2,1,0:T(8,128)S(1)} %copy-done, f32[100,16]{1,0:T(8,128)S(1)} %copy.13.refs_1_, f32[100,16]{1,0:T(8,128)S(1)} %copy.14.refs_2_), custom_call_target="tpu_custom_call" | custom-call | tf_op jit(solution)/shard_map/root_first/pallas_call | solution.py:216
  41.1 0.0 copy-start.2
  41.1 0.0 all-to-all-done
  41.1 0.1 fusion
  41.2 0.0 copy-start.5
  41.2 0.0 copy-done.3
  41.2 0.0 copy-done.4
  41.3 0.8 copy-done.2
  42.0 0.0 copy-done.5
  42.0 34.7 %observe.1 = (f32[1600,128]{1,0:T(8,128)}, f32[1600,128]{1,0:T(8,128)S(1)}) custom-call(s32[1,128]{1,0:T(1,128)S(1)} %copy-done.5, f32[1600,128]{1,0:T(8,128)S(1)} %bitcast.14, s32[128,128]{1,0:T(8,128)S(1)} %bitcast.19, s32[128,128]{1,0:T(8,128)S(1)} %bitcast.20, f32[4,128,128]{2,1,0:T(8,128)S(1)} %bitcast.16, f32[128,128]{1,0:T(8,128)S(1)} %bitcast.18, ...), custom_call_target="tpu_custom_call" | custom-call | tf_op jit(solution)/shard_map/observe/pallas_call | solution.py:367
  76.7 0.0 copy-start.1
  76.8 22.0 %root_second.1 = f32[100,16,128]{2,1,0:T(8,128)S(1)} custom-call(f32[100,16,128]{2,1,0:T(8,128)S(1)} %bitcast.15, f32[3,24,128]{2,1,0:T(8,128)S(1)} %get-tuple-element.9.refs_1_), custom_call_target="tpu_custom_call" | custom-call | tf_op jit(solution)/shard_map/root_second/pallas_call | solution.py:216
  98.7 0.0 copy-done.1
  98.8 1.0 add.3
Async XLA Ops:
  2.3 11.5 %copy-start.6 = (f32[100,16]{0,1:T(8,128)S(1)}, f32[100,16]{0,1:T(8,128)}, u32[]{:S(2)}) copy-start(f32[100,16]{0,1:T(8,128)} %param.10) | copy-start | bytes 19204
  2.3 38.8 %all-to-all-start = ((f32[128,2,128]{2,1,0:T(2,128)}), f32[128,2,128]{2,1,0:T(2,128)S(1)}, u32[]{:S(2)}, u32[]{:S(2)}) async-start(f32[128,2,128]{2,1,0:T(2,128)} %pad_maximum_fusion), calls=%async_computation | async-start | bytes 262144 | tf_op jit(solution)/shard_map/all_to_all | solution.py:399
  13.8 0.7 copy-start.7
  14.6 1.1 %copy-start = (f32[100,16,128]{2,1,0:T(8,128)S(1)}, f32[100,16,128]{2,1,0:T(8,128)}, u32[]{:S(2)}) copy-start(f32[100,16,128]{2,1,0:T(8,128)} %refs_0_.1) | copy-start | bytes 2457604
  15.7 25.5 %copy-start.3 = (s32[1,128,128]{2,1,0:T(8,128)S(1)}, s32[1,128,128]{2,1,0:T(8,128)}, u32[]{:S(2)}) copy-start(s32[1,128,128]{2,1,0:T(8,128)} %param.12) | copy-start | bytes 196612
  15.7 25.5 %copy-start.4 = (s32[1,128,128]{2,1,0:T(8,128)S(1)}, s32[1,128,128]{2,1,0:T(8,128)}, u32[]{:S(2)}) copy-start(s32[1,128,128]{2,1,0:T(8,128)} %param.13) | copy-start | bytes 196612
  41.1 1.0 copy-start.2
  41.2 0.8 copy-start.5
  76.7 22.0 %copy-start.1 = (f32[100,16,128]{2,1,0:T(8,128)S(1)}, f32[100,16,128]{2,1,0:T(8,128)}, u32[]{:S(2)}) copy-start(f32[100,16,128]{2,1,0:T(8,128)} %refs_0_.1) | copy-start | bytes 2457604

commit v3 on v2

v3 whole, which is shorter than its diff:
```python
import functools

import jax
import jax.numpy as jnp
from jax import lax
from jax.experimental import pallas as pl
from jax.experimental.pallas import tpu as pltpu
from jax.sharding import PartitionSpec as P

MESH = pl.DeviceIdType.MESH
DEEP = 4
STRIP = 10
GROUP = 20
UNROLL = 20


LANES = lax.GatherDimensionNumbers(
    offset_dims=(), collapsed_slice_dims=(1,), start_index_map=(1,),
    operand_batching_dims=(0,), start_indices_batching_dims=(0,))


def pick_lanes(value, index):
    return lax.gather(value, index[:, :, None], LANES, slice_sizes=(1, 1), mode="promise_in_bounds")


def root_kernel(first, *refs):
    if first:
        (x_ref, zonal_ref, merid_ref, value_ref, precision_ref, out_ref, coef_out, value_out, precision_out, *scratch) = refs
        (coef, value_mid, precision_mid, near_sems, far_sems, own_sems, *scratch) = scratch
    else:
        (x_ref, coef, out_ref, *scratch) = refs
    (main, main2, side, side2, zonal, merid, centre, packed, left, right, send_sems, recv_sems) = scratch
    fields, rows, cols = x_ref.shape
    ext = rows + 2 * DEEP
    groups, strips = fields // GROUP, GROUP // STRIP
    n_lon, n_lat = lax.axis_size("lon"), lax.axis_size("lat")
    lon, lat = lax.axis_index("lon"), lax.axis_index("lat")
    west, east = lax.rem(lon + n_lon - 1, n_lon), lax.rem(lon + 1, n_lon)
    has_up, has_down = lat > 0, lat < n_lat - 1
    lane = lax.broadcasted_iota(jnp.int32, (8, cols), 1)
    low, high, own = pl.ds(0, DEEP), pl.ds(rows + DEEP, DEEP), pl.ds(DEEP, rows)
    top, bottom = pl.ds(0, DEEP), pl.ds(rows - DEEP, DEEP)

    barrier = pltpu.get_barrier_semaphore()

    def greet(there_lon, there_lat):
        pl.semaphore_signal(barrier, inc=1, device_id={"lon": there_lon, "lat": there_lat}, device_id_type=MESH)

    sides = has_up.astype(jnp.int32) + has_down.astype(jnp.int32)
    for present, there_lat in ((has_up, lat - 1), (has_down, lat + 1)):
        @pl.when(present)
        def _():
            for there_lon in (west, east) if first else (lon, west, east):
                greet(there_lon, there_lat)

    if first:
        for k in range(1, n_lat):
            greet(lon, lax.rem(lat + k, n_lat))

        @pl.loop(1, n_lon)
        def _(k):
            greet(lax.rem(lon + k, n_lon), lat)

        greetings = 2 * sides + (n_lat - 1) + (n_lon - 1)
    else:
        greet(west, lat)
        greet(east, lat)
        greetings = 3 * sides + 2

    def remote(source, target, send, recv, there_lon, there_lat):
        return pltpu.make_async_remote_copy(
            src_ref=source, dst_ref=target, send_sem=send, recv_sem=recv,
            device_id={"lon": there_lon, "lat": there_lat}, device_id_type=MESH,
        )

    def exchange(kind, g):
        fs, ss = pl.ds(g * GROUP, GROUP), pl.ds(g * strips, strips)
        source, target, there_lon, there_lat = {
            "up_main": (x_ref.at[fs, top], main.at[fs, high], lon, lat - 1),
            "up_west": (packed.at[ss, top], right.at[ss, high], west, lat - 1),
            "up_east": (packed.at[ss, top], left.at[ss, high], east, lat - 1),
            "down_main": (x_ref.at[fs, bottom], main.at[fs, low], lon, lat + 1),
            "down_west": (packed.at[ss, bottom], right.at[ss, low], west, lat + 1),
            "down_east": (packed.at[ss, bottom], left.at[ss, low], east, lat + 1),
            "west": (packed.at[ss], right.at[ss, own], west, lat),
            "east": (packed.at[ss], left.at[ss, own], east, lat),
        }[kind]
        slot = KINDS.index(kind)
        return remote(source, target, send_sems.at[slot, g], recv_sems.at[slot, g], there_lon, there_lat)

    def exchange_coef(kind):
        pair, slot = pl.ds(0, 2), KINDS.index(kind)
        source, target, there_lat = {
            "up_coef": (coef.at[pair, pl.ds(DEEP, DEEP)], coef.at[pair, high], lat - 1),
            "down_coef": (coef.at[pair, pl.ds(rows, DEEP)], coef.at[pair, low], lat + 1),
        }[kind]
        return remote(source, target, send_sems.at[slot, 0], recv_sems.at[slot, 0], lon, there_lat)

    if first:
        row = lax.broadcasted_iota(jnp.int32, (rows, fields), 0)
        closed = jnp.logical_and(row == rows - 1, lat == n_lat - 1)
        blank = jnp.zeros((rows, cols), jnp.float32)
        for k, rates in enumerate((zonal_ref[...], jnp.where(closed, 0.0, merid_ref[...]))):
            coef[k, own] = blank
            coef[k, own, pl.ds(0, fields)] = rates

    pl.semaphore_wait(barrier, greetings)

    for present, way, at in ((has_up, "up", low), (has_down, "down", high)):
        @pl.when(present)
        def _():
            if first:
                exchange_coef(way + "_coef").start()

            @pl.loop(0, groups)
            def _(g):
                exchange(way + "_main", g).start()

        @pl.when(jnp.logical_not(present))
        def _():
            main[:, at] = jnp.zeros((fields, DEEP, cols), jnp.float32)
            for halo in (left, right):
                halo[:, at] = jnp.zeros((fields // STRIP, DEEP, cols), jnp.float32)
            if first:
                coef[pl.ds(0, 2), at] = jnp.zeros((2, DEEP, cols), jnp.float32)

    key = lax.shift_right_logical(lax.bitwise_and(lane + 4, 127), 3)

    @pl.loop(0, groups)
    def _(g):
        for s in range(strips):
            for part in range(rows // 8):
                at = pl.ds(8 * part, 8)
                strip = x_ref[g * GROUP + s * STRIP, at, :]
                for k in range(1, STRIP):
                    value = x_ref[g * GROUP + s * STRIP + k, at, :]
                    strip = jnp.where(key == k, pltpu.roll(value, 8 * k, 1), strip)
                packed[g * strips + s, at, :] = strip
        exchange("west", g).start()
        exchange("east", g).start()
        for present, way in ((has_up, "up"), (has_down, "down")):
            @pl.when(present)
            def _():
                exchange(way + "_west", g).start()
                exchange(way + "_east", g).start()

    if first:
        pairs = ((value_ref, value_mid, value_out), (precision_ref, precision_mid, precision_out))

        def near(n, k):
            source, target, _ = pairs[n]
            there = lax.rem(lat + k, n_lat)
            return remote(source.at[:, there], target.at[lat], near_sems.at[0, n, k], near_sems.at[1, n, k], lon, there)

        def far(n, k):
            _, source, target = pairs[n]
            there = lax.rem(lon + k, n_lon)
            return remote(source.at[:, there], target.at[lon], far_sems.at[0, n, k], far_sems.at[1, n, k], there, lat)

        def stays(n, stage):
            source, middle, target = pairs[n]
            if stage == 0:
                return pltpu.make_async_copy(source.at[:, lat], middle.at[lat], own_sems.at[0, n])
            return pltpu.make_async_copy(middle.at[:, lon], target.at[lon], own_sems.at[1, n])

        for n in range(2):
            for k in range(1, n_lat):
                near(n, k).start()
            stays(n, 0).start()

    @pl.loop(0, fields // 10)
    def _(g):
        for k in range(10):
            for part in range(rows // 8):
                main[g * 10 + k, pl.ds(DEEP + 8 * part, 8), :] = x_ref[g * 10 + k, pl.ds(8 * part, 8), :]

    def spread_tables(tables, targets):
        @pl.loop(0, fields // 10)
        def _(g):
            for k in range(10):
                f = g * 10 + k
                which = jnp.full((8, cols), f, jnp.int32)
                for table, (target, places) in zip(tables, targets):
                    value = pick_lanes(table, which)
                    for start, size, at in places:
                        target[f, pl.ds(at, size), :] = value[start:start + size]

    whole = lambda at: ((0, 8, at),)
    if first:
        spread_tables(
            [coef[k, pl.ds(at, 8), :] for k in range(2) for at in (DEEP, DEEP + 8)],
            [(target, whole(at)) for target in (zonal, merid) for at in (DEEP, DEEP + 8)],
        )
        for n in range(2):
            for k in range(1, n_lat):
                near(n, k).wait_recv()
            stays(n, 0).wait()

        @pl.loop(1, n_lon)
        def _(k):
            for n in range(2):
                far(n, k).start()

        for n in range(2):
            stays(n, 1).start()

        for present, way in ((has_up, "down_coef"), (has_down, "up_coef")):
            @pl.when(present)
            def _():
                exchange_coef(way).wait_recv()

        coef[2] = jnp.zeros((ext, cols), jnp.float32)
        for start in (1, 9, ext - 9):
            at = pl.ds(start, 8)
            coef[2, at] = 1.0 - 2.0 * coef[0, at] - coef[1, at] - coef[1, pl.ds(start - 1, 8)]
        coef_out[...] = coef[...]
        rims = [jnp.concatenate([coef[k, low], coef[k, high]], axis=0) for k in range(2)]
        parts = ((0, DEEP, 0), (DEEP, DEEP, rows + DEEP))
        spread_tables(
            rims + [coef[2, pl.ds(8 * part, 8), :] for part in range(ext // 8)],
            [(zonal, parts), (merid, parts)] + [(centre, whole(8 * part)) for part in range(ext // 8)],
        )
    else:
        spread_tables(
            [coef[k, pl.ds(8 * part, 8), :] for k in range(3) for part in range(ext // 8)],
            [(target, whole(8 * part)) for target in (zonal, merid, centre) for part in range(ext // 8)],
        )

    def sweep(g, source, source_side, target, target_side, starts, shift):
        def fields_from(base):
            for k in range(UNROLL):
                f = base + k
                for start in starts:
                    at, before, after = pl.ds(start, 8), pl.ds(start - 1, 8), pl.ds(start + 1, 8)
                    m, e = source[f, at, :], source_side[f, at, :]
                    m_w, e_w = pltpu.roll(m, 1, 1), pltpu.roll(e, 1, 1)
                    m_e, e_e = pltpu.roll(m, 127, 1), pltpu.roll(e, 127, 1)
                    c, z, n, s = centre[f, at, :], zonal[f, at, :], merid[f, at, :], merid[f, before, :]
                    out = c * m + z * (jnp.where(lane == 0, e_w, m_w) + jnp.where(lane == 127, e_e, m_e))
                    out = out + n * source[f, after, :] + s * source[f, before, :]
                    target[f, pl.ds(start - shift, 8), :] = out
                    if target_side is not None:
                        out = c * e + z * (jnp.where(lane == 0, m_w, e_w) + jnp.where(lane == 127, m_e, e_e))
                        out = out + n * source_side[f, after, :] + s * source_side[f, before, :]
                        target_side[f, at, :] = out

        if UNROLL == GROUP:
            fields_from(g * GROUP)
        else:
            @pl.loop(0, GROUP // UNROLL)
            def _(u):
                fields_from(g * GROUP + u * UNROLL)

    @pl.loop(0, groups)
    def _(g):
        for kind in ("west", "east"):
            exchange(kind, g).wait_recv()
        for present, way in ((has_up, "down"), (has_down, "up")):
            @pl.when(present)
            def _():
                for kind in ("_main", "_west", "_east"):
                    exchange(way + kind, g).wait_recv()

        for s in range(strips):
            for part in range(ext // 8):
                at = pl.ds(8 * part, 8)
                both = jnp.where(lax.bitwise_and(lane, 7) >= 4, left[g * strips + s, at, :], right[g * strips + s, at, :])
                for k in range(STRIP):
                    side[g * GROUP + s * STRIP + k, at, :] = pltpu.roll(both, (-8 * k) % 128, 1) if k else both

        sweep(g, main, side, main2, side2, (1, 9, 15), 0)
        sweep(g, main2, side2, main, side, (2, 10, 14), 0)
        sweep(g, main, side, main2, side2, (3, 11, 13), 0)
        sweep(g, main2, side2, out_ref, None, (4, 12), 4)

    @pl.loop(0, groups)
    def _(g):
        for kind in ("west", "east"):
            exchange(kind, g).wait_send()
        for present, way in ((has_up, "up"), (has_down, "down")):
            @pl.when(present)
            def _():
                for kind in ("_main", "_west", "_east"):
                    exchange(way + kind, g).wait_send()

    if first:
        for present, way in ((has_up, "up_coef"), (has_down, "down_coef")):
            @pl.when(present)
            def _():
                exchange_coef(way).wait_send()

        for n in range(2):
            for k in range(1, n_lat):
                near(n, k).wait_send()

        @pl.loop(1, n_lon)
        def _(k):
            for n in range(2):
                far(n, k).wait_recv()
                far(n, k).wait_send()

        for n in range(2):
            stays(n, 1).wait()


KINDS = (
    "up_main", "up_west", "up_east", "down_main", "down_west", "down_east", "west", "east", "up_coef", "down_coef",
)


def root(field, operands, first):
    fields, rows, cols = field.shape
    ext = rows + 2 * DEEP
    vmem = pl.BlockSpec(memory_space=pltpu.VMEM)
    f32 = lambda *shape: jax.ShapeDtypeStruct(shape, jnp.float32)
    scratch = [pltpu.VMEM((fields, ext, cols), jnp.float32)] * 7
    scratch += [pltpu.VMEM((fields // STRIP, rows, cols), jnp.float32)]
    scratch += [pltpu.VMEM((fields // STRIP, ext, cols), jnp.float32)] * 2
    scratch += [pltpu.SemaphoreType.DMA((len(KINDS), fields // GROUP))] * 2
    outs = [f32(fields, rows, cols)]
    in_specs, out_specs = [vmem] * (1 + len(operands)), [vmem]
    if first:
        anywhere = [pl.BlockSpec(memory_space=pl.ANY)] * 2
        in_specs[3:] = anywhere
        out_specs += [vmem] + anywhere
        n_lon, n_lat = lax.axis_size("lon"), lax.axis_size("lat")
        outs += [f32(3, ext, cols)] + [f32(n_lon, n_lat, 1, cols)] * 2
        scratch = (
            [pltpu.VMEM((3, ext, cols), jnp.float32)]
            + [pltpu.VMEM((n_lat, n_lon, 1, cols), jnp.float32)] * 2
            + [pltpu.SemaphoreType.DMA((2, 2, n_lat)), pltpu.SemaphoreType.DMA((2, 2, n_lon)), pltpu.SemaphoreType.DMA((2, 2))]
            + scratch
        )
    return pl.pallas_call(
        functools.partial(root_kernel, first),
        out_shape=outs,
        in_specs=in_specs,
        out_specs=out_specs,
        scratch_shapes=scratch,
        compiler_params=pltpu.CompilerParams(
            collective_id=0 if first else 1, has_side_effects=True, vmem_limit_bytes=60 * 2**20),
        name="root_first" if first else "root_second",
    )(field, *operands)


PAD = 8
NACC = 8


def obs_kernel(cnt_ref, tab_ref, base_ref, field_ref, w_ref, val_ref, prec_ref, inc_ref, out_ref,
               tab, stack, dense, cidx, ridx, ridx_s, sem, *accs):
    rows = tab_ref.shape[0]
    cells = 16 * 128
    lane = lax.broadcasted_iota(jnp.int32, (8, 128), 1)
    sub = lax.broadcasted_iota(jnp.int32, (8, 128), 0)
    zero = jnp.zeros((8, 128), jnp.float32)

    @pl.loop(0, rows // 80)
    def _(i):
        for k in range(10):
            at = pl.multiple_of(i * 80 + 8 * k, 8)
            value = tab_ref[pl.ds(at, 8), :]
            tab[pl.ds(at + PAD, 8), :] = value
            inc_ref[pl.ds(at, 8), :] = value

    tab[pl.ds(0, 8), :] = zero
    tab[pl.ds(rows + PAD, 8), :] = zero

    @pl.loop(0, 16)
    def _(b):
        at = pl.multiple_of(b * 8, 8)
        part = pl.ds(at, 8)
        index = field_ref[part, :] * cells + base_ref[part, :]
        arrays = [w_ref[k, part, :] for k in range(4)]
        arrays += [val_ref[part, :], prec_ref[part, :], index.astype(jnp.float32)]
        for k, array in enumerate(arrays):
            stack[pl.ds(at * 8 + k, 8, stride=8), :] = array

    def compact(o, start):
        group = stack[pl.ds(pl.multiple_of(o * 8, 8), 8), :]
        shift = lax.bitwise_and(start, 127)
        row = pl.multiple_of(lax.shift_right_logical(start, 7) * 8, 8)
        rolled = pltpu.roll(group, shift, 1)
        dense[pl.ds(row, 8), :] = jnp.where(lane >= shift, rolled, dense[pl.ds(row, 8), :])
        dense[pl.ds(row + 8, 8), :] = rolled
        return start + cnt_ref[0, o]

    total = lax.fori_loop(0, 128, compact, jnp.int32(0), unroll=8)
    chunks = lax.shift_right_logical(total + 127, 7)

    @pl.loop(0, 16)
    def _(b):
        at = pl.multiple_of(b * 8, 8)
        index = dense[pl.ds(at * 8 + 6, 8, stride=8), :].astype(jnp.int32)
        position = (at + sub) * 128 + lane
        index = jnp.where(position < total, index, 0)
        cidx[pl.ds(at, 8), :] = lax.bitwise_and(index, 127)
        ridx[pl.ds(at, 8), :] = lax.shift_right_logical(index, 7) + PAD

    copy = pltpu.make_async_copy(ridx, ridx_s, sem)
    copy.start()

    @pl.loop(0, (rows + 2 * PAD) // 8)
    def _(i):
        for acc in accs:
            acc[pl.ds(pl.multiple_of(i * 8, 8), 8), :] = zero

    copy.wait()

    even = lax.bitwise_and(lane, 1) == 0
    quad = lax.shift_right_logical(sub, 1)
    first = lax.bitwise_and(sub, 1) == 0
    keys = (
        lax.shift_right_logical(lane, 1) - 16 * quad,
        lax.shift_right_logical(lax.bitwise_and(lane - 1, 127), 1) - 16 * quad,
    )

    def spread(row):
        return jnp.broadcast_to(row, (8, 128))

    def gather(d):
        group = dense[pl.ds(pl.multiple_of(d * 8, 8), 8), :]
        cols = spread(cidx[pl.ds(d, 1), :])
        after = pltpu.roll(cols, 1, 1) + 1
        starts = (jnp.where(even, cols, after), jnp.where(even, after, cols))
        w0 = jnp.where(first, spread(group[0:1]), spread(group[2:3]))
        w1 = pltpu.roll(jnp.where(first, spread(group[1:2]), spread(group[3:4])), 1, 1)
        weights = (jnp.where(even, w0, w1), jnp.where(even, w1, w0))
        row_at = ridx_s.at[d]
        sums = []
        for par in range(2):
            found = zero
            for g in range(16):
                merged = None
                for q in range(4):
                    r = row_at[2 * (g + 16 * q) + par]
                    value = tab[pl.ds(r - 2 * q, 8), :]
                    merged = value if q == 0 else jnp.where(sub >= 2 * q, value, merged)
                picked = pick_lanes(merged, starts[par])
                found = jnp.where(keys[par] == g, picked, found)
            sums.append(spread(jnp.sum(found * weights[par], axis=0, keepdims=True)))
        here = jnp.where(even, sums[0], sums[1])
        there = jnp.where(even, sums[1], sums[0])
        modelled = here + pltpu.roll(there, 127, 1)
        misfit = spread(group[5:6]) * (modelled - spread(group[4:5]))
        misfit = jnp.where(d * 128 + lane < total, misfit, 0.0)
        moved = pltpu.roll(misfit, 1, 1)
        amounts = (
            weights[0] * jnp.where(even, misfit, moved),
            weights[1] * jnp.where(even, moved, misfit),
        )
        return amounts[0], amounts[1], lane - cols

    lane_par = lax.bitwise_and(lane, 1)
    ones = jnp.ones((128, 128), jnp.bfloat16)

    def scatter(d, amounts, shift):
        row_at = ridx_s.at[d]
        turn = shift.astype(jnp.float32)
        picked = [jnp.where(jnp.logical_and(keys[par] == g, lane_par == par), turn, 0.0) for par in range(2) for g in range(16)]
        picked = jnp.concatenate(picked, axis=0).astype(jnp.bfloat16)
        turns = jnp.dot(picked, ones, preferred_element_type=jnp.float32).astype(jnp.int32)
        for par in range(2):
            for g in range(16):
                masked = jnp.where(keys[par] == g, amounts[par], 0.0)
                at = 8 * (16 * par + g)
                source = lax.bitwise_and(lane + turns[at:at + 8], 127)
                placed = pick_lanes(masked, source)
                for q in range(4):
                    r = row_at[2 * (g + 16 * q) + par]
                    acc = accs[(g % (len(accs) // 4)) * 4 + q]
                    at = pl.ds(r - 2 * q, 8)
                    acc[at, :] = acc[at, :] + jnp.where(quad == q, placed, 0.0)

    def step(d, carry):
        new = gather(jnp.minimum(d, chunks - 1))
        scatter(jnp.maximum(d - 1, 0), carry[:2], carry[2])
        return new

    lax.fori_loop(0, chunks + 1, step, (zero, zero, lane))

    @pl.loop(0, rows // 8)
    def _(i):
        at = pl.multiple_of(i * 8, 8)
        parts = [acc[pl.ds(at + PAD, 8), :] for acc in accs]
        while len(parts) > 1:
            parts = [a + b for a, b in zip(parts[::2], parts[1::2])]
        out_ref[pl.ds(at, 8), :] = parts[0]


def observe(table, count, base, field, weight, value, precision):
    rows, cols = table.shape
    vmem = pl.BlockSpec(memory_space=pltpu.VMEM)
    smem = pl.BlockSpec(memory_space=pltpu.SMEM)
    return pl.pallas_call(
        obs_kernel,
        out_shape=[jax.ShapeDtypeStruct((rows, cols), jnp.float32)] * 2,
        in_specs=[smem] + [vmem] * 6,
        out_specs=[vmem] * 2,
        scratch_shapes=[
            pltpu.VMEM((rows + 2 * PAD, cols), jnp.float32),
            pltpu.VMEM((1024, 128), jnp.float32),
            pltpu.VMEM((129 * 8, 128), jnp.float32),
            pltpu.VMEM((128, 128), jnp.int32),
            pltpu.VMEM((128, 128), jnp.int32),
            pltpu.SMEM((128, 128), jnp.int32),
            pltpu.SemaphoreType.DMA,
        ] + [pltpu.VMEM((rows + 2 * PAD, cols), jnp.float32)] * NACC,
        compiler_params=pltpu.CompilerParams(vmem_limit_bytes=60 * 2**20),
        name="observe",
    )(count, table, base, field, weight, value, precision)


def per_device(
    control,
    lon_coef,
    lat_coef,
    obs_base,
    obs_field,
    obs_weight,
    obs_count,
    obs_value,
    obs_precision,
):
    fields, band_rows, block_cols = control.shape
    owners, slots = obs_base.shape[1:]
    by_device = (lax.axis_size("lon"), lax.axis_size("lat"), 1, slots)
    increment, coefs, value, precision = root(
        control,
        (lon_coef.T, lat_coef.T, obs_value.reshape(by_device), obs_precision.reshape(by_device)),
        True,
    )
    increment, forcing = observe(
        increment.reshape(fields * band_rows, block_cols),
        obs_count,
        obs_base[0],
        obs_field[0],
        obs_weight[:, 0],
        value.reshape(owners, slots),
        precision.reshape(owners, slots),
    )
    (adjoint,) = root(forcing.reshape(control.shape), (coefs,), False)
    return (increment.reshape(control.shape), control + adjoint)


def solution(mesh):
    in_specs = (
        P(None, "lat", "lon"),
        P(None, "lat"),
        P(None, "lat"),
        P(("lon", "lat"), None, None),
        P(("lon", "lat"), None, None),
        P(None, ("lon", "lat"), None, None),
        P(("lon", "lat"), None),
        P(("lon", "lat"), None, None),
        P(("lon", "lat"), None, None),
    )
    out_specs = (P(None, "lat", "lon"), P(None, "lat", "lon"))
    return jax.shard_map(
        per_device, mesh=mesh, in_specs=in_specs, out_specs=out_specs, check_vma=False
    )
```

time: 100 us -> 87.5 us (0.88)
  starting transfers between devices: 11.5 us -> 0 us
  local copies, waits for them, and re-layouts: 2.86 us -> 0.01 us
  Pallas kernels: 82 us -> 84.4 us
    all_to_all x1 -> x0, starting transfers between devices: 11.5 us -> none  [per_device(): lax.all_to_all(sent, ('lon', 'lat'), split_axis=0, concat_axis=0, tiled=T...]
    pallas_call x2, Pallas kernels: 47.3 us -> 50.1 us  [root(): pl.pallas_call(functools.partial(root_kernel, first), out_shape=outs, in_...]
    unnamed x18 -> x2, local copies, waits for them, and re-layouts: 2.76 us -> 0.01 us
    another operation x1 -> x0, other arithmetic: 1.65 us -> none  [per_device(): sent = jnp.stack([obs_value[0], obs_precision[0]], axis=1)]
    add x1, other arithmetic: 1 us -> 2.14 us  [per_device(): return (increment.reshape(control.shape), control + adjoint)]
  transfers between devices with their start and end apart: 1 -> 0, of which waited for: 0 -> 0; matrix products, arithmetic and copies ran while one was open for 0% -> 0% of each run, Pallas kernels for 25% -> 0%
where the time goes in v3:
time: 87.5 us; the launch traced here: 87.2 us
  Pallas kernels  84.4 us (96%)
  other arithmetic  2.14 us (2%)
    pallas_call x2, Pallas kernels, root(): pl.pallas_call(functools.partial(root_kernel, first), out_shape=outs, in_...  50.1 us
    pallas_call x1, Pallas kernels, observe(): pl.pallas_call(obs_kernel, out_shape=[jax.ShapeDtypeStruct((rows, cols),...  34.4 us
    add x1, other arithmetic, per_device(): return (increment.reshape(control.shape), control + adjoint)  2.14 us

profile of v3, /device:TPU:1, one launch (start us, length us, event | category | flops | bytes accessed | tf_op | source)
XLA Modules:
  0.0 87.2 jit_solution(16678470015749449)
XLA Ops:
  0.6 32.3 %root_first.1 = (f32[100,16,128]{2,1,0:T(8,128)}, f32[3,24,128]{2,1,0:T(8,128)}, f32[32,4,1,128]{3,2,1,0:T(1,128)}, f32[32,4,1,128]{3,2,1,0:T(1,128)}) custom-call(f32[100,16,128]{2,1,0:T(8,128)} %refs_0_.1, f32[16,100]{1,0:T(8,128)} %bitcast.21, f32[16,100]{1,0:T(8,128)} %bitcast.22, f32[32,4,1,128]{3,2,1,0:T(1,128)} %bitcast.19, f32[32,4,1,128]{3,2,1,0:T(1,128)} %bitcast.20), custom_call_target="tpu_custom_call" | custom-call | tf_op jit(solution)/shard_map/root_first/pallas_call | solution.py:334
  32.9 34.4 %observe.1 = (f32[1600,128]{1,0:T(8,128)}, f32[1600,128]{1,0:T(8,128)}) custom-call(s32[1,128]{1,0:T(1,128)} %cnt_ref.1, f32[1600,128]{1,0:T(8,128)} %bitcast.12, s32[128,128]{1,0:T(8,128)} %bitcast.15, s32[128,128]{1,0:T(8,128)} %bitcast.16, f32[4,128,128]{2,1,0:T(8,128)} %bitcast.14, f32[128,128]{1,0:T(8,128)} %bitcast.17, f32[128,128]{1,0:T(8,128)} %bitcast.18), custom_call_target="tpu_custom_call" | custom-call | tf_op jit(solution)/shard_map/observe/pallas_call | solution.py:495
  67.3 0.0 copy-start
  67.3 17.7 %root_second.1 = f32[100,16,128]{2,1,0:T(8,128)} custom-call(f32[100,16,128]{2,1,0:T(8,128)} %bitcast.13, f32[3,24,128]{2,1,0:T(8,128)} %get-tuple-element.13.refs_1_), custom_call_target="tpu_custom_call" | custom-call | tf_op jit(solution)/shard_map/root_second/pallas_call | solution.py:334
  85.1 0.0 copy-done
  85.1 2.1 %add.3 = f32[100,16,128]{2,1,0:T(8,128)} add(f32[100,16,128]{2,1,0:T(8,128)S(1)} %copy-done, f32[100,16,128]{2,1,0:T(8,128)} %root_second.1) | non-fusion elementwise | flops 204800 | bytes 2457600 | tf_op jit(solution)/shard_map/add | solution.py:543
Async XLA Ops:
  67.3 17.8 %copy-start = (f32[100,16,128]{2,1,0:T(8,128)S(1)}, f32[100,16,128]{2,1,0:T(8,128)}, u32[]{:S(2)}) copy-start(f32[100,16,128]{2,1,0:T(8,128)} %refs_0_.1) | copy-start | bytes 2457604

commit v4 on v3

--- a/solution.py
+++ b/solution.py
@@ -28,7 +28,9 @@
         (x_ref, zonal_ref, merid_ref, value_ref, precision_ref, out_ref, coef_out, value_out, precision_out, *scratch) = refs
         (coef, value_mid, precision_mid, near_sems, far_sems, own_sems, *scratch) = scratch
     else:
-        (x_ref, coef, out_ref, *scratch) = refs
+        (x_ref, coef, add_hbm, out_ref, add_ref, add_sem, *scratch) = refs
+        addend = pltpu.make_async_copy(add_hbm, add_ref, add_sem)
+        addend.start()
     (main, main2, side, side2, zonal, merid, centre, packed, left, right, send_sems, recv_sems) = scratch
     fields, rows, cols = x_ref.shape
     ext = rows + 2 * DEEP
@@ -227,6 +229,8 @@
         )
 
     def sweep(g, source, source_side, target, target_side, starts, shift):
+        last = target_side is None and not first
+
         def fields_from(base):
             for k in range(UNROLL):
                 f = base + k
@@ -238,6 +242,8 @@
                     c, z, n, s = centre[f, at, :], zonal[f, at, :], merid[f, at, :], merid[f, before, :]
                     out = c * m + z * (jnp.where(lane == 0, e_w, m_w) + jnp.where(lane == 127, e_e, m_e))
                     out = out + n * source[f, after, :] + s * source[f, before, :]
+                    if last:
+                        out = out + add_ref[f, pl.ds(start - shift, 8), :]
                     target[f, pl.ds(start - shift, 8), :] = out
                     if target_side is not None:
                         out = c * e + z * (jnp.where(lane == 0, m_w, e_w) + jnp.where(lane == 127, m_e, e_e))
@@ -250,6 +256,9 @@
             @pl.loop(0, GROUP // UNROLL)
             def _(u):
                 fields_from(g * GROUP + u * UNROLL)
+
+    if not first:
+        addend.wait()
 
     @pl.loop(0, groups)
     def _(g):
@@ -331,6 +340,9 @@
             + [pltpu.SemaphoreType.DMA((2, 2, n_lat)), pltpu.SemaphoreType.DMA((2, 2, n_lon)), pltpu.SemaphoreType.DMA((2, 2))]
             + scratch
         )
+    else:
+        in_specs[2] = pl.BlockSpec(memory_space=pl.ANY)
+        scratch = [pltpu.VMEM((fields, rows, cols), jnp.float32), pltpu.SemaphoreType.DMA] + scratch
     return pl.pallas_call(
         functools.partial(root_kernel, first),
         out_shape=outs,
@@ -347,24 +359,29 @@
 NACC = 8
 
 
-def obs_kernel(cnt_ref, tab_ref, base_ref, field_ref, w_ref, val_ref, prec_ref, inc_ref, out_ref,
-               tab, stack, dense, cidx, ridx, ridx_s, sem, *accs):
-    rows = tab_ref.shape[0]
+def obs_kernel(cnt_ref, tab_hbm, base_hbm, field_hbm, w_hbm, val_hbm, prec_hbm, inc_hbm, out_ref,
+               base_ref, field_ref, w_ref, val_ref, prec_ref, in_sems,
+               tab, stack, dense, plan, cidx, ridx, ridx_s, sem, windows, places, sources, *accs):
+    rows = tab_hbm.shape[0]
     cells = 16 * 128
     lane = lax.broadcasted_iota(jnp.int32, (8, 128), 1)
     sub = lax.broadcasted_iota(jnp.int32, (8, 128), 0)
     zero = jnp.zeros((8, 128), jnp.float32)
-
-    @pl.loop(0, rows // 80)
-    def _(i):
-        for k in range(10):
-            at = pl.multiple_of(i * 80 + 8 * k, 8)
-            value = tab_ref[pl.ds(at, 8), :]
-            tab[pl.ds(at + PAD, 8), :] = value
-            inc_ref[pl.ds(at, 8), :] = value
-
+    body = pl.ds(PAD, rows)
+    loads = [
+        pltpu.make_async_copy(source, target, in_sems.at[k])
+        for k, (source, target) in enumerate((
+            (base_hbm, base_ref), (field_hbm, field_ref), (w_hbm, w_ref), (val_hbm, val_ref), (prec_hbm, prec_ref),
+            (tab_hbm, tab.at[body]),
+        ))
+    ]
+    keep = pltpu.make_async_copy(tab.at[body], inc_hbm, in_sems.at[6])
+    for load in loads:
+        load.start()
     tab[pl.ds(0, 8), :] = zero
     tab[pl.ds(rows + PAD, 8), :] = zero
+    for load in loads[:-1]:
+        load.wait()
 
     @pl.loop(0, 16)
     def _(b):
@@ -376,38 +393,61 @@
         for k, array in enumerate(arrays):
             stack[pl.ds(at * 8 + k, 8, stride=8), :] = array
 
-    def compact(o, start):
+    def compact(o, carry):
+        start, kept = carry
         group = stack[pl.ds(pl.multiple_of(o * 8, 8), 8), :]
         shift = lax.bitwise_and(start, 127)
-        row = pl.multiple_of(lax.shift_right_logical(start, 7) * 8, 8)
+        row = lax.shift_right_logical(start, 7)
         rolled = pltpu.roll(group, shift, 1)
-        dense[pl.ds(row, 8), :] = jnp.where(lane >= shift, rolled, dense[pl.ds(row, 8), :])
-        dense[pl.ds(row + 8, 8), :] = rolled
-        return start + cnt_ref[0, o]
-
-    total = lax.fori_loop(0, 128, compact, jnp.int32(0), unroll=8)
+        merged = jnp.where(lane >= shift, rolled, kept)
+        at = pl.multiple_of(row * 8, 8)
+        dense[pl.ds(at, 8), :] = merged
+        dense[pl.ds(at + 8, 8), :] = rolled
+        after = start + cnt_ref[0, o]
+        moved = lax.shift_right_logical(after, 7) > row
+        return after, jnp.where(moved, rolled, merged)
+
+    total, _ = lax.fori_loop(0, 128, compact, (jnp.int32(0), zero), unroll=32)
     chunks = lax.shift_right_logical(total + 127, 7)
+
+    even = lax.bitwise_and(lane, 1) == 0
+
+    def paired(low, high, add=0):
+        after = pltpu.roll(high, 1, 1) + add
+        return jnp.where(even, low, after), jnp.where(even, after, low)
 
     @pl.loop(0, 16)
     def _(b):
         at = pl.multiple_of(b * 8, 8)
-        index = dense[pl.ds(at * 8 + 6, 8, stride=8), :].astype(jnp.int32)
-        position = (at + sub) * 128 + lane
-        index = jnp.where(position < total, index, 0)
-        cidx[pl.ds(at, 8), :] = lax.bitwise_and(index, 127)
-        ridx[pl.ds(at, 8), :] = lax.shift_right_logical(index, 7) + PAD
+        part = pl.ds(at, 8)
+        arrays = [dense[pl.ds(at * 8 + k, 8, stride=8), :] for k in range(7)]
+        live = (at + sub) * 128 + lane < total
+        index = jnp.where(live, arrays[6].astype(jnp.int32), 0)
+        ridx[part, :] = lax.shift_right_logical(index, 7) + PAD
+        cols = lax.bitwise_and(index, 127)
+        cidx[0, part, :], cidx[1, part, :] = paired(cols, cols, 1)
+        cidx[2, part, :] = lane - cols
+        for a in range(2):
+            first_row, second_row = paired(arrays[2 * a], arrays[2 * a + 1])
+            plan[a, part, :], plan[2 + a, part, :] = first_row, second_row
+        precision = jnp.where(live, arrays[5], 0.0)
+        value = jnp.where(live, arrays[4], 0.0)
+        plan[4, part, :], plan[5, part, :] = value, precision
+        plan[6, part, :], plan[7, part, :] = pltpu.roll(value, 1, 1), pltpu.roll(precision, 1, 1)
 
     copy = pltpu.make_async_copy(ridx, ridx_s, sem)
     copy.start()
 
-    @pl.loop(0, (rows + 2 * PAD) // 8)
+    @pl.loop(0, (rows + 2 * PAD) // 16)
     def _(i):
         for acc in accs:
-            acc[pl.ds(pl.multiple_of(i * 8, 8), 8), :] = zero
+            for k in range(2):
+                acc[pl.ds(pl.multiple_of(i * 16 + 8 * k, 8), 8), :] = zero
 
     copy.wait()
-
-    even = lax.bitwise_and(lane, 1) == 0
+    loads[-1].wait()
+    keep.start()
+
     quad = lax.shift_right_logical(sub, 1)
     first = lax.bitwise_and(sub, 1) == 0
     keys = (
@@ -418,93 +458,135 @@
     def spread(row):
         return jnp.broadcast_to(row, (8, 128))
 
-    def gather(d):
-        group = dense[pl.ds(pl.multiple_of(d * 8, 8), 8), :]
-        cols = spread(cidx[pl.ds(d, 1), :])
-        after = pltpu.roll(cols, 1, 1) + 1
-        starts = (jnp.where(even, cols, after), jnp.where(even, after, cols))
-        w0 = jnp.where(first, spread(group[0:1]), spread(group[2:3]))
-        w1 = pltpu.roll(jnp.where(first, spread(group[1:2]), spread(group[3:4])), 1, 1)
-        weights = (jnp.where(even, w0, w1), jnp.where(even, w1, w0))
+    def weights(d):
+        line = pl.ds(d, 1)
+        return [jnp.where(first, spread(plan[2 * par, line, :]), spread(plan[2 * par + 1, line, :])) for par in range(2)]
+
+    def load_windows(d):
         row_at = ridx_s.at[d]
-        sums = []
         for par in range(2):
-            found = zero
             for g in range(16):
                 merged = None
                 for q in range(4):
                     r = row_at[2 * (g + 16 * q) + par]
                     value = tab[pl.ds(r - 2 * q, 8), :]
                     merged = value if q == 0 else jnp.where(sub >= 2 * q, value, merged)
-                picked = pick_lanes(merged, starts[par])
-                found = jnp.where(keys[par] == g, picked, found)
-            sums.append(spread(jnp.sum(found * weights[par], axis=0, keepdims=True)))
+                windows[16 * par + g] = merged
+
+    def gather(d):
+        sums = []
+        for par in range(2):
+            start = spread(cidx[par, pl.ds(d, 1), :])
+            found = zero
+            for g in range(16):
+                found = jnp.where(keys[par] == g, pick_lanes(windows[16 * par + g], start), found)
+            sums.append(found)
+        return sums
+
+    def compare(d, found):
+        line = pl.ds(d, 1)
+        weight = weights(d)
+        sums = [spread(jnp.sum(found[par] * weight[par], axis=0, keepdims=True)) for par in range(2)]
         here = jnp.where(even, sums[0], sums[1])
         there = jnp.where(even, sums[1], sums[0])
-        modelled = here + pltpu.roll(there, 127, 1)
-        misfit = spread(group[5:6]) * (modelled - spread(group[4:5]))
-        misfit = jnp.where(d * 128 + lane < total, misfit, 0.0)
-        moved = pltpu.roll(misfit, 1, 1)
-        amounts = (
-            weights[0] * jnp.where(even, misfit, moved),
-            weights[1] * jnp.where(even, moved, misfit),
+        value, precision, value_w, precision_w = [spread(plan[k, line, :]) for k in range(4, 8)]
+        misfit = precision * (here + pltpu.roll(there, 127, 1) - value)
+        moved = precision_w * (pltpu.roll(here, 1, 1) + there - value_w)
+        return (
+            weight[0] * jnp.where(even, misfit, moved),
+            weight[1] * jnp.where(even, moved, misfit),
         )
-        return amounts[0], amounts[1], lane - cols
 
     lane_par = lax.bitwise_and(lane, 1)
     ones = jnp.ones((128, 128), jnp.bfloat16)
 
-    def scatter(d, amounts, shift):
-        row_at = ridx_s.at[d]
-        turn = shift.astype(jnp.float32)
-        picked = [jnp.where(jnp.logical_and(keys[par] == g, lane_par == par), turn, 0.0) for par in range(2) for g in range(16)]
+    def turn_lanes(d):
+        turn = spread(cidx[2, pl.ds(d, 1), :]).astype(jnp.float32)
+        picked = [
+            jnp.where(jnp.logical_and(keys[par] == g, lane_par == par), turn, 0.0)
+            for par in range(2) for g in range(16)
+        ]
         picked = jnp.concatenate(picked, axis=0).astype(jnp.bfloat16)
         turns = jnp.dot(picked, ones, preferred_element_type=jnp.float32).astype(jnp.int32)
+        for k in range(32):
+            sources[k] = lax.bitwise_and(lane + turns[8 * k:8 * k + 8], 127)
+
+    def place(amounts):
         for par in range(2):
             for g in range(16):
                 masked = jnp.where(keys[par] == g, amounts[par], 0.0)
-                at = 8 * (16 * par + g)
-                source = lax.bitwise_and(lane + turns[at:at + 8], 127)
-                placed = pick_lanes(masked, source)
+                places[16 * par + g] = pick_lanes(masked, sources[16 * par + g])
+
+    def add_rows(d):
+        row_at = ridx_s.at[d]
+        for par in range(2):
+            for g in range(16):
+                placed = places[16 * par + g]
                 for q in range(4):
                     r = row_at[2 * (g + 16 * q) + par]
                     acc = accs[(g % (len(accs) // 4)) * 4 + q]
                     at = pl.ds(r - 2 * q, 8)
                     acc[at, :] = acc[at, :] + jnp.where(quad == q, placed, 0.0)
 
+    for k in range(32):
+        windows[k] = zero
+        places[k] = zero
+        sources[k] = lane
+
     def step(d, carry):
-        new = gather(jnp.minimum(d, chunks - 1))
-        scatter(jnp.maximum(d - 1, 0), carry[:2], carry[2])
-        return new
-
-    lax.fori_loop(0, chunks + 1, step, (zero, zero, lane))
-
-    @pl.loop(0, rows // 8)
+        found_e, found_o, amounts_e, amounts_o = carry
+        last = chunks - 1
+        add_rows(jnp.clip(d - 4, 0, last))
+        place((amounts_e, amounts_o))
+        turn_lanes(jnp.clip(d - 2, 0, last))
+        amounts = compare(jnp.clip(d - 2, 0, last), (found_e, found_o))
+        found = gather(jnp.clip(d - 1, 0, last))
+        load_windows(jnp.minimum(d, last))
+        ready = d > 1
+        return (*found, jnp.where(ready, amounts[0], 0.0), jnp.where(ready, amounts[1], 0.0))
+
+    lax.fori_loop(0, chunks + 4, step, (zero,) * 4)
+
+    @pl.loop(0, rows // 80)
     def _(i):
-        at = pl.multiple_of(i * 8, 8)
-        parts = [acc[pl.ds(at + PAD, 8), :] for acc in accs]
-        while len(parts) > 1:
-            parts = [a + b for a, b in zip(parts[::2], parts[1::2])]
-        out_ref[pl.ds(at, 8), :] = parts[0]
+        for k in range(10):
+            at = pl.multiple_of(i * 80 + 8 * k, 8)
+            parts = [acc[pl.ds(at + PAD, 8), :] for acc in accs]
+            while len(parts) > 1:
+                parts = [a + b for a, b in zip(parts[::2], parts[1::2])]
+            out_ref[pl.ds(at, 8), :] = parts[0]
+
+    keep.wait()
 
 
 def observe(table, count, base, field, weight, value, precision):
     rows, cols = table.shape
     vmem = pl.BlockSpec(memory_space=pltpu.VMEM)
+    anywhere = pl.BlockSpec(memory_space=pl.ANY)
     smem = pl.BlockSpec(memory_space=pltpu.SMEM)
     return pl.pallas_call(
         obs_kernel,
         out_shape=[jax.ShapeDtypeStruct((rows, cols), jnp.float32)] * 2,
-        in_specs=[smem] + [vmem] * 6,
-        out_specs=[vmem] * 2,
+        in_specs=[smem] + [anywhere] * 6,
+        out_specs=[anywhere, vmem],
         scratch_shapes=[
+            pltpu.VMEM((128, 128), jnp.int32),
+            pltpu.VMEM((128, 128), jnp.int32),
+            pltpu.VMEM((4, 128, 128), jnp.float32),
+            pltpu.VMEM((128, 128), jnp.float32),
+            pltpu.VMEM((128, 128), jnp.float32),
+            pltpu.SemaphoreType.DMA((7,)),
             pltpu.VMEM((rows + 2 * PAD, cols), jnp.float32),
             pltpu.VMEM((1024, 128), jnp.float32),
             pltpu.VMEM((129 * 8, 128), jnp.float32),
-            pltpu.VMEM((128, 128), jnp.int32),
+            pltpu.VMEM((8, 128, 128), jnp.float32),
+            pltpu.VMEM((3, 128, 128), jnp.int32),
             pltpu.VMEM((128, 128), jnp.int32),
             pltpu.SMEM((128, 128), jnp.int32),
             pltpu.SemaphoreType.DMA,
+            pltpu.VMEM((32, 8, 128), jnp.float32),
+            pltpu.VMEM((32, 8, 128), jnp.float32),
+            pltpu.VMEM((32, 8, 128), jnp.int32),
         ] + [pltpu.VMEM((rows + 2 * PAD, cols), jnp.float32)] * NACC,
         compiler_params=pltpu.CompilerParams(vmem_limit_bytes=60 * 2**20),
         name="observe",
@@ -539,8 +621,8 @@
         value.reshape(owners, slots),
         precision.reshape(owners, slots),
     )
-    (adjoint,) = root(forcing.reshape(control.shape), (coefs,), False)
-    return (increment.reshape(control.shape), control + adjoint)
+    (gradient,) = root(forcing.reshape(control.shape), (coefs, control), False)
+    return (increment.reshape(control.shape), gradient)
 
 
 def solution(mesh):

time: 87.5 us -> 79.5 us (0.909)
  Pallas kernels: 84.4 us -> 76.5 us
  other arithmetic: 2.14 us -> 0 us
  local copies, waits for them, and re-layouts: 0.01 us -> 2.09 us
    pallas_call x1, Pallas kernels: 34.4 us -> 23.8 us  [observe(): pl.pallas_call(obs_kernel, out_shape=[jax.ShapeDtypeStruct((rows, cols),...]
    pallas_call x2, Pallas kernels: 50.1 us -> 52.7 us  [root(): pl.pallas_call(functools.partial(root_kernel, first), out_shape=outs, in_...]
    add x1 -> x0, other arithmetic: 2.14 us -> none  [per_device(): return (increment.reshape(control.shape), control + adjoint)]
    unnamed x2 -> x1, local copies, waits for them, and re-layouts: 0.01 us -> 2.09 us
where the time goes in v4:
time: 79.5 us; the launch traced here: 79.2 us
  Pallas kernels  76.5 us (96%)
  local copies, waits for them, and re-layouts  2.09 us (3%)
    pallas_call x2, Pallas kernels, root(): pl.pallas_call(functools.partial(root_kernel, first), out_shape=outs, in_...  52.7 us
    pallas_call x1, Pallas kernels, observe(): pl.pallas_call(obs_kernel, out_shape=[jax.ShapeDtypeStruct((rows, cols),...  23.8 us
    unnamed x1, local copies, waits for them, and re-layouts  2.09 us

profile of v4, /device:TPU:1, one launch (start us, length us, event | category | flops | bytes accessed | tf_op | source)
XLA Modules:
  0.0 79.2 jit_solution(9829188441031617833)
XLA Ops:
  0.6 32.3 %root_first.1 = (f32[100,16,128]{2,1,0:T(8,128)}, f32[3,24,128]{2,1,0:T(8,128)}, f32[32,4,1,128]{3,2,1,0:T(1,128)}, f32[32,4,1,128]{3,2,1,0:T(1,128)}) custom-call(f32[100,16,128]{2,1,0:T(8,128)} %refs_2_.1, f32[16,100]{1,0:T(8,128)} %bitcast.21, f32[16,100]{1,0:T(8,128)} %bitcast.22, f32[32,4,1,128]{3,2,1,0:T(1,128)} %bitcast.19, f32[32,4,1,128]{3,2,1,0:T(1,128)} %bitcast.20), custom_call_target="tpu_custom_call" | custom-call | tf_op jit(solution)/shard_map/root_first/pallas_call | solution.py:346
  32.9 23.8 %observe.1 = (f32[1600,128]{1,0:T(8,128)}, f32[1600,128]{1,0:T(8,128)}) custom-call(s32[1,128]{1,0:T(1,128)} %cnt_ref.1, f32[1600,128]{1,0:T(8,128)} %bitcast.12, s32[128,128]{1,0:T(8,128)} %bitcast.15, s32[128,128]{1,0:T(8,128)} %bitcast.16, f32[4,128,128]{2,1,0:T(8,128)} %bitcast.14, f32[128,128]{1,0:T(8,128)} %bitcast.17, f32[128,128]{1,0:T(8,128)} %bitcast.18), custom_call_target="tpu_custom_call" | custom-call | tf_op jit(solution)/shard_map/observe/pallas_call | solution.py:567
  56.7 20.4 %root_second.1 = f32[100,16,128]{2,1,0:T(8,128)} custom-call(f32[100,16,128]{2,1,0:T(8,128)} %bitcast.13, f32[3,24,128]{2,1,0:T(8,128)} %get-tuple-element.13.refs_1_, f32[100,16,128]{2,1,0:T(8,128)} %refs_2_.1), custom_call_target="tpu_custom_call" | custom-call | tf_op jit(solution)/shard_map/root_second/pallas_call | solution.py:346
  77.1 2.1 %copy.12 = f32[100,16,128]{2,1,0:T(8,128)} copy(f32[100,16,128]{2,1,0:T(8,128)} %root_second.1) | data formatting | bytes 1638400

commit v5 on v4

--- a/solution.py
+++ b/solution.py
@@ -9,21 +9,13 @@
 
 MESH = pl.DeviceIdType.MESH
 DEEP = 4
-STRIP = 10
-GROUP = 20
-UNROLL = 20
-
-
-LANES = lax.GatherDimensionNumbers(
-    offset_dims=(), collapsed_slice_dims=(1,), start_index_map=(1,),
-    operand_batching_dims=(0,), start_indices_batching_dims=(0,))
-
-
-def pick_lanes(value, index):
-    return lax.gather(value, index[:, :, None], LANES, slice_sizes=(1, 1), mode="promise_in_bounds")
-
-
-def root_kernel(first, *refs):
+EDGE = 8
+KINDS = (
+    "up_main", "up_west", "up_east", "down_main", "down_west", "down_east", "west", "east", "up_coef", "down_coef",
+)
+
+
+def root_kernel(first, rows, *refs):
     if first:
         (x_ref, zonal_ref, merid_ref, value_ref, precision_ref, out_ref, coef_out, value_out, precision_out, *scratch) = refs
         (coef, value_mid, precision_mid, near_sems, far_sems, own_sems, *scratch) = scratch
@@ -31,18 +23,14 @@
         (x_ref, coef, add_hbm, out_ref, add_ref, add_sem, *scratch) = refs
         addend = pltpu.make_async_copy(add_hbm, add_ref, add_sem)
         addend.start()
-    (main, main2, side, side2, zonal, merid, centre, packed, left, right, send_sems, recv_sems) = scratch
-    fields, rows, cols = x_ref.shape
+    (main, main2, send_sems, recv_sems) = scratch
+    cols = x_ref.shape[1]
+    fields = x_ref.shape[0] // rows
     ext = rows + 2 * DEEP
-    groups, strips = fields // GROUP, GROUP // STRIP
     n_lon, n_lat = lax.axis_size("lon"), lax.axis_size("lat")
     lon, lat = lax.axis_index("lon"), lax.axis_index("lat")
     west, east = lax.rem(lon + n_lon - 1, n_lon), lax.rem(lon + 1, n_lon)
     has_up, has_down = lat > 0, lat < n_lat - 1
-    lane = lax.broadcasted_iota(jnp.int32, (8, cols), 1)
-    low, high, own = pl.ds(0, DEEP), pl.ds(rows + DEEP, DEEP), pl.ds(DEEP, rows)
-    top, bottom = pl.ds(0, DEEP), pl.ds(rows - DEEP, DEEP)
-
     barrier = pltpu.get_barrier_semaphore()
 
     def greet(there_lon, there_lat):
@@ -75,76 +63,91 @@
             device_id={"lon": there_lon, "lat": there_lat}, device_id_type=MESH,
         )
 
-    def exchange(kind, g):
-        fs, ss = pl.ds(g * GROUP, GROUP), pl.ds(g * strips, strips)
-        source, target, there_lon, there_lat = {
-            "up_main": (x_ref.at[fs, top], main.at[fs, high], lon, lat - 1),
-            "up_west": (packed.at[ss, top], right.at[ss, high], west, lat - 1),
-            "up_east": (packed.at[ss, top], left.at[ss, high], east, lat - 1),
-            "down_main": (x_ref.at[fs, bottom], main.at[fs, low], lon, lat + 1),
-            "down_west": (packed.at[ss, bottom], right.at[ss, low], west, lat + 1),
-            "down_east": (packed.at[ss, bottom], left.at[ss, low], east, lat + 1),
-            "west": (packed.at[ss], right.at[ss, own], west, lat),
-            "east": (packed.at[ss], left.at[ss, own], east, lat),
+    above, below = pl.ds(0, DEEP), pl.ds(rows + DEEP, DEEP)
+    top, bottom, band = pl.ds(DEEP, DEEP), pl.ds(rows, DEEP), pl.ds(DEEP, rows)
+    block = pl.ds(EDGE, cols)
+    west_edge, east_edge = pl.ds(EDGE, DEEP), pl.ds(EDGE + cols - DEEP, DEEP)
+    west_halo, east_halo = pl.ds(EDGE - DEEP, DEEP), pl.ds(EDGE + cols, DEEP)
+
+    def exchange(kind):
+        source_rows, target_rows, source_cols, target_cols, there_lon, there_lat = {
+            "up_main": (top, below, block, block, lon, lat - 1),
+            "up_west": (top, below, west_edge, east_halo, west, lat - 1),
+            "up_east": (top, below, east_edge, west_halo, east, lat - 1),
+            "down_main": (bottom, above, block, block, lon, lat + 1),
+            "down_west": (bottom, above, west_edge, east_halo, west, lat + 1),
+            "down_east": (bottom, above, east_edge, west_halo, east, lat + 1),
+            "west": (band, band, west_edge, east_halo, west, lat),
+            "east": (band, band, east_edge, west_halo, east, lat),
         }[kind]
         slot = KINDS.index(kind)
-        return remote(source, target, send_sems.at[slot, g], recv_sems.at[slot, g], there_lon, there_lat)
+        return remote(
+            main.at[source_rows, source_cols], main.at[target_rows, target_cols],
+            send_sems.at[slot], recv_sems.at[slot], there_lon, there_lat,
+        )
 
     def exchange_coef(kind):
         pair, slot = pl.ds(0, 2), KINDS.index(kind)
-        source, target, there_lat = {
-            "up_coef": (coef.at[pair, pl.ds(DEEP, DEEP)], coef.at[pair, high], lat - 1),
-            "down_coef": (coef.at[pair, pl.ds(rows, DEEP)], coef.at[pair, low], lat + 1),
-        }[kind]
-        return remote(source, target, send_sems.at[slot, 0], recv_sems.at[slot, 0], lon, there_lat)
+        source, target, there_lat = (top, below, lat - 1) if kind == "up_coef" else (bottom, above, lat + 1)
+        return remote(coef.at[pair, source], coef.at[pair, target], send_sems.at[slot], recv_sems.at[slot], lon, there_lat)
+
+    whole = fields // 8
+    rest = fields - 8 * whole
+
+    def turn_in(j):
+        parts = [x_ref[pl.ds(j + rows * 8 * k, 8, stride=rows), :] for k in range(whole)]
+        if rest:
+            tail = x_ref[pl.ds(j + rows * 8 * whole, rest, stride=rows), :]
+            parts.append(jnp.concatenate([tail, jnp.zeros((8 - rest, cols), jnp.float32)], axis=0))
+        parts.append(jnp.zeros((cols - 8 * len(parts), cols), jnp.float32))
+        main[j + DEEP, block] = jnp.concatenate(parts, axis=0).T
+
+    def turn_out(j, plane):
+        turned = plane.T
+        for k in range(whole + (rest > 0)):
+            size = 8 if k < whole else rest
+            at = pl.ds(j + rows * 8 * k, size, stride=rows)
+            value = turned[8 * k:8 * k + size]
+            if not first:
+                value = value + add_ref[at, :]
+            out_ref[at, :] = value
 
     if first:
         row = lax.broadcasted_iota(jnp.int32, (rows, fields), 0)
         closed = jnp.logical_and(row == rows - 1, lat == n_lat - 1)
         blank = jnp.zeros((rows, cols), jnp.float32)
         for k, rates in enumerate((zonal_ref[...], jnp.where(closed, 0.0, merid_ref[...]))):
-            coef[k, own] = blank
-            coef[k, own, pl.ds(0, fields)] = rates
+            coef[k, band] = blank
+            coef[k, band, pl.ds(0, fields)] = rates
+
+    for start in (0, rows - DEEP):
+        @pl.loop(start, start + DEEP)
+        def _(j):
+            turn_in(j)
 
     pl.semaphore_wait(barrier, greetings)
 
-    for present, way, at in ((has_up, "up", low), (has_down, "down", high)):
+    for present, way, at in ((has_up, "up", above), (has_down, "down", below)):
         @pl.when(present)
         def _():
             if first:
                 exchange_coef(way + "_coef").start()
-
-            @pl.loop(0, groups)
-            def _(g):
-                exchange(way + "_main", g).start()
+            exchange(way + "_main").start()
+            exchange(way + "_west").start()
+            exchange(way + "_east").start()
 
         @pl.when(jnp.logical_not(present))
         def _():
-            main[:, at] = jnp.zeros((fields, DEEP, cols), jnp.float32)
-            for halo in (left, right):
-                halo[:, at] = jnp.zeros((fields // STRIP, DEEP, cols), jnp.float32)
+            main[at] = jnp.zeros((DEEP,) + main.shape[1:], jnp.float32)
             if first:
                 coef[pl.ds(0, 2), at] = jnp.zeros((2, DEEP, cols), jnp.float32)
 
-    key = lax.shift_right_logical(lax.bitwise_and(lane + 4, 127), 3)
-
-    @pl.loop(0, groups)
-    def _(g):
-        for s in range(strips):
-            for part in range(rows // 8):
-                at = pl.ds(8 * part, 8)
-                strip = x_ref[g * GROUP + s * STRIP, at, :]
-                for k in range(1, STRIP):
-                    value = x_ref[g * GROUP + s * STRIP + k, at, :]
-                    strip = jnp.where(key == k, pltpu.roll(value, 8 * k, 1), strip)
-                packed[g * strips + s, at, :] = strip
-        exchange("west", g).start()
-        exchange("east", g).start()
-        for present, way in ((has_up, "up"), (has_down, "down")):
-            @pl.when(present)
-            def _():
-                exchange(way + "_west", g).start()
-                exchange(way + "_east", g).start()
+    @pl.loop(DEEP, rows - DEEP)
+    def _(j):
+        turn_in(j)
+
+    for kind in ("west", "east"):
+        exchange(kind).start()
 
     if first:
         pairs = ((value_ref, value_mid, value_out), (precision_ref, precision_mid, precision_out))
@@ -170,42 +173,6 @@
                 near(n, k).start()
             stays(n, 0).start()
 
-    @pl.loop(0, fields // 10)
-    def _(g):
-        for k in range(10):
-            for part in range(rows // 8):
-                main[g * 10 + k, pl.ds(DEEP + 8 * part, 8), :] = x_ref[g * 10 + k, pl.ds(8 * part, 8), :]
-
-    def spread_tables(tables, targets):
-        @pl.loop(0, fields // 10)
-        def _(g):
-            for k in range(10):
-                f = g * 10 + k
-                which = jnp.full((8, cols), f, jnp.int32)
-                for table, (target, places) in zip(tables, targets):
-                    value = pick_lanes(table, which)
-                    for start, size, at in places:
-                        target[f, pl.ds(at, size), :] = value[start:start + size]
-
-    whole = lambda at: ((0, 8, at),)
-    if first:
-        spread_tables(
-            [coef[k, pl.ds(at, 8), :] for k in range(2) for at in (DEEP, DEEP + 8)],
-            [(target, whole(at)) for target in (zonal, merid) for at in (DEEP, DEEP + 8)],
-        )
-        for n in range(2):
-            for k in range(1, n_lat):
-                near(n, k).wait_recv()
-            stays(n, 0).wait()
-
-        @pl.loop(1, n_lon)
-        def _(k):
-            for n in range(2):
-                far(n, k).start()
-
-        for n in range(2):
-            stays(n, 1).start()
-
         for present, way in ((has_up, "down_coef"), (has_down, "up_coef")):
             @pl.when(present)
             def _():
@@ -216,81 +183,67 @@
             at = pl.ds(start, 8)
             coef[2, at] = 1.0 - 2.0 * coef[0, at] - coef[1, at] - coef[1, pl.ds(start - 1, 8)]
         coef_out[...] = coef[...]
-        rims = [jnp.concatenate([coef[k, low], coef[k, high]], axis=0) for k in range(2)]
-        parts = ((0, DEEP, 0), (DEEP, DEEP, rows + DEEP))
-        spread_tables(
-            rims + [coef[2, pl.ds(8 * part, 8), :] for part in range(ext // 8)],
-            [(zonal, parts), (merid, parts)] + [(centre, whole(8 * part)) for part in range(ext // 8)],
-        )
-    else:
-        spread_tables(
-            [coef[k, pl.ds(8 * part, 8), :] for k in range(3) for part in range(ext // 8)],
-            [(target, whole(8 * part)) for target in (zonal, merid, centre) for part in range(ext // 8)],
-        )
-
-    def sweep(g, source, source_side, target, target_side, starts, shift):
-        last = target_side is None and not first
-
-        def fields_from(base):
-            for k in range(UNROLL):
-                f = base + k
-                for start in starts:
-                    at, before, after = pl.ds(start, 8), pl.ds(start - 1, 8), pl.ds(start + 1, 8)
-                    m, e = source[f, at, :], source_side[f, at, :]
-                    m_w, e_w = pltpu.roll(m, 1, 1), pltpu.roll(e, 1, 1)
-                    m_e, e_e = pltpu.roll(m, 127, 1), pltpu.roll(e, 127, 1)
-                    c, z, n, s = centre[f, at, :], zonal[f, at, :], merid[f, at, :], merid[f, before, :]
-                    out = c * m + z * (jnp.where(lane == 0, e_w, m_w) + jnp.where(lane == 127, e_e, m_e))
-                    out = out + n * source[f, after, :] + s * source[f, before, :]
-                    if last:
-                        out = out + add_ref[f, pl.ds(start - shift, 8), :]
-                    target[f, pl.ds(start - shift, 8), :] = out
-                    if target_side is not None:
-                        out = c * e + z * (jnp.where(lane == 0, m_w, e_w) + jnp.where(lane == 127, m_e, e_e))
-                        out = out + n * source_side[f, after, :] + s * source_side[f, before, :]
-                        target_side[f, at, :] = out
-
-        if UNROLL == GROUP:
-            fields_from(g * GROUP)
-        else:
-            @pl.loop(0, GROUP // UNROLL)
-            def _(u):
-                fields_from(g * GROUP + u * UNROLL)
-
+
+    for kind in ("west", "east"):
+        exchange(kind).wait_recv()
+    for present, way in ((has_up, "down"), (has_down, "up")):
+        @pl.when(present)
+        def _():
+            for kind in ("_main", "_west", "_east"):
+                exchange(way + kind).wait_recv()
+
+    def swept(source, p, starts):
+        rate = lambda k, q: jnp.broadcast_to(coef[k, pl.ds(q, 1), :], (8, cols))
+        c, z, n, s = rate(2, p), rate(0, p), rate(1, p), rate(1, p - 1)
+        out = []
+        for start in starts:
+            at = pl.ds(start, 8)
+            value = c * source[p, at, :] + z * (source[p, pl.ds(start - 1, 8), :] + source[p, pl.ds(start + 1, 8), :])
+            out.append(value + n * source[p + 1, at, :] + s * source[p - 1, at, :])
+        return out
+
+    def sweep(source, target, t):
+        starts = range(EDGE - DEEP + t, EDGE + cols + DEEP - t, 8)
+
+        @pl.loop(t, ext - t)
+        def _(p):
+            for start, value in zip(starts, swept(source, p, starts)):
+                target[p, pl.ds(start, 8), :] = value
+
+    sweep(main, main2, 1)
+
+    if first:
+        for n in range(2):
+            for k in range(1, n_lat):
+                near(n, k).wait_recv()
+            stays(n, 0).wait()
+
+        @pl.loop(1, n_lon)
+        def _(k):
+            for n in range(2):
+                far(n, k).start()
+
+        for n in range(2):
+            stays(n, 1).start()
+
+    for kind in ("west", "east"):
+        exchange(kind).wait_send()
+    for present, way in ((has_up, "up"), (has_down, "down")):
+        @pl.when(present)
+        def _():
+            for kind in ("_main", "_west", "_east"):
+                exchange(way + kind).wait_send()
+
+    sweep(main2, main, 2)
+    sweep(main, main2, 3)
     if not first:
         addend.wait()
 
-    @pl.loop(0, groups)
-    def _(g):
-        for kind in ("west", "east"):
-            exchange(kind, g).wait_recv()
-        for present, way in ((has_up, "down"), (has_down, "up")):
-            @pl.when(present)
-            def _():
-                for kind in ("_main", "_west", "_east"):
-                    exchange(way + kind, g).wait_recv()
-
-        for s in range(strips):
-            for part in range(ext // 8):
-                at = pl.ds(8 * part, 8)
-                both = jnp.where(lax.bitwise_and(lane, 7) >= 4, left[g * strips + s, at, :], right[g * strips + s, at, :])
-                for k in range(STRIP):
-                    side[g * GROUP + s * STRIP + k, at, :] = pltpu.roll(both, (-8 * k) % 128, 1) if k else both
-
-        sweep(g, main, side, main2, side2, (1, 9, 15), 0)
-        sweep(g, main2, side2, main, side, (2, 10, 14), 0)
-        sweep(g, main, side, main2, side2, (3, 11, 13), 0)
-        sweep(g, main2, side2, out_ref, None, (4, 12), 4)
-
-    @pl.loop(0, groups)
-    def _(g):
-        for kind in ("west", "east"):
-            exchange(kind, g).wait_send()
-        for present, way in ((has_up, "up"), (has_down, "down")):
-            @pl.when(present)
-            def _():
-                for kind in ("_main", "_west", "_east"):
-                    exchange(way + kind, g).wait_send()
+    @pl.loop(0, rows // 2)
+    def _(i):
+        for k in range(2):
+            j = i * 2 + k
+            turn_out(j, jnp.concatenate(swept(main2, j + DEEP, range(EDGE, EDGE + cols, 8)), axis=0))
 
     if first:
         for present, way in ((has_up, "up_coef"), (has_down, "down_coef")):
@@ -312,21 +265,14 @@
             stays(n, 1).wait()
 
 
-KINDS = (
-    "up_main", "up_west", "up_east", "down_main", "down_west", "down_east", "west", "east", "up_coef", "down_coef",
-)
-
-
-def root(field, operands, first):
-    fields, rows, cols = field.shape
+def root(field, operands, rows, first):
+    cols = field.shape[1]
     ext = rows + 2 * DEEP
     vmem = pl.BlockSpec(memory_space=pltpu.VMEM)
     f32 = lambda *shape: jax.ShapeDtypeStruct(shape, jnp.float32)
-    scratch = [pltpu.VMEM((fields, ext, cols), jnp.float32)] * 7
-    scratch += [pltpu.VMEM((fields // STRIP, rows, cols), jnp.float32)]
-    scratch += [pltpu.VMEM((fields // STRIP, ext, cols), jnp.float32)] * 2
-    scratch += [pltpu.SemaphoreType.DMA((len(KINDS), fields // GROUP))] * 2
-    outs = [f32(fields, rows, cols)]
+    scratch = [pltpu.VMEM((ext, cols + 2 * EDGE, cols), jnp.float32)] * 2
+    scratch += [pltpu.SemaphoreType.DMA((len(KINDS),))] * 2
+    outs = [f32(*field.shape)]
     in_specs, out_specs = [vmem] * (1 + len(operands)), [vmem]
     if first:
         anywhere = [pl.BlockSpec(memory_space=pl.ANY)] * 2
@@ -342,9 +288,9 @@
         )
     else:
         in_specs[2] = pl.BlockSpec(memory_space=pl.ANY)
-        scratch = [pltpu.VMEM((fields, rows, cols), jnp.float32), pltpu.SemaphoreType.DMA] + scratch
+        scratch = [pltpu.VMEM(field.shape, jnp.float32), pltpu.SemaphoreType.DMA] + scratch
     return pl.pallas_call(
-        functools.partial(root_kernel, first),
+        functools.partial(root_kernel, first, rows),
         out_shape=outs,
         in_specs=in_specs,
         out_specs=out_specs,
@@ -357,6 +303,13 @@
 
 PAD = 8
 NACC = 8
+LANES = lax.GatherDimensionNumbers(
+    offset_dims=(), collapsed_slice_dims=(1,), start_index_map=(1,),
+    operand_batching_dims=(0,), start_indices_batching_dims=(0,))
+
+
+def pick_lanes(value, index):
+    return lax.gather(value, index[:, :, None], LANES, slice_sizes=(1, 1), mode="promise_in_bounds")
 
 
 def obs_kernel(cnt_ref, tab_hbm, base_hbm, field_hbm, w_hbm, val_hbm, prec_hbm, inc_hbm, out_ref,
@@ -607,13 +560,15 @@
     fields, band_rows, block_cols = control.shape
     owners, slots = obs_base.shape[1:]
     by_device = (lax.axis_size("lon"), lax.axis_size("lat"), 1, slots)
+    lines = control.reshape(fields * band_rows, block_cols)
     increment, coefs, value, precision = root(
-        control,
+        lines,
         (lon_coef.T, lat_coef.T, obs_value.reshape(by_device), obs_precision.reshape(by_device)),
+        band_rows,
         True,
     )
     increment, forcing = observe(
-        increment.reshape(fields * band_rows, block_cols),
+        increment,
         obs_count,
         obs_base[0],
         obs_field[0],
@@ -621,8 +576,8 @@
         value.reshape(owners, slots),
         precision.reshape(owners, slots),
     )
-    (gradient,) = root(forcing.reshape(control.shape), (coefs, control), False)
-    return (increment.reshape(control.shape), gradient)
+    (gradient,) = root(forcing, (coefs, lines), band_rows, False)
+    return (increment.reshape(control.shape), gradient.reshape(control.shape))
 
 
 def solution(mesh):

time: 79.5 us -> 70.1 us (0.88)
  Pallas kernels: 76.5 us -> 67.2 us
    pallas_call x2, Pallas kernels: 52.7 us -> 43.9 us  [root(): pl.pallas_call(functools.partial(root_kernel, first, rows), out_shape=out...]
where the time goes in v5:
time: 70.1 us; the launch traced here: 69.9 us
  Pallas kernels  67.2 us (96%)
  local copies, waits for them, and re-layouts  2.09 us (3%)
    pallas_call x2, Pallas kernels, root(): pl.pallas_call(functools.partial(root_kernel, first, rows), out_shape=out...  43.9 us
    pallas_call x1, Pallas kernels, observe(): pl.pallas_call(obs_kernel, out_shape=[jax.ShapeDtypeStruct((rows, cols),...  23.3 us
    unnamed x1, local copies, waits for them, and re-layouts  2.09 us

profile of v5, /device:TPU:1, one launch (start us, length us, event | category | flops | bytes accessed | tf_op | source)
XLA Modules:
  0.0 69.9 jit_solution(11147707817880083661)
XLA Ops:
  0.6 26.0 %root_first.1 = (f32[1600,128]{1,0:T(8,128)}, f32[3,24,128]{2,1,0:T(8,128)}, f32[32,4,1,128]{3,2,1,0:T(1,128)}, f32[32,4,1,128]{3,2,1,0:T(1,128)}) custom-call(f32[1600,128]{1,0:T(8,128)} %bitcast.13, f32[16,100]{1,0:T(8,128)} %bitcast.22, f32[16,100]{1,0:T(8,128)} %bitcast.23, f32[32,4,1,128]{3,2,1,0:T(1,128)} %bitcast.20, f32[32,4,1,128]{3,2,1,0:T(1,128)} %bitcast.21), custom_call_target="tpu_custom_call" | custom-call | tf_op jit(solution)/shard_map/root_first/pallas_call | solution.py:292
  26.6 23.3 %observe.1 = (f32[1600,128]{1,0:T(8,128)}, f32[1600,128]{1,0:T(8,128)}) custom-call(s32[1,128]{1,0:T(1,128)} %cnt_ref.1, f32[1600,128]{1,0:T(8,128)} %get-tuple-element.8.tab_hbm, s32[128,128]{1,0:T(8,128)} %bitcast.16, s32[128,128]{1,0:T(8,128)} %bitcast.17, f32[4,128,128]{2,1,0:T(8,128)} %bitcast.15, f32[128,128]{1,0:T(8,128)} %bitcast.18, f32[128,128]{1,0:T(8,128)} %bitcast.19), custom_call_target="tpu_custom_call" | custom-call | tf_op jit(solution)/shard_map/observe/pallas_call | solution.py:520
  49.9 17.9 %root_second.1 = f32[1600,128]{1,0:T(8,128)} custom-call(f32[1600,128]{1,0:T(8,128)} %get-tuple-element.12.refs_0_, f32[3,24,128]{2,1,0:T(8,128)} %get-tuple-element.13.refs_1_, f32[1600,128]{1,0:T(8,128)} %bitcast.14), custom_call_target="tpu_custom_call" | custom-call | tf_op jit(solution)/shard_map/root_second/pallas_call | solution.py:292
  67.8 2.1 %copy.12 = f32[100,16,128]{2,1,0:T(8,128)} copy(f32[100,16,128]{2,1,0:T(8,128)} %bitcast.12) | data formatting | bytes 1638400

commit v6 on v5

--- a/solution.py
+++ b/solution.py
@@ -17,8 +17,14 @@
 
 def root_kernel(first, rows, *refs):
     if first:
-        (x_ref, zonal_ref, merid_ref, value_ref, precision_ref, out_ref, coef_out, value_out, precision_out, *scratch) = refs
-        (coef, value_mid, precision_mid, near_sems, far_sems, own_sems, *scratch) = scratch
+        (x_hbm, zonal_hbm, merid_hbm, value_ref, precision_ref, out_ref, coef_out, held_out, *scratch) = refs
+        (x_ref, zonal_ref, merid_ref, in_sems, coef, held_mid, near_sems, far_sems, own_sems, *scratch) = scratch
+        loads = [
+            pltpu.make_async_copy(source, target, in_sems.at[k])
+            for k, (source, target) in enumerate(((zonal_hbm, zonal_ref), (merid_hbm, merid_ref), (x_hbm, x_ref)))
+        ]
+        for load in loads:
+            load.start()
     else:
         (x_ref, coef, add_hbm, out_ref, add_ref, add_sem, *scratch) = refs
         addend = pltpu.make_async_copy(add_hbm, add_ref, add_sem)
@@ -113,6 +119,8 @@
             out_ref[at, :] = value
 
     if first:
+        for load in loads:
+            load.wait()
         row = lax.broadcasted_iota(jnp.int32, (rows, fields), 0)
         closed = jnp.logical_and(row == rows - 1, lat == n_lat - 1)
         blank = jnp.zeros((rows, cols), jnp.float32)
@@ -125,7 +133,33 @@
         def _(j):
             turn_in(j)
 
+    if first:
+        sent = (value_ref, precision_ref)
+
+        def near(n, k):
+            there = lax.rem(lat + k, n_lat)
+            return remote(
+                sent[n].at[:, there], held_mid.at[lat, :, pl.ds(n, 1)],
+                near_sems.at[0, n, k], near_sems.at[1, n, k], lon, there,
+            )
+
+        def near_own(n):
+            return pltpu.make_async_copy(sent[n].at[:, lat], held_mid.at[lat, :, pl.ds(n, 1)], own_sems.at[n])
+
+        def far(k):
+            there = lax.rem(lon + k, n_lon)
+            return remote(held_mid.at[:, there], held_out.at[lon], far_sems.at[0, k], far_sems.at[1, k], there, lat)
+
+        def far_own():
+            return pltpu.make_async_copy(held_mid.at[:, lon], held_out.at[lon], own_sems.at[2])
+
     pl.semaphore_wait(barrier, greetings)
+
+    if first:
+        for n in range(2):
+            for k in range(1, n_lat):
+                near(n, k).start()
+            near_own(n).start()
 
     for present, way, at in ((has_up, "up", above), (has_down, "down", below)):
         @pl.when(present)
@@ -150,28 +184,16 @@
         exchange(kind).start()
 
     if first:
-        pairs = ((value_ref, value_mid, value_out), (precision_ref, precision_mid, precision_out))
-
-        def near(n, k):
-            source, target, _ = pairs[n]
-            there = lax.rem(lat + k, n_lat)
-            return remote(source.at[:, there], target.at[lat], near_sems.at[0, n, k], near_sems.at[1, n, k], lon, there)
-
-        def far(n, k):
-            _, source, target = pairs[n]
-            there = lax.rem(lon + k, n_lon)
-            return remote(source.at[:, there], target.at[lon], far_sems.at[0, n, k], far_sems.at[1, n, k], there, lat)
-
-        def stays(n, stage):
-            source, middle, target = pairs[n]
-            if stage == 0:
-                return pltpu.make_async_copy(source.at[:, lat], middle.at[lat], own_sems.at[0, n])
-            return pltpu.make_async_copy(middle.at[:, lon], target.at[lon], own_sems.at[1, n])
-
         for n in range(2):
             for k in range(1, n_lat):
-                near(n, k).start()
-            stays(n, 0).start()
+                near(n, k).wait_recv()
+            near_own(n).wait()
+
+        @pl.loop(1, n_lon)
+        def _(k):
+            far(k).start()
+
+        far_own().start()
 
         for present, way in ((has_up, "down_coef"), (has_down, "up_coef")):
             @pl.when(present)
@@ -212,20 +234,6 @@
 
     sweep(main, main2, 1)
 
-    if first:
-        for n in range(2):
-            for k in range(1, n_lat):
-                near(n, k).wait_recv()
-            stays(n, 0).wait()
-
-        @pl.loop(1, n_lon)
-        def _(k):
-            for n in range(2):
-                far(n, k).start()
-
-        for n in range(2):
-            stays(n, 1).start()
-
     for kind in ("west", "east"):
         exchange(kind).wait_send()
     for present, way in ((has_up, "up"), (has_down, "down")):
@@ -257,12 +265,10 @@
 
         @pl.loop(1, n_lon)
         def _(k):
-            for n in range(2):
-                far(n, k).wait_recv()
-                far(n, k).wait_send()
-
-        for n in range(2):
-            stays(n, 1).wait()
+            far(k).wait_recv()
+            far(k).wait_send()
+
+        far_own().wait()
 
 
 def root(field, operands, rows, first):
@@ -273,21 +279,24 @@
     scratch = [pltpu.VMEM((ext, cols + 2 * EDGE, cols), jnp.float32)] * 2
     scratch += [pltpu.SemaphoreType.DMA((len(KINDS),))] * 2
     outs = [f32(*field.shape)]
+    far_memory = pl.BlockSpec(memory_space=pltpu.HBM)
     in_specs, out_specs = [vmem] * (1 + len(operands)), [vmem]
     if first:
-        anywhere = [pl.BlockSpec(memory_space=pl.ANY)] * 2
-        in_specs[3:] = anywhere
-        out_specs += [vmem] + anywhere
+        in_specs = [far_memory] * 5
+        out_specs += [vmem, far_memory]
         n_lon, n_lat = lax.axis_size("lon"), lax.axis_size("lat")
-        outs += [f32(3, ext, cols)] + [f32(n_lon, n_lat, 1, cols)] * 2
+        outs += [f32(3, ext, cols)] + [f32(n_lon, n_lat, 2, cols)]
         scratch = (
-            [pltpu.VMEM((3, ext, cols), jnp.float32)]
-            + [pltpu.VMEM((n_lat, n_lon, 1, cols), jnp.float32)] * 2
-            + [pltpu.SemaphoreType.DMA((2, 2, n_lat)), pltpu.SemaphoreType.DMA((2, 2, n_lon)), pltpu.SemaphoreType.DMA((2, 2))]
+            [pltpu.VMEM(field.shape, jnp.float32)]
+            + [pltpu.VMEM(operands[0].shape, jnp.float32)] * 2
+            + [pltpu.SemaphoreType.DMA((3,))]
+            + [pltpu.VMEM((3, ext, cols), jnp.float32)]
+            + [pltpu.VMEM((n_lat, n_lon, 2, cols), jnp.float32)]
+            + [pltpu.SemaphoreType.DMA((2, 2, n_lat)), pltpu.SemaphoreType.DMA((2, n_lon)), pltpu.SemaphoreType.DMA((3,))]
             + scratch
         )
     else:
-        in_specs[2] = pl.BlockSpec(memory_space=pl.ANY)
+        in_specs[2] = far_memory
         scratch = [pltpu.VMEM(field.shape, jnp.float32), pltpu.SemaphoreType.DMA] + scratch
     return pl.pallas_call(
         functools.partial(root_kernel, first, rows),
@@ -296,13 +305,13 @@
         out_specs=out_specs,
         scratch_shapes=scratch,
         compiler_params=pltpu.CompilerParams(
-            collective_id=0 if first else 1, has_side_effects=True, vmem_limit_bytes=60 * 2**20),
+            collective_id=0 if first else 1, has_side_effects=True, vmem_limit_bytes=(60 if first else 16) * 2**20),
         name="root_first" if first else "root_second",
     )(field, *operands)
 
 
 PAD = 8
-NACC = 8
+NACC = 16
 LANES = lax.GatherDimensionNumbers(
     offset_dims=(), collapsed_slice_dims=(1,), start_index_map=(1,),
     operand_batching_dims=(0,), start_indices_batching_dims=(0,))
@@ -312,8 +321,8 @@
     return lax.gather(value, index[:, :, None], LANES, slice_sizes=(1, 1), mode="promise_in_bounds")
 
 
-def obs_kernel(cnt_ref, tab_hbm, base_hbm, field_hbm, w_hbm, val_hbm, prec_hbm, inc_hbm, out_ref,
-               base_ref, field_ref, w_ref, val_ref, prec_ref, in_sems,
+def obs_kernel(cnt_ref, tab_hbm, base_hbm, field_hbm, w_hbm, held_hbm, inc_hbm, out_ref,
+               base_ref, field_ref, in_sems,
                tab, stack, dense, plan, cidx, ridx, ridx_s, sem, windows, places, sources, *accs):
     rows = tab_hbm.shape[0]
     cells = 16 * 128
@@ -324,31 +333,31 @@
     loads = [
         pltpu.make_async_copy(source, target, in_sems.at[k])
         for k, (source, target) in enumerate((
-            (base_hbm, base_ref), (field_hbm, field_ref), (w_hbm, w_ref), (val_hbm, val_ref), (prec_hbm, prec_ref),
-            (tab_hbm, tab.at[body]),
+            (base_hbm, base_ref), (field_hbm, field_ref), (held_hbm, stack.at[:, pl.ds(4, 2)]),
+            *((w_hbm.at[k], stack.at[:, pl.ds(k, 1)]) for k in range(4)), (tab_hbm, tab.at[body]),
         ))
     ]
-    keep = pltpu.make_async_copy(tab.at[body], inc_hbm, in_sems.at[6])
+    keep = pltpu.make_async_copy(tab.at[body], inc_hbm, in_sems.at[8])
     for load in loads:
         load.start()
     tab[pl.ds(0, 8), :] = zero
     tab[pl.ds(rows + PAD, 8), :] = zero
-    for load in loads[:-1]:
+    for load in loads[:2]:
         load.wait()
 
-    @pl.loop(0, 16)
+    @pl.loop(0, 4)
     def _(b):
-        at = pl.multiple_of(b * 8, 8)
-        part = pl.ds(at, 8)
-        index = field_ref[part, :] * cells + base_ref[part, :]
-        arrays = [w_ref[k, part, :] for k in range(4)]
-        arrays += [val_ref[part, :], prec_ref[part, :], index.astype(jnp.float32)]
-        for k, array in enumerate(arrays):
-            stack[pl.ds(at * 8 + k, 8, stride=8), :] = array
+        for k in range(4):
+            at = pl.multiple_of(b * 32 + 8 * k, 8)
+            index = field_ref[pl.ds(at, 8), :] * cells + base_ref[pl.ds(at, 8), :]
+            stack[pl.ds(at, 8), 6, :] = index.astype(jnp.float32)
+
+    for load in loads[2:-1]:
+        load.wait()
 
     def compact(o, carry):
         start, kept = carry
-        group = stack[pl.ds(pl.multiple_of(o * 8, 8), 8), :]
+        group = stack[o]
         shift = lax.bitwise_and(start, 127)
         row = lax.shift_right_logical(start, 7)
         rolled = pltpu.roll(group, shift, 1)
@@ -369,9 +378,8 @@
         after = pltpu.roll(high, 1, 1) + add
         return jnp.where(even, low, after), jnp.where(even, after, low)
 
-    @pl.loop(0, 16)
-    def _(b):
-        at = pl.multiple_of(b * 8, 8)
+    def plan_chunks(at):
+        at = pl.multiple_of(at, 8)
         part = pl.ds(at, 8)
         arrays = [dense[pl.ds(at * 8 + k, 8, stride=8), :] for k in range(7)]
         live = (at + sub) * 128 + lane < total
@@ -388,6 +396,11 @@
         plan[4, part, :], plan[5, part, :] = value, precision
         plan[6, part, :], plan[7, part, :] = pltpu.roll(value, 1, 1), pltpu.roll(precision, 1, 1)
 
+    @pl.loop(0, 4)
+    def _(b):
+        for k in range(4):
+            plan_chunks(b * 32 + 8 * k)
+
     copy = pltpu.make_async_copy(ridx, ridx_s, sem)
     copy.start()
 
@@ -488,7 +501,7 @@
 
     def step(d, carry):
         found_e, found_o, amounts_e, amounts_o = carry
-        last = chunks - 1
+        last = jnp.maximum(chunks - 1, 0)
         add_rows(jnp.clip(d - 4, 0, last))
         place((amounts_e, amounts_o))
         turn_lanes(jnp.clip(d - 2, 0, last))
@@ -512,25 +525,23 @@
     keep.wait()
 
 
-def observe(table, count, base, field, weight, value, precision):
+def observe(table, count, base, field, weight, held):
     rows, cols = table.shape
     vmem = pl.BlockSpec(memory_space=pltpu.VMEM)
     anywhere = pl.BlockSpec(memory_space=pl.ANY)
+    far_memory = pl.BlockSpec(memory_space=pltpu.HBM)
     smem = pl.BlockSpec(memory_space=pltpu.SMEM)
     return pl.pallas_call(
         obs_kernel,
         out_shape=[jax.ShapeDtypeStruct((rows, cols), jnp.float32)] * 2,
-        in_specs=[smem] + [anywhere] * 6,
-        out_specs=[anywhere, vmem],
+        in_specs=[smem, anywhere] + [far_memory] * 4,
+        out_specs=[far_memory, vmem],
         scratch_shapes=[
             pltpu.VMEM((128, 128), jnp.int32),
             pltpu.VMEM((128, 128), jnp.int32),
-            pltpu.VMEM((4, 128, 128), jnp.float32),
-            pltpu.VMEM((128, 128), jnp.float32),
-            pltpu.VMEM((128, 128), jnp.float32),
-            pltpu.SemaphoreType.DMA((7,)),
+            pltpu.SemaphoreType.DMA((9,)),
             pltpu.VMEM((rows + 2 * PAD, cols), jnp.float32),
-            pltpu.VMEM((1024, 128), jnp.float32),
+            pltpu.VMEM((128, 8, 128), jnp.float32),
             pltpu.VMEM((129 * 8, 128), jnp.float32),
             pltpu.VMEM((8, 128, 128), jnp.float32),
             pltpu.VMEM((3, 128, 128), jnp.int32),
@@ -541,9 +552,9 @@
             pltpu.VMEM((32, 8, 128), jnp.float32),
             pltpu.VMEM((32, 8, 128), jnp.int32),
         ] + [pltpu.VMEM((rows + 2 * PAD, cols), jnp.float32)] * NACC,
-        compiler_params=pltpu.CompilerParams(vmem_limit_bytes=60 * 2**20),
+        compiler_params=pltpu.CompilerParams(vmem_limit_bytes=30 * 2**20),
         name="observe",
-    )(count, table, base, field, weight, value, precision)
+    )(count, table, base, field, weight, held)
 
 
 def per_device(
@@ -561,7 +572,7 @@
     owners, slots = obs_base.shape[1:]
     by_device = (lax.axis_size("lon"), lax.axis_size("lat"), 1, slots)
     lines = control.reshape(fields * band_rows, block_cols)
-    increment, coefs, value, precision = root(
+    increment, coefs, held = root(
         lines,
         (lon_coef.T, lat_coef.T, obs_value.reshape(by_device), obs_precision.reshape(by_device)),
         band_rows,
@@ -572,9 +583,8 @@
         obs_count,
         obs_base[0],
         obs_field[0],
-        obs_weight[:, 0],
-        value.reshape(owners, slots),
-        precision.reshape(owners, slots),
+        obs_weight.reshape(obs_weight.shape[0], owners, 1, slots),
+        held.reshape(owners, 2, slots),
     )
     (gradient,) = root(forcing, (coefs, lines), band_rows, False)
     return (increment.reshape(control.shape), gradient.reshape(control.shape))

time: 70.1 us -> 61.2 us (0.87)
  Pallas kernels: 67.2 us -> 57.3 us
  local copies, waits for them, and re-layouts: 2.09 us -> 3.03 us
    pallas_call x2, Pallas kernels: 43.9 us -> 35.7 us  [root(): pl.pallas_call(functools.partial(root_kernel, first, rows), out_shape=out...]
    pallas_call x1, Pallas kernels: 23.3 us -> 21.6 us  [observe(): pl.pallas_call(obs_kernel, out_shape=[jax.ShapeDtypeStruct((rows, cols),...]
    unnamed x1 -> x17, local copies, waits for them, and re-layouts: 2.09 us -> 3.03 us
where the time goes in v6:
time: 61.2 us; the launch traced here: 61.1 us
  Pallas kernels  57.3 us (94%)
  local copies, waits for them, and re-layouts  3.03 us (5%)
  between operations  0.75 us (1%)
    pallas_call x2, Pallas kernels, root(): pl.pallas_call(functools.partial(root_kernel, first, rows), out_shape=out...  35.7 us
    pallas_call x1, Pallas kernels, observe(): pl.pallas_call(obs_kernel, out_shape=[jax.ShapeDtypeStruct((rows, cols),...  21.6 us
    unnamed x17, local copies, waits for them, and re-layouts  3.03 us

profile of v6, /device:TPU:1, one launch (start us, length us, event | category | flops | bytes accessed | tf_op | source)
XLA Modules:
  0.0 61.1 jit_solution(1816232364025041141)
XLA Ops:
  0.6 0.0 copy-start.2
  0.6 0.0 copy-start.4
  0.7 0.0 copy-start.5
  0.7 0.0 copy-start.7
  0.7 23.5 %root_first.1 = (f32[1600,128]{1,0:T(8,128)}, f32[3,24,128]{2,1,0:T(8,128)}, f32[32,4,2,128]{3,2,1,0:T(2,128)}) custom-call(f32[1600,128]{1,0:T(8,128)} %bitcast.12, f32[16,100]{1,0:T(8,128)} %bitcast.20, f32[16,100]{1,0:T(8,128)} %bitcast.21, f32[32,4,1,128]{3,2,1,0:T(1,128)} %bitcast.18, f32[32,4,1,128]{3,2,1,0:T(1,128)} %bitcast.19), custom_call_target="tpu_custom_call" | custom-call | tf_op jit(solution)/shard_map/root_first/pallas_call | solution.py:301
  24.1 0.0 copy-start
  24.2 0.0 copy-done.2
  24.2 0.0 copy-done.4
  24.2 0.0 copy-done.5
  24.2 0.0 copy-done.7
  24.2 0.0 copy-start.1
  24.2 1.2 %copy-done.1 = f32[1600,128]{1,0:T(8,128)S(1)} copy-done((f32[1600,128]{1,0:T(8,128)S(1)}, f32[1600,128]{1,0:T(8,128)}, u32[]{:S(2)}) %copy-start.1) | copy-done | bytes 819224
  25.4 0.0 copy-start.3
  25.4 0.9 %copy-done.3 = f32[32,4,2,128]{3,2,1,0:T(2,128)S(1)} copy-done((f32[32,4,2,128]{3,2,1,0:T(2,128)S(1)}, f32[32,4,2,128]{3,2,1,0:T(2,128)}, u32[]{:S(2)}) %copy-start.3) | copy-done | bytes 131096
  26.3 0.0 copy-start.6
  26.3 21.6 %observe.1 = (f32[1600,128]{1,0:T(8,128)}, f32[1600,128]{1,0:T(8,128)S(1)}) custom-call(s32[1,128]{1,0:T(1,128)S(1)} %copy-done.7, f32[1600,128]{1,0:T(8,128)S(1)} %copy-done.1, s32[128,128]{1,0:T(8,128)S(1)} %bitcast.16, s32[128,128]{1,0:T(8,128)S(1)} %bitcast.17, f32[4,128,1,128]{3,2,1,0:T(1,128)S(1)} %bitcast.14, f32[128,2,128]{2,1,0:T(2,128)S(1)} %bitcast.15), custom_call_target="tpu_custom_call" | custom-call | tf_op jit(solution)/shard_map/observe/pallas_call | solution.py:534
  47.9 0.0 copy-done
  47.9 0.0 copy-done.6
  47.9 12.2 %root_second.1 = f32[1600,128]{1,0:T(8,128)S(1)} custom-call(f32[1600,128]{1,0:T(8,128)S(1)} %get-tuple-element.10.refs_0_, f32[3,24,128]{2,1,0:T(8,128)S(1)} %copy-done.6, f32[1600,128]{1,0:T(8,128)S(1)} %bitcast.13), custom_call_target="tpu_custom_call" | custom-call | tf_op jit(solution)/shard_map/root_second/pallas_call | solution.py:301
  60.2 0.9 %copy.12 = f32[100,16,128]{2,1,0:T(8,128)} copy(f32[100,16,128]{2,1,0:T(8,128)S(1)} %bitcast.11) | data formatting | bytes 1638400
Async XLA Ops:
  0.6 23.5 %copy-start.2 = (f32[4,1,128,128]{3,2,1,0:T(8,128)S(1)}, f32[4,1,128,128]{3,2,1,0:T(8,128)}, u32[]{:S(2)}) copy-start(f32[4,1,128,128]{3,2,1,0:T(8,128)} %param.14) | copy-start | bytes 786436
  0.6 23.5 %copy-start.4 = (s32[1,128,128]{2,1,0:T(8,128)S(1)}, s32[1,128,128]{2,1,0:T(8,128)}, u32[]{:S(2)}) copy-start(s32[1,128,128]{2,1,0:T(8,128)} %param.12) | copy-start | bytes 196612
  0.7 23.5 %copy-start.5 = (s32[1,128,128]{2,1,0:T(8,128)S(1)}, s32[1,128,128]{2,1,0:T(8,128)}, u32[]{:S(2)}) copy-start(s32[1,128,128]{2,1,0:T(8,128)} %param.13) | copy-start | bytes 196612
  0.7 23.5 %copy-start.7 = (s32[1,128]{1,0:T(1,128)S(1)}, s32[1,128]{1,0:T(1,128)}, u32[]{:S(2)}) copy-start(s32[1,128]{1,0:T(1,128)} %cnt_ref.1) | copy-start | bytes 1540
  24.1 23.8 %copy-start = (f32[100,16,128]{2,1,0:T(8,128)S(1)}, f32[100,16,128]{2,1,0:T(8,128)}, u32[]{:S(2)}) copy-start(f32[100,16,128]{2,1,0:T(8,128)} %param.9) | copy-start | bytes 2457604
  24.2 1.2 %copy-start.1 = (f32[1600,128]{1,0:T(8,128)S(1)}, f32[1600,128]{1,0:T(8,128)}, u32[]{:S(2)}) copy-start(f32[1600,128]{1,0:T(8,128)} %get-tuple-element.7.tab_hbm) | copy-start | bytes 2457604
  25.4 0.9 %copy-start.3 = (f32[32,4,2,128]{3,2,1,0:T(2,128)S(1)}, f32[32,4,2,128]{3,2,1,0:T(2,128)}, u32[]{:S(2)}) copy-start(f32[32,4,2,128]{3,2,1,0:T(2,128)} %get-tuple-element.8) | copy-start | bytes 393220
  26.3 21.6 %copy-start.6 = (f32[3,24,128]{2,1,0:T(8,128)S(1)}, f32[3,24,128]{2,1,0:T(8,128)}, u32[]{:S(2)}) copy-start(f32[3,24,128]{2,1,0:T(8,128)} %get-tuple-element.11.refs_1_) | copy-start | bytes 110596

commit v7 on v6

--- a/solution.py
+++ b/solution.py
@@ -389,7 +389,8 @@
         cidx[0, part, :], cidx[1, part, :] = paired(cols, cols, 1)
         cidx[2, part, :] = lane - cols
         for a in range(2):
-            first_row, second_row = paired(arrays[2 * a], arrays[2 * a + 1])
+            pair = [jnp.where(live, arrays[2 * a + b], 0.0) for b in range(2)]
+            first_row, second_row = paired(*pair)
             plan[a, part, :], plan[2 + a, part, :] = first_row, second_row
         precision = jnp.where(live, arrays[5], 0.0)
         value = jnp.where(live, arrays[4], 0.0)

time: 61.2 us -> 60.6 us (level)
  Pallas kernels: 57.3 us -> 56.6 us
where the time goes in v7:
time: 60.6 us; the launch traced here: 60.4 us
  Pallas kernels  56.6 us (93%)
  local copies, waits for them, and re-layouts  3.03 us (5%)
  between operations  0.75 us (1%)
    pallas_call x2, Pallas kernels, root(): pl.pallas_call(functools.partial(root_kernel, first, rows), out_shape=out...  35.3 us
    pallas_call x1, Pallas kernels, observe(): pl.pallas_call(obs_kernel, out_shape=[jax.ShapeDtypeStruct((rows, cols),...  21.3 us
    unnamed x17, local copies, waits for them, and re-layouts  3.03 us

profile of v7, /device:TPU:1, one launch (start us, length us, event | category | flops | bytes accessed | tf_op | source)
XLA Modules:
  0.0 60.4 jit_solution(17939595342093788205)
XLA Ops:
  0.6 0.0 copy-start.2
  0.6 0.0 copy-start.4
  0.7 0.0 copy-start.5
  0.7 0.0 copy-start.7
  0.7 23.5 %root_first.1 = (f32[1600,128]{1,0:T(8,128)}, f32[3,24,128]{2,1,0:T(8,128)}, f32[32,4,2,128]{3,2,1,0:T(2,128)}) custom-call(f32[1600,128]{1,0:T(8,128)} %bitcast.12, f32[16,100]{1,0:T(8,128)} %bitcast.20, f32[16,100]{1,0:T(8,128)} %bitcast.21, f32[32,4,1,128]{3,2,1,0:T(1,128)} %bitcast.18, f32[32,4,1,128]{3,2,1,0:T(1,128)} %bitcast.19), custom_call_target="tpu_custom_call" | custom-call | tf_op jit(solution)/shard_map/root_first/pallas_call | solution.py:301
  24.1 0.0 copy-start
  24.2 0.0 copy-done.2
  24.2 0.0 copy-done.4
  24.2 0.0 copy-done.5
  24.2 0.0 copy-done.7
  24.2 0.0 copy-start.1
  24.2 1.2 %copy-done.1 = f32[1600,128]{1,0:T(8,128)S(1)} copy-done((f32[1600,128]{1,0:T(8,128)S(1)}, f32[1600,128]{1,0:T(8,128)}, u32[]{:S(2)}) %copy-start.1) | copy-done | bytes 819224
  25.4 0.0 copy-start.3
  25.4 0.9 %copy-done.3 = f32[32,4,2,128]{3,2,1,0:T(2,128)S(1)} copy-done((f32[32,4,2,128]{3,2,1,0:T(2,128)S(1)}, f32[32,4,2,128]{3,2,1,0:T(2,128)}, u32[]{:S(2)}) %copy-start.3) | copy-done | bytes 131096
  26.3 0.0 copy-start.6
  26.3 21.3 %observe.1 = (f32[1600,128]{1,0:T(8,128)}, f32[1600,128]{1,0:T(8,128)S(1)}) custom-call(s32[1,128]{1,0:T(1,128)S(1)} %copy-done.7, f32[1600,128]{1,0:T(8,128)S(1)} %copy-done.1, s32[128,128]{1,0:T(8,128)S(1)} %bitcast.16, s32[128,128]{1,0:T(8,128)S(1)} %bitcast.17, f32[4,128,1,128]{3,2,1,0:T(1,128)S(1)} %bitcast.14, f32[128,2,128]{2,1,0:T(2,128)S(1)} %bitcast.15), custom_call_target="tpu_custom_call" | custom-call | tf_op jit(solution)/shard_map/observe/pallas_call | solution.py:535
  47.7 0.0 copy-done
  47.7 0.0 copy-done.6
  47.7 11.8 %root_second.1 = f32[1600,128]{1,0:T(8,128)S(1)} custom-call(f32[1600,128]{1,0:T(8,128)S(1)} %get-tuple-element.10.refs_0_, f32[3,24,128]{2,1,0:T(8,128)S(1)} %copy-done.6, f32[1600,128]{1,0:T(8,128)S(1)} %bitcast.13), custom_call_target="tpu_custom_call" | custom-call | tf_op jit(solution)/shard_map/root_second/pallas_call | solution.py:301
  59.5 0.9 %copy.12 = f32[100,16,128]{2,1,0:T(8,128)} copy(f32[100,16,128]{2,1,0:T(8,128)S(1)} %bitcast.11) | data formatting | bytes 1638400
Async XLA Ops:
  0.6 23.5 %copy-start.2 = (f32[4,1,128,128]{3,2,1,0:T(8,128)S(1)}, f32[4,1,128,128]{3,2,1,0:T(8,128)}, u32[]{:S(2)}) copy-start(f32[4,1,128,128]{3,2,1,0:T(8,128)} %param.14) | copy-start | bytes 786436
  0.6 23.5 %copy-start.4 = (s32[1,128,128]{2,1,0:T(8,128)S(1)}, s32[1,128,128]{2,1,0:T(8,128)}, u32[]{:S(2)}) copy-start(s32[1,128,128]{2,1,0:T(8,128)} %param.12) | copy-start | bytes 196612
  0.7 23.5 %copy-start.5 = (s32[1,128,128]{2,1,0:T(8,128)S(1)}, s32[1,128,128]{2,1,0:T(8,128)}, u32[]{:S(2)}) copy-start(s32[1,128,128]{2,1,0:T(8,128)} %param.13) | copy-start | bytes 196612
  0.7 23.5 %copy-start.7 = (s32[1,128]{1,0:T(1,128)S(1)}, s32[1,128]{1,0:T(1,128)}, u32[]{:S(2)}) copy-start(s32[1,128]{1,0:T(1,128)} %cnt_ref.1) | copy-start | bytes 1540
  24.1 23.5 %copy-start = (f32[100,16,128]{2,1,0:T(8,128)S(1)}, f32[100,16,128]{2,1,0:T(8,128)}, u32[]{:S(2)}) copy-start(f32[100,16,128]{2,1,0:T(8,128)} %param.9) | copy-start | bytes 2457604
  24.2 1.2 %copy-start.1 = (f32[1600,128]{1,0:T(8,128)S(1)}, f32[1600,128]{1,0:T(8,128)}, u32[]{:S(2)}) copy-start(f32[1600,128]{1,0:T(8,128)} %get-tuple-element.7.tab_hbm) | copy-start | bytes 2457604
  25.4 0.9 %copy-start.3 = (f32[32,4,2,128]{3,2,1,0:T(2,128)S(1)}, f32[32,4,2,128]{3,2,1,0:T(2,128)}, u32[]{:S(2)}) copy-start(f32[32,4,2,128]{3,2,1,0:T(2,128)} %get-tuple-element.8) | copy-start | bytes 393220
  26.3 21.4 %copy-start.6 = (f32[3,24,128]{2,1,0:T(8,128)S(1)}, f32[3,24,128]{2,1,0:T(8,128)}, u32[]{:S(2)}) copy-start(f32[3,24,128]{2,1,0:T(8,128)} %get-tuple-element.11.refs_1_) | copy-start | bytes 110596

commit v8 on v7

--- a/solution.py
+++ b/solution.py
@@ -512,7 +512,22 @@
         ready = d > 1
         return (*found, jnp.where(ready, amounts[0], 0.0), jnp.where(ready, amounts[1], 0.0))
 
-    lax.fori_loop(0, chunks + 4, step, (zero,) * 4)
+    def first_step(d, carry):
+        last = jnp.maximum(chunks - 1, 0)
+        turn_lanes(jnp.clip(d - 2, 0, last))
+        amounts = compare(jnp.clip(d - 2, 0, last), carry[:2])
+        found = gather(jnp.clip(d - 1, 0, last))
+        load_windows(jnp.minimum(d, last))
+        return (*found, jnp.where(d > 1, amounts[0], 0.0), jnp.where(d > 1, amounts[1], 0.0))
+
+    def last_step(d, carry):
+        add_rows(jnp.clip(d - 4, 0, jnp.maximum(chunks - 1, 0)))
+        place(carry[2:])
+        return carry
+
+    carry = lax.fori_loop(0, 3, first_step, (zero,) * 4)
+    carry = lax.fori_loop(3, chunks + 2, step, carry)
+    lax.fori_loop(chunks + 2, chunks + 4, last_step, carry)
 
     @pl.loop(0, rows // 80)
     def _(i):

time: 60.6 us -> 61 us (level)
  Pallas kernels: 56.6 us -> 57.3 us
    pallas_call x2, Pallas kernels: 35.3 us -> 36.1 us  [root(): pl.pallas_call(functools.partial(root_kernel, first, rows), out_shape=out...]
where the time goes in v8:
time: 61 us; the launch traced here: 61.1 us
  Pallas kernels  57.3 us (94%)
  local copies, waits for them, and re-layouts  3.03 us (5%)
  between operations  0.75 us (1%)
    pallas_call x2, Pallas kernels, root(): pl.pallas_call(functools.partial(root_kernel, first, rows), out_shape=out...  36.1 us
    pallas_call x1, Pallas kernels, observe(): pl.pallas_call(obs_kernel, out_shape=[jax.ShapeDtypeStruct((rows, cols),...  21.2 us
    unnamed x17, local copies, waits for them, and re-layouts  3.03 us

profile of v8, /device:TPU:1, one launch (start us, length us, event | category | flops | bytes accessed | tf_op | source)
XLA Modules:
  0.0 61.1 jit_solution(8759834780604719489)
XLA Ops:
  0.6 0.0 copy-start.2
  0.6 0.0 copy-start.4
  0.7 0.0 copy-start.5
  0.7 0.0 copy-start.7
  0.7 23.5 %root_first.1 = (f32[1600,128]{1,0:T(8,128)}, f32[3,24,128]{2,1,0:T(8,128)}, f32[32,4,2,128]{3,2,1,0:T(2,128)}) custom-call(f32[1600,128]{1,0:T(8,128)} %bitcast.12, f32[16,100]{1,0:T(8,128)} %bitcast.20, f32[16,100]{1,0:T(8,128)} %bitcast.21, f32[32,4,1,128]{3,2,1,0:T(1,128)} %bitcast.18, f32[32,4,1,128]{3,2,1,0:T(1,128)} %bitcast.19), custom_call_target="tpu_custom_call" | custom-call | tf_op jit(solution)/shard_map/root_first/pallas_call | solution.py:301
  24.1 0.0 copy-start
  24.2 0.0 copy-done.2
  24.2 0.0 copy-done.4
  24.2 0.0 copy-done.5
  24.2 0.0 copy-done.7
  24.2 0.0 copy-start.1
  24.2 1.2 %copy-done.1 = f32[1600,128]{1,0:T(8,128)S(1)} copy-done((f32[1600,128]{1,0:T(8,128)S(1)}, f32[1600,128]{1,0:T(8,128)}, u32[]{:S(2)}) %copy-start.1) | copy-done | bytes 819224
  25.4 0.0 copy-start.3
  25.4 0.9 %copy-done.3 = f32[32,4,2,128]{3,2,1,0:T(2,128)S(1)} copy-done((f32[32,4,2,128]{3,2,1,0:T(2,128)S(1)}, f32[32,4,2,128]{3,2,1,0:T(2,128)}, u32[]{:S(2)}) %copy-start.3) | copy-done | bytes 131096
  26.3 0.0 copy-start.6
  26.3 21.2 %observe.1 = (f32[1600,128]{1,0:T(8,128)}, f32[1600,128]{1,0:T(8,128)S(1)}) custom-call(s32[1,128]{1,0:T(1,128)S(1)} %copy-done.7, f32[1600,128]{1,0:T(8,128)S(1)} %copy-done.1, s32[128,128]{1,0:T(8,128)S(1)} %bitcast.16, s32[128,128]{1,0:T(8,128)S(1)} %bitcast.17, f32[4,128,1,128]{3,2,1,0:T(1,128)S(1)} %bitcast.14, f32[128,2,128]{2,1,0:T(2,128)S(1)} %bitcast.15), custom_call_target="tpu_custom_call" | custom-call | tf_op jit(solution)/shard_map/observe/pallas_call | solution.py:550
  47.5 0.0 copy-done
  47.5 0.0 copy-done.6
  47.5 12.6 %root_second.1 = f32[1600,128]{1,0:T(8,128)S(1)} custom-call(f32[1600,128]{1,0:T(8,128)S(1)} %get-tuple-element.10.refs_0_, f32[3,24,128]{2,1,0:T(8,128)S(1)} %copy-done.6, f32[1600,128]{1,0:T(8,128)S(1)} %bitcast.13), custom_call_target="tpu_custom_call" | custom-call | tf_op jit(solution)/shard_map/root_second/pallas_call | solution.py:301
  60.2 0.9 %copy.12 = f32[100,16,128]{2,1,0:T(8,128)} copy(f32[100,16,128]{2,1,0:T(8,128)S(1)} %bitcast.11) | data formatting | bytes 1638400
Async XLA Ops:
  0.6 23.5 %copy-start.2 = (f32[4,1,128,128]{3,2,1,0:T(8,128)S(1)}, f32[4,1,128,128]{3,2,1,0:T(8,128)}, u32[]{:S(2)}) copy-start(f32[4,1,128,128]{3,2,1,0:T(8,128)} %param.14) | copy-start | bytes 786436
  0.6 23.5 %copy-start.4 = (s32[1,128,128]{2,1,0:T(8,128)S(1)}, s32[1,128,128]{2,1,0:T(8,128)}, u32[]{:S(2)}) copy-start(s32[1,128,128]{2,1,0:T(8,128)} %param.12) | copy-start | bytes 196612
  0.7 23.5 %copy-start.5 = (s32[1,128,128]{2,1,0:T(8,128)S(1)}, s32[1,128,128]{2,1,0:T(8,128)}, u32[]{:S(2)}) copy-start(s32[1,128,128]{2,1,0:T(8,128)} %param.13) | copy-start | bytes 196612
  0.7 23.5 %copy-start.7 = (s32[1,128]{1,0:T(1,128)S(1)}, s32[1,128]{1,0:T(1,128)}, u32[]{:S(2)}) copy-start(s32[1,128]{1,0:T(1,128)} %cnt_ref.1) | copy-start | bytes 1540
  24.1 23.4 %copy-start = (f32[100,16,128]{2,1,0:T(8,128)S(1)}, f32[100,16,128]{2,1,0:T(8,128)}, u32[]{:S(2)}) copy-start(f32[100,16,128]{2,1,0:T(8,128)} %param.9) | copy-start | bytes 2457604
  24.2 1.2 %copy-start.1 = (f32[1600,128]{1,0:T(8,128)S(1)}, f32[1600,128]{1,0:T(8,128)}, u32[]{:S(2)}) copy-start(f32[1600,128]{1,0:T(8,128)} %get-tuple-element.7.tab_hbm) | copy-start | bytes 2457604
  25.4 0.9 %copy-start.3 = (f32[32,4,2,128]{3,2,1,0:T(2,128)S(1)}, f32[32,4,2,128]{3,2,1,0:T(2,128)}, u32[]{:S(2)}) copy-start(f32[32,4,2,128]{3,2,1,0:T(2,128)} %get-tuple-element.8) | copy-start | bytes 393220
  26.3 21.2 %copy-start.6 = (f32[3,24,128]{2,1,0:T(8,128)S(1)}, f32[3,24,128]{2,1,0:T(8,128)}, u32[]{:S(2)}) copy-start(f32[3,24,128]{2,1,0:T(8,128)} %get-tuple-element.11.refs_1_) | copy-start | bytes 110596

commit v9 on v8

--- a/solution.py
+++ b/solution.py
@@ -129,9 +129,10 @@
             coef[k, band, pl.ds(0, fields)] = rates
 
     for start in (0, rows - DEEP):
-        @pl.loop(start, start + DEEP)
-        def _(j):
-            turn_in(j)
+        @pl.loop(start // 2, (start + DEEP) // 2)
+        def _(i):
+            turn_in(2 * i)
+            turn_in(2 * i + 1)
 
     if first:
         sent = (value_ref, precision_ref)
@@ -176,9 +177,10 @@
             if first:
                 coef[pl.ds(0, 2), at] = jnp.zeros((2, DEEP, cols), jnp.float32)
 
-    @pl.loop(DEEP, rows - DEEP)
-    def _(j):
-        turn_in(j)
+    @pl.loop(DEEP // 2, (rows - DEEP) // 2)
+    def _(i):
+        turn_in(2 * i)
+        turn_in(2 * i + 1)
 
     for kind in ("west", "east"):
         exchange(kind).start()

time: 61 us -> 61 us (level)
    pallas_call x1, Pallas kernels: 21.2 us -> 22.7 us  [observe(): pl.pallas_call(obs_kernel, out_shape=[jax.ShapeDtypeStruct((rows, cols),...]
    pallas_call x2, Pallas kernels: 36.1 us -> 35.1 us  [root(): pl.pallas_call(functools.partial(root_kernel, first, rows), out_shape=out...]
where the time goes in v9:
time: 61 us; the launch traced here: 61.5 us
  Pallas kernels  57.7 us (95%)
  local copies, waits for them, and re-layouts  3.03 us (5%)
  between operations  0.75 us (1%)
    pallas_call x2, Pallas kernels, root(): pl.pallas_call(functools.partial(root_kernel, first, rows), out_shape=out...  35.1 us
    pallas_call x1, Pallas kernels, observe(): pl.pallas_call(obs_kernel, out_shape=[jax.ShapeDtypeStruct((rows, cols),...  22.7 us
    unnamed x17, local copies, waits for them, and re-layouts  3.03 us

profile of v9, /device:TPU:1, one launch (start us, length us, event | category | flops | bytes accessed | tf_op | source)
XLA Modules:
  0.0 61.5 jit_solution(485565344684766842)
XLA Ops:
  0.6 0.0 copy-start.2
  0.6 0.0 copy-start.4
  0.7 0.0 copy-start.5
  0.7 0.0 copy-start.7
  0.7 23.6 %root_first.1 = (f32[1600,128]{1,0:T(8,128)}, f32[3,24,128]{2,1,0:T(8,128)}, f32[32,4,2,128]{3,2,1,0:T(2,128)}) custom-call(f32[1600,128]{1,0:T(8,128)} %bitcast.12, f32[16,100]{1,0:T(8,128)} %bitcast.20, f32[16,100]{1,0:T(8,128)} %bitcast.21, f32[32,4,1,128]{3,2,1,0:T(1,128)} %bitcast.18, f32[32,4,1,128]{3,2,1,0:T(1,128)} %bitcast.19), custom_call_target="tpu_custom_call" | custom-call | tf_op jit(solution)/shard_map/root_first/pallas_call | solution.py:303
  24.3 0.0 copy-start
  24.3 0.0 copy-done.2
  24.3 0.0 copy-done.4
  24.4 0.0 copy-done.5
  24.4 0.0 copy-done.7
  24.4 0.0 copy-start.1
  24.4 1.2 %copy-done.1 = f32[1600,128]{1,0:T(8,128)S(1)} copy-done((f32[1600,128]{1,0:T(8,128)S(1)}, f32[1600,128]{1,0:T(8,128)}, u32[]{:S(2)}) %copy-start.1) | copy-done | bytes 819224
  25.6 0.0 copy-start.3
  25.6 0.9 %copy-done.3 = f32[32,4,2,128]{3,2,1,0:T(2,128)S(1)} copy-done((f32[32,4,2,128]{3,2,1,0:T(2,128)S(1)}, f32[32,4,2,128]{3,2,1,0:T(2,128)}, u32[]{:S(2)}) %copy-start.3) | copy-done | bytes 131096
  26.5 0.0 copy-start.6
  26.5 22.7 %observe.1 = (f32[1600,128]{1,0:T(8,128)}, f32[1600,128]{1,0:T(8,128)S(1)}) custom-call(s32[1,128]{1,0:T(1,128)S(1)} %copy-done.7, f32[1600,128]{1,0:T(8,128)S(1)} %copy-done.1, s32[128,128]{1,0:T(8,128)S(1)} %bitcast.16, s32[128,128]{1,0:T(8,128)S(1)} %bitcast.17, f32[4,128,1,128]{3,2,1,0:T(1,128)S(1)} %bitcast.14, f32[128,2,128]{2,1,0:T(2,128)S(1)} %bitcast.15), custom_call_target="tpu_custom_call" | custom-call | tf_op jit(solution)/shard_map/observe/pallas_call | solution.py:552
  49.2 0.0 copy-done
  49.2 0.0 copy-done.6
  49.2 11.4 %root_second.1 = f32[1600,128]{1,0:T(8,128)S(1)} custom-call(f32[1600,128]{1,0:T(8,128)S(1)} %get-tuple-element.10.refs_0_, f32[3,24,128]{2,1,0:T(8,128)S(1)} %copy-done.6, f32[1600,128]{1,0:T(8,128)S(1)} %bitcast.13), custom_call_target="tpu_custom_call" | custom-call | tf_op jit(solution)/shard_map/root_second/pallas_call | solution.py:303
  60.6 0.9 %copy.12 = f32[100,16,128]{2,1,0:T(8,128)} copy(f32[100,16,128]{2,1,0:T(8,128)S(1)} %bitcast.11) | data formatting | bytes 1638400
Async XLA Ops:
  0.6 23.7 %copy-start.2 = (f32[4,1,128,128]{3,2,1,0:T(8,128)S(1)}, f32[4,1,128,128]{3,2,1,0:T(8,128)}, u32[]{:S(2)}) copy-start(f32[4,1,128,128]{3,2,1,0:T(8,128)} %param.14) | copy-start | bytes 786436
  0.6 23.7 %copy-start.4 = (s32[1,128,128]{2,1,0:T(8,128)S(1)}, s32[1,128,128]{2,1,0:T(8,128)}, u32[]{:S(2)}) copy-start(s32[1,128,128]{2,1,0:T(8,128)} %param.12) | copy-start | bytes 196612
  0.7 23.7 %copy-start.5 = (s32[1,128,128]{2,1,0:T(8,128)S(1)}, s32[1,128,128]{2,1,0:T(8,128)}, u32[]{:S(2)}) copy-start(s32[1,128,128]{2,1,0:T(8,128)} %param.13) | copy-start | bytes 196612
  0.7 23.7 %copy-start.7 = (s32[1,128]{1,0:T(1,128)S(1)}, s32[1,128]{1,0:T(1,128)}, u32[]{:S(2)}) copy-start(s32[1,128]{1,0:T(1,128)} %cnt_ref.1) | copy-start | bytes 1540
  24.3 24.8 %copy-start = (f32[100,16,128]{2,1,0:T(8,128)S(1)}, f32[100,16,128]{2,1,0:T(8,128)}, u32[]{:S(2)}) copy-start(f32[100,16,128]{2,1,0:T(8,128)} %param.9) | copy-start | bytes 2457604
  24.4 1.2 %copy-start.1 = (f32[1600,128]{1,0:T(8,128)S(1)}, f32[1600,128]{1,0:T(8,128)}, u32[]{:S(2)}) copy-start(f32[1600,128]{1,0:T(8,128)} %get-tuple-element.7.tab_hbm) | copy-start | bytes 2457604
  25.6 0.9 %copy-start.3 = (f32[32,4,2,128]{3,2,1,0:T(2,128)S(1)}, f32[32,4,2,128]{3,2,1,0:T(2,128)}, u32[]{:S(2)}) copy-start(f32[32,4,2,128]{3,2,1,0:T(2,128)} %get-tuple-element.8) | copy-start | bytes 393220
  26.5 22.7 %copy-start.6 = (f32[3,24,128]{2,1,0:T(8,128)S(1)}, f32[3,24,128]{2,1,0:T(8,128)}, u32[]{:S(2)}) copy-start(f32[3,24,128]{2,1,0:T(8,128)} %get-tuple-element.11.refs_1_) | copy-start | bytes 110596
